TPU v7x, 32 devices: a whole 2x2x4 slice. The times are simulated.
32 devices in a mesh: image: 4 (over z), ri: 8 (over y, x, core).
Axes of the slice: x: 2, y: 2, z: 4, core: 2. Of those that a mesh axis runs over, the one named last changes fastest.
Arguments:
- blocks: bfloat16 [1024, 64, 256], P(('image', 'ri')), may hold values from -0.59765625 to 0.59765625
- block_owner: int32 [1024, 1], P(('image', 'ri')), may hold values from 0 to 7; in each aligned block of 32 rows (0 to 31, 32 to 63, ...) at most 8 rows name the same one
- block_basis: int32 [1024, 2], P(('image', 'ri')), may hold values from 0 to 255
- pair_images: int32 [1024, 2, 4], P(('image', 'ri')), may hold values from 0 to 3
- pair_cell: int32 [1024, 4], P(('image', 'ri')), may hold values from 0 to 3
- lattice: int32 [4, 2], replicated, may hold values from -3 to 3
- dens_occ: bfloat16 [4, 256, 64], P('image'), may hold values from -1.5 to 1.5
- dens_virt: bfloat16 [4, 256, 64], P('image'), may hold values from -1.5 to 1.5
Outputs:
- chi_k: float32 [2, 64, 8, 256, 256], P(None, None, 'ri', 'image')
Inputs may be any that keep to these rules, and one draw needn't show every extreme that they name: `block_owner`: within the 32 blocks of one device no owner is named by more than 8 blocks.
All inputs are finite; a program needn't handle non-finite values.
Results may differ from a plain program's by a relative error of at most 0.0041.
Values may be sent and summed in bfloat16 or wider, within the bound.
No kernel may reach another device: no remote copies, remote signals or barrier semaphores. Data moves between devices by JAX's collectives and lax.ppermute only.
A program may use at most 128 MiB of HBM per device.

v0:
```python
import math

import jax
import jax.numpy as jnp
from jax import lax
from jax.sharding import PartitionSpec as P

KGRID = 8


def density_terms(occ_piece, first_image, virt_whole, listing, pair_count, cell_count):
    image_count, block_count, square = occ_piece.shape
    side_len = math.isqrt(square)
    row_count = listing.shape[0]
    first_block = listing[:, 0]
    second = listing[:, 1]
    occ_img = listing[:, 2 : 2 + pair_count]
    virt_img = listing[:, 2 + pair_count : 2 + 2 * pair_count]
    cell_ids = listing[:, 2 + 2 * pair_count : 2 + 3 * pair_count]
    offset = occ_img - first_image
    inside = ((offset >= 0) & (offset < image_count)).astype(jnp.float32)
    occ_rows = jnp.clip(offset, 0, image_count - 1) * block_count + first_block[:, None]
    virt_rows = virt_img * block_count + second[:, None]
    occ_vals = (
        occ_piece.reshape(image_count * block_count, square)[occ_rows].astype(jnp.float32)
        * inside[:, :, None]
    )
    virt_vals = virt_whole.reshape(-1, square)[virt_rows].astype(jnp.float32)
    select = (
        cell_ids[:, :, None] == jnp.arange(cell_count, dtype=jnp.int32)[None, None, :]
    ).astype(jnp.float32)
    term_sum = jnp.einsum(
        "sjr,sjlm,sjnq->srlqmn",
        select,
        occ_vals.reshape(row_count, pair_count, side_len, side_len),
        virt_vals.reshape(row_count, pair_count, side_len, side_len),
        precision=lax.Precision.HIGHEST,
    )
    return term_sum.reshape(row_count, cell_count, square, square)


def operators(listing, occ_local, virt_local, pair_count, cell_count):
    occ_whole, virt_whole = (
        lax.all_gather(occ_local, "image", axis=0, tiled=True),
        lax.all_gather(virt_local, "image", axis=0, tiled=True),
    )
    summed = density_terms(occ_whole, 0, virt_whole, listing, pair_count, cell_count)
    return summed.astype(jnp.bfloat16)


def local(blocks, block_owner, block_basis, pair_images, pair_cell, lattice, dens_occ, dens_virt):
    owners = lax.axis_size("ri")
    local_rows, square, ri_width = blocks.shape
    pair_count = pair_cell.shape[1]
    cell_count = lattice.shape[0]
    capacity = max(2, (2 * local_rows + owners - 1) // owners)
    slot_count = owners * capacity
    target = block_owner[:, 0]
    order_ids = jnp.arange(local_rows, dtype=jnp.int32)
    same_owner = (target[:, None] == target[None, :]) & (order_ids[:, None] > order_ids[None, :])
    owner_rank = jnp.sum(same_owner.astype(jnp.int32), axis=1)
    slot_index = target * capacity + owner_rank
    listing = jnp.concatenate(
        [block_basis, pair_images[:, 0, :], pair_images[:, 1, :], pair_cell], axis=1
    )
    packed = jnp.zeros((slot_count, square, ri_width), blocks.dtype).at[slot_index].set(blocks)
    packed_list = jnp.zeros((slot_count, listing.shape[1]), jnp.int32).at[slot_index].set(listing)
    got_blocks, got_list = (
        lax.all_to_all(
            packed.reshape(owners, capacity, square, ri_width),
            "ri",
            split_axis=0,
            concat_axis=0,
            tiled=True,
        ),
        lax.all_to_all(
            packed_list.reshape(owners, capacity, listing.shape[1]),
            "ri",
            split_axis=0,
            concat_axis=0,
            tiled=True,
        ),
    )
    got_blocks = got_blocks.reshape(slot_count, square, ri_width)
    density_ops = operators(
        got_list.reshape(slot_count, listing.shape[1]), dens_occ, dens_virt, pair_count, cell_count
    )
    group_size = 16
    group_count = slot_count // group_size

    def accumulate(running, pieces):
        op_part, blk_part = pieces
        mixed_rows = jnp.einsum(
            "srkm,smp->srkp", op_part, blk_part, preferred_element_type=jnp.float32
        ).astype(jnp.bfloat16)
        return (
            running
            + jnp.einsum("srkp,skq->rpq", mixed_rows, blk_part, preferred_element_type=jnp.float32),
            None,
        )

    start_total = jnp.zeros((cell_count, ri_width, ri_width), jnp.float32)
    chi_cells, _ = lax.scan(
        accumulate,
        start_total,
        (
            density_ops.reshape(group_count, group_size, cell_count, square, square),
            got_blocks.reshape(group_count, group_size, square, ri_width),
        ),
    )
    chi_share = lax.psum_scatter(chi_cells, "image", scatter_dimension=1, tiled=True)
    share_rows = chi_share.shape[1]
    points = jnp.arange(KGRID * KGRID, dtype=jnp.int32)
    wrapped = (
        (points // KGRID)[:, None] * lattice[None, :, 0]
        + (points % KGRID)[:, None] * lattice[None, :, 1]
    ) % KGRID
    angles = 2.0 * math.pi / KGRID * wrapped.astype(jnp.float32)
    phases = jnp.concatenate([jnp.cos(angles), jnp.sin(angles)], axis=0)
    result = jnp.dot(
        phases,
        chi_share.reshape(cell_count, share_rows * ri_width),
        precision=lax.Precision.HIGHEST,
    )
    return result.reshape(2, KGRID * KGRID, 1, share_rows, ri_width)


def solution(mesh):
    placed = (
        P(("image", "ri"), None, None),
        P(("image", "ri"), None),
        P(("image", "ri"), None),
        P(("image", "ri"), None, None),
        P(("image", "ri"), None),
        P(),
        P("image", None, None),
        P("image", None, None),
    )
    return jax.shard_map(
        local,
        mesh=mesh,
        in_specs=placed,
        out_specs=P(None, None, "ri", "image", None),
        check_vma=False,
    )
```

profile of v0, /device:TPU:0, one launch (start us, length us, event | category | flops | bytes accessed | tf_op | source)
XLA Modules:
  0.0 249.5 jit_solution(16602488156167313123)
XLA Ops:
  6.5 0.7 slice_bitcast_fusion.1
  7.2 0.7 pad_add_fusion
  7.9 0.1 copy.59
  8.0 0.9 convert_reduce_fusion
  8.9 0.7 fusion.35
  9.6 1.2 scatter_custom_fusion
  10.8 5.2 %all-to-all-start = ((s32[8,8,14]{2,1,0:T(8,128)}), s32[8,8,14]{2,1,0:T(8,128)S(1)}, u32[]{:S(2)}, u32[]{:S(2)}) async-start(s32[8,8,14]{2,1,0:T(8,128)} %bitcast.9), calls=%async_computation | async-start | bytes 65536 | tf_op jit(solution)/shard_map/all_to_all | solution.py:76
  16.0 13.8 %all_gather.6 = bf16[4,256,64]{1,2,0:T(8,128)(2,1)S(1)} all-gather(bf16[1,256,64]{1,2,0:T(8,128)(2,1)} %param.16), channel_id=1, replica_groups=mesh['image'=4,'ri'=8] {'image'}, dimensions={0}, use_global_device_ids=true | all-gather | bytes 163840 | tf_op jit(solution)/shard_map/all_gather | solution.py:44
  29.8 13.9 %all_gather.7 = bf16[4,256,64]{1,2,0:T(8,128)(2,1)S(1)} all-gather(bf16[1,256,64]{1,2,0:T(8,128)(2,1)} %param.17), channel_id=1, replica_groups=mesh['image'=4,'ri'=8] {'image'}, dimensions={0}, use_global_device_ids=true | all-gather | bytes 163840 | tf_op jit(solution)/shard_map/all_gather | solution.py:45
  43.7 0.2 copy.58
  43.8 0.2 copy.64
  44.0 1.6 broadcast_in_dim.28
  45.6 5.3 %scatter_fusion = bf16[64,64,256]{2,1,0:T(8,128)(2,1)} fusion(bf16[64,64,256]{2,1,0:T(8,128)(2,1)} %broadcast_in_dim.28, s32[32]{0:T(128)S(1)} %fusion.35, bf16[32,64,256]{2,1,0:T(8,128)(2,1)} %param.10), kind=kCustom, calls=%fused_computation.3 | custom fusion | bytes 3145856 | tf_op jit(solution)/shard_map/scatter | solution.py:66
  50.9 0.0 all-to-all-done
  50.9 4.4 %all-to-all-start.1 = ((bf16[8,8,64,256]{3,2,1,0:T(8,128)(2,1)}), bf16[8,8,64,256]{3,2,1,0:T(8,128)(2,1)}, u32[]{:S(2)}, u32[]{:S(2)}) async-start(bf16[8,8,64,256]{3,2,1,0:T(8,128)(2,1)} %bitcast.16), calls=%async_computation.1 | async-start | bytes 4194304 | tf_op jit(solution)/shard_map/all_to_all | solution.py:69
  55.3 0.0 reduce-scatter.2.cloned.1.call-start
  55.3 0.1 fusion.36
  55.4 0.2 slice_reduce_fusion
  55.6 0.1 copy.80
  55.7 0.1 copy.81
  55.8 0.1 copy.61
  55.9 0.1 reshape.76
  56.0 0.9 gather_fusion
  56.9 0.3 reshape.73
  57.2 0.1 copy.62
  57.3 0.3 broadcast_multiply_fusion
  57.6 0.3 copy.63
  57.9 0.1 copy.66
  58.0 0.1 reshape.84
  58.1 0.9 gather_fusion.1
  59.0 0.4 reshape.69
  59.4 33.6 %convert_bitcast_fusion = bf16[64,4,8,8,8,8]{3,4,5,1,2,0:T(8,128)(2,1)} fusion(f32[64,4,4]{1,2,0:T(4,128)S(1)} %fusion.25, f32[64,4,8,8]{3,1,2,0:T(4,128)S(1)} %copy.63, bf16[64,4,8,8,1,1]{3,2,1,0,5,4:T(8,128)(2,1)S(1)} %bitcast.73), kind=kOutput, calls=%fused_computation.14 | convolution fusion | flops 51445760 | bytes 2199552 | tf_op jit(solution)/shard_map/sjr,sjlm,sjnq->srlqmn/dot_general | solution.py:32
  93.0 44.4 %copy.68 = bf16[64,4,8,8,8,8]{0,5,4,3,2,1:T(8,128)(2,1)} copy(bf16[64,4,8,8,8,8]{3,4,5,1,2,0:T(8,128)(2,1)} %convert_bitcast_fusion) | data formatting | bytes 4194304 | tf_op jit(solution)/shard_map/convert_element_type | solution.py:48
  137.4 21.8 %convert_element_type.38 = bf16[4,16,4,64,64]{1,0,4,3,2:T(4,128)(2,1)} reshape(bf16[64,4,8,8,8,8]{0,5,4,3,2,1:T(8,128)(2,1)} %copy.68) | data formatting | bytes 4194304 | tf_op jit(solution)/shard_map/convert_element_type | solution.py:48
  159.3 25.1 %copy.69 = bf16[4,16,4,64,64]{4,3,1,2,0:T(8,128)(2,1)} copy(bf16[4,16,4,64,64]{1,0,4,3,2:T(4,128)(2,1)} %convert_element_type.38) | data formatting | bytes 4194304
  184.4 0.0 all-to-all-done.1
  184.4 0.0 copy-start.1
  184.4 12.6 %while.11 = (s32[]{:T(128)}, f32[4,256,256]{2,1,0:T(8,128)S(1)}, bf16[4,16,4,64,64]{4,3,1,2,0:T(8,128)(2,1)}, bf16[4,16,64,256]{3,2,1,0:T(8,128)(2,1)}, s32[]{:T(128)}, /*index=5*/s32[]{:T(128)}) while((s32[]{:T(128)}, f32[4,256,256]{2,1,0:T(8,128)S(1)}, bf16[4,16,4,64,64]{4,3,1,2,0:T(8,128)(2,1)}, ...), condition=%wide.region_4.5_spmd.clone, body=%wide.region_3.4_spmd.clone.sunk | while | flops 672661504 | bytes 4195919 | solution.py:103
  184.4 3.1 %fusion.51 = f32[4,256,256]{2,1,0:T(8,128)S(1)} fusion(f32[4,256,256]{2,1,0:T(8,128)S(1)} %get-tuple-element.118, bf16[4,16,4,64,64]{4,3,1,2,0:T(8,128)(2,1)} %get-tuple-element.125, s32[]{:T(128)} %get-tuple-element.117, bf16[4,16,64,256]{3,2,1,0:T(8,128)(2,1)} %get-tuple-element.126, pred[]{:T(512)S(6)} %compare.9), kind=kOutput, calls=%fused_computation.8.clone.1 | convolution fusion | flops 672661504 | bytes 4195841 | tf_op jit(solution)/shard_map/while/body/eval_jaxpr/srkp,skq->rpq/dot_general | solution.py:98
  187.5 3.1 %fusion.51 = f32[4,256,256]{2,1,0:T(8,128)S(1)} fusion(f32[4,256,256]{2,1,0:T(8,128)S(1)} %get-tuple-element.118, bf16[4,16,4,64,64]{4,3,1,2,0:T(8,128)(2,1)} %get-tuple-element.125, s32[]{:T(128)} %get-tuple-element.117, bf16[4,16,64,256]{3,2,1,0:T(8,128)(2,1)} %get-tuple-element.126, pred[]{:T(512)S(6)} %compare.9), kind=kOutput, calls=%fused_computation.8.clone.1 | convolution fusion | flops 672661504 | bytes 4195841 | tf_op jit(solution)/shard_map/while/body/eval_jaxpr/srkp,skq->rpq/dot_general | solution.py:98
  190.6 3.1 %fusion.51 = f32[4,256,256]{2,1,0:T(8,128)S(1)} fusion(f32[4,256,256]{2,1,0:T(8,128)S(1)} %get-tuple-element.118, bf16[4,16,4,64,64]{4,3,1,2,0:T(8,128)(2,1)} %get-tuple-element.125, s32[]{:T(128)} %get-tuple-element.117, bf16[4,16,64,256]{3,2,1,0:T(8,128)(2,1)} %get-tuple-element.126, pred[]{:T(512)S(6)} %compare.9), kind=kOutput, calls=%fused_computation.8.clone.1 | convolution fusion | flops 672661504 | bytes 4195841 | tf_op jit(solution)/shard_map/while/body/eval_jaxpr/srkp,skq->rpq/dot_general | solution.py:98
  193.7 3.1 %fusion.51 = f32[4,256,256]{2,1,0:T(8,128)S(1)} fusion(f32[4,256,256]{2,1,0:T(8,128)S(1)} %get-tuple-element.118, bf16[4,16,4,64,64]{4,3,1,2,0:T(8,128)(2,1)} %get-tuple-element.125, s32[]{:T(128)} %get-tuple-element.117, bf16[4,16,64,256]{3,2,1,0:T(8,128)(2,1)} %get-tuple-element.126, pred[]{:T(512)S(6)} %compare.9), kind=kOutput, calls=%fused_computation.8.clone.1 | convolution fusion | flops 672661504 | bytes 4195841 | tf_op jit(solution)/shard_map/while/body/eval_jaxpr/srkp,skq->rpq/dot_general | solution.py:98
  197.0 0.0 copy-start
  197.0 1.0 copy-done
  198.0 0.0 reduce-scatter.2.cloned.1.call-update
  198.0 0.0 copy-done.1
  198.0 0.1 fusion.34
  198.2 0.1 pad_maximum_fusion
  198.2 0.1 dot_general.25
  198.3 28.4 %reduce-scatter.2.cloned.1.call-done = f32[4,64,256]{2,1,0:T(8,128)} async-done(((f32[4,256,256]{2,1,0:T(8,128)}), f32[4,64,256]{2,1,0:T(8,128)}) %reduce-scatter.2.cloned.1.call-update) | async-done | bytes 262160 | tf_op jit(solution)/shard_map/reduce_scatter | solution.py:111
  226.7 7.7 %convolution_bitcast_fusion = f32[2,64,1,64,256]{4,1,3,0,2:T(8,128)S(1)} fusion(f32[2,64,4,1]{1,0,2,3:T(2,128)S(1)} %bitcast.79, f32[1,4,64,256]{3,2,1,0:T(8,128)} %bitcast.78), kind=kOutput, calls=%fused_computation.17 | convolution fusion | flops 100663296 | bytes 8652800 | tf_op jit(solution)/shard_map/dot_general | solution.py:120
  234.4 8.3 %copy.71 = f32[2,64,1,64,256]{4,3,2,1,0:T(8,128)} copy(f32[2,64,1,64,256]{4,1,3,0,2:T(8,128)S(1)} %convolution_bitcast_fusion) | data formatting | bytes 16777216 | tf_op jit(solution)/shard_map/dot_general | solution.py:120
  (8 shorter events, 0.1 us)
Async XLA Ops:
  10.8 40.1 %all-to-all-start = ((s32[8,8,14]{2,1,0:T(8,128)}), s32[8,8,14]{2,1,0:T(8,128)S(1)}, u32[]{:S(2)}, u32[]{:S(2)}) async-start(s32[8,8,14]{2,1,0:T(8,128)} %bitcast.9), calls=%async_computation | async-start | bytes 65536 | tf_op jit(solution)/shard_map/all_to_all | solution.py:76
  50.9 133.5 %all-to-all-start.1 = ((bf16[8,8,64,256]{3,2,1,0:T(8,128)(2,1)}), bf16[8,8,64,256]{3,2,1,0:T(8,128)(2,1)}, u32[]{:S(2)}, u32[]{:S(2)}) async-start(bf16[8,8,64,256]{3,2,1,0:T(8,128)(2,1)} %bitcast.16), calls=%async_computation.1 | async-start | bytes 4194304 | tf_op jit(solution)/shard_map/all_to_all | solution.py:69
  55.3 171.4 %reduce-scatter.2.cloned.1.call-start = ((), (), s32[]{:S(2)}) async-start(), calls=%async_computation.3 | async-start | bytes 1310720 | tf_op jit(solution)/shard_map/reduce_scatter | solution.py:111
  184.4 13.6 %copy-start.1 = (s32[4,2]{0,1:T(2,128)S(1)}, s32[4,2]{0,1:T(2,128)}, u32[]{:S(2)}) copy-start(s32[4,2]{0,1:T(2,128)} %param.15) | copy-start | bytes 100
  197.0 1.0 copy-start
Sparse Core Ops, SparseCore 0:
  198.1 28.5 reduce-scatter.1
where the time goes:
time: 252 us; the launch traced here: 250 us
  local copies, waits for them, and re-layouts  114 us (45%)
  matrix products  53.7 us (21%)
  waiting for transfers between devices  28.4 us (11%)
  blocking collectives  27.7 us (11%)
  between operations  13.6 us (5%)
  starting transfers between devices  9.56 us (4%)
  other arithmetic  2.9 us (1%)
    convert_element_type x2, local copies, waits for them, and re-layouts, operators(): return summed.astype(jnp.bfloat16)  66.3 us
    dot_general x1, matrix products, density_terms(): jnp.einsum('sjr,sjlm,sjnq->srlqmn', select, occ_vals.reshape(row_count, p...  33.6 us
    reduce_scatter x1, waiting for transfers between devices, local(): lax.psum_scatter(chi_cells, 'image', scatter_dimension=1, tiled=True)  28.4 us
    unnamed x7, local copies, waits for them, and re-layouts  26.2 us
    all_gather x1, blocking collectives, operators(): lax.all_gather(virt_local, 'image', axis=0, tiled=True)  13.9 us
    all_gather x1, blocking collectives, operators(): lax.all_gather(occ_local, 'image', axis=0, tiled=True)  13.8 us
    dot_general x4, matrix products, accumulate(): jnp.einsum('srkp,skq->rpq', mixed_rows, blk_part, preferred_element_type=...  12.3 us
    dot_general x2, local copies, waits for them, and re-layouts, local(): jnp.dot(phases, chi_share.reshape(cell_count, share_rows * ri_width), pre...  8.34 us
  transfers between devices with their start and end apart: 3, of which 1 were waited for; matrix products, arithmetic and copies ran while one was open for 55% of the time, Pallas kernels for 0%

commit v1 on v0

v1 whole, which is shorter than its diff:
```python
import functools
import math

import jax
import jax.numpy as jnp
from jax import lax
from jax.experimental import pallas as pl
from jax.experimental.pallas import tpu as pltpu
from jax.sharding import PartitionSpec as P

KGRID = 8
QUAD = 4
LIST_ROWS = 16
BF16 = jnp.bfloat16
F32 = jnp.float32
VMEM_LIMIT = 48 * 1024 * 1024


def iota(shape, dim):
    return lax.broadcasted_iota(jnp.int32, shape, dim)


def pack_kernel(
    n, cap, pairs, owner_s, owner_v, basis, images, cells, blocks, *rest
):
    outs, (nothing, table, lists, count, place, sems, list_sems) = rest[:n], rest[n:]
    rows, square, width = blocks.shape
    me = lax.axis_index("ri")
    nothing[...] = jnp.zeros_like(nothing)
    for k in range(n):
        count[k] = 0

    @pl.loop(0, rows)
    def _(e):
        k = owner_s[0, e] ^ me
        r = count[k]
        place[k * cap + r] = e
        count[k] = r + 1

    def slot(k, r, source):
        return pltpu.make_async_copy(
            source, outs[k].at[pl.ds(r * square, square)], sems.at[k * cap + r]
        )

    for k in range(n):
        for r in range(cap):
            used = r < count[k]

            @pl.when(used)
            def _():
                slot(k, r, blocks.at[place[k * cap + r]]).start()

            @pl.when(jnp.logical_not(used))
            def _():
                slot(k, r, nothing).start()

    distance = owner_v[...] ^ me
    as_column = jnp.sum(
        jnp.where(iota((rows, rows), 0) == iota((rows, rows), 1), distance, 0),
        axis=1,
        keepdims=True,
    )
    before = (as_column == distance) & (iota((rows, rows), 0) < iota((rows, rows), 1))
    rank = jnp.sum(before.astype(jnp.int32), axis=0, keepdims=True)
    chosen = iota((n * LIST_ROWS, rows), 0) == distance * LIST_ROWS + rank
    table[...] = jnp.zeros_like(table)
    table[0:2, :] = basis[...].astype(F32)
    table[2 : 2 + pairs, :] = images[0].astype(F32)
    table[2 + pairs : 2 + 2 * pairs, :] = images[1].astype(F32)
    table[2 + 2 * pairs : 2 + 3 * pairs, :] = cells[...].astype(F32)
    ordered = lax.dot_general(
        chosen.astype(BF16),
        table[...].astype(BF16),
        (((1,), (1,)), ((), ())),
        preferred_element_type=F32,
    )
    lists[:, 0:128] = ordered.astype(BF16)
    lists[:, 128:width] = jnp.zeros((n * LIST_ROWS, width - 128), BF16)

    def list_copy(k):
        return pltpu.make_async_copy(
            lists.at[pl.ds(k * LIST_ROWS, LIST_ROWS)],
            outs[k].at[pl.ds(cap * square, LIST_ROWS)],
            list_sems.at[k],
        )

    for k in range(n):
        list_copy(k).start()
    for k in range(n):
        for r in range(cap):
            slot(k, r, nothing).wait()
        list_copy(k).wait()


def pack(n, cap, blocks, block_owner, block_basis, pair_images, pair_cell):
    rows, square, width = blocks.shape
    pairs = pair_cell.shape[1]
    owner = block_owner.T
    vmem = pl.BlockSpec(memory_space=pltpu.VMEM)
    payload = jax.ShapeDtypeStruct((cap * square + LIST_ROWS, width), BF16)
    return pl.pallas_call(
        functools.partial(pack_kernel, n, cap, pairs),
        out_shape=[payload] * n,
        in_specs=[pl.BlockSpec(memory_space=pltpu.SMEM), vmem, vmem, vmem, vmem]
        + [pl.BlockSpec(memory_space=pl.ANY)],
        out_specs=[pl.BlockSpec(memory_space=pl.ANY)] * n,
        scratch_shapes=[
            pltpu.VMEM((square, width), BF16),
            pltpu.VMEM((128, rows), F32),
            pltpu.VMEM((n * LIST_ROWS, width), BF16),
            pltpu.SMEM((n,), jnp.int32),
            pltpu.SMEM((n * cap,), jnp.int32),
            pltpu.SemaphoreType.DMA((n * cap,)),
            pltpu.SemaphoreType.DMA((n,)),
        ],
        compiler_params=pltpu.CompilerParams(vmem_limit_bytes=VMEM_LIMIT),
        cost_estimate=pl.CostEstimate(flops=0, bytes_accessed=6 << 20, transcendentals=0),
        name="pack_by_owner",
    )(
        owner,
        owner,
        block_basis.T,
        jnp.transpose(pair_images, (1, 2, 0)),
        pair_cell.T,
        blocks,
    )


def dot(a, b, contract=(1, 0)):
    return lax.dot_general(
        a, b, (((contract[0],), (contract[1],)), ((), ())), preferred_element_type=F32
    )


def chi_kernel(cap, pairs, cell_count, first, last, *refs):
    refs = list(refs)
    images = lax.axis_size("image")
    payloads = [refs.pop(0) for _ in range(QUAD)]
    pieces = [refs.pop(0) for _ in range(images)]
    before = None if first else refs.pop(0)
    if last:
        own, *sends = [refs.pop(0) for _ in range(images)]
        total = refs.pop(0)
    else:
        total = refs.pop(0)
    mixed, stacked = refs
    z = lax.axis_index("image")
    width = payloads[0].shape[1]
    square = (payloads[0].shape[0] - LIST_ROWS) // cap
    side = math.isqrt(square)
    lanes = QUAD * square
    list_at = cap * square

    lane = iota((1, lanes), 1)
    listing = jnp.concatenate(
        [p[list_at : list_at + LIST_ROWS, 0:128].astype(F32)[0:8] for p in payloads], axis=0
    )

    def columns(start):
        return jnp.concatenate(
            [listing[:, start + j : start + j + 1] for j in range(pairs)], axis=0
        ).astype(jnp.int32)

    def to_lanes(rows):
        out = []
        for j in range(pairs):
            acc = 0.0
            for s in range(QUAD):
                at = (j * QUAD + s) * 8
                acc = acc + jnp.where(lane // square == s, rows[at : at + 8], 0.0)
            out.append(acc)
        return out

    def density_rows(basis_at, image_at, piece_at):
        block = jnp.concatenate([listing[:, basis_at : basis_at + 1]] * pairs, axis=0)
        block = block.astype(jnp.int32)
        image = columns(image_at) ^ z
        block_count = pieces[0].shape[1]
        hit = iota((QUAD * 8 * pairs, block_count), 1) == block
        found = 0.0
        for i in range(images):
            part = pieces[i][piece_at : piece_at + square, :]
            chosen = jnp.where(hit & (image == i), 1.0, 0.0).astype(BF16)
            found = found + dot(chosen, jnp.concatenate([part] * QUAD, axis=0), (1, 1))
        return to_lanes(found)

    occ = density_rows(0, 2, 0)
    virt = density_rows(1, 2 + pairs, square)
    cell = to_lanes(columns(2 + 2 * pairs).astype(F32))

    shape = (square, lanes)
    occ_mask = (iota(shape, 1) % side == iota(shape, 0) // side).astype(BF16)
    virt_mask = (iota(shape, 1) % square // side == iota(shape, 0) % side).astype(BF16)
    shape = (lanes, lanes)
    occ_spread = (iota(shape, 0) // side == iota(shape, 1) // side).astype(BF16)
    virt_spread = (
        (iota(shape, 0) // square == iota(shape, 1) // square)
        & (iota(shape, 0) % side == iota(shape, 1) % side)
    ).astype(BF16)
    own_lanes = [(lane // square == s) for s in range(QUAD)]

    for r in range(cap):
        rows = slice(r * square, (r + 1) * square)
        block = jnp.concatenate([p[rows, :] for p in payloads], axis=0)
        stacked[r * lanes : (r + 1) * lanes, :] = block
        turned = block.T
        occ_in = jnp.concatenate([occ_mask * o[r : r + 1].astype(BF16) for o in occ], axis=0)
        virt_in = jnp.concatenate([virt_mask * v[r : r + 1].astype(BF16) for v in virt], axis=0)
        terms = dot(occ_in, occ_spread) * dot(virt_in, virt_spread)
        for c in range(cell_count):
            op = 0.0
            for j in range(pairs):
                here = cell[j][r : r + 1] == float(c)
                op = op + jnp.where(here, terms[j * square : (j + 1) * square], 0.0)
            diagonal = jnp.concatenate([jnp.where(m, op, 0.0) for m in own_lanes], axis=0)
            mixed[c, :, r * lanes : (r + 1) * lanes] = dot(turned, diagonal.astype(BF16)).astype(
                BF16
            )
    for c in range(cell_count):
        acc = dot(mixed[c], stacked[...])
        if not first:
            acc = acc + before[c]
        total[c] = acc
    if last:
        share = own.shape[1]
        own[...] = total[:, pl.ds(pl.multiple_of(z * share, share), share), :]
        for k in range(1, images):
            at = pl.multiple_of((z ^ k) * share, share)
            sends[k - 1][...] = total[:, pl.ds(at, share), :].astype(BF16)


def chi_part(cap, pairs, cell_count, payloads, pieces, before, last):
    images = len(pieces)
    width = payloads[0].shape[1]
    square = (payloads[0].shape[0] - LIST_ROWS) // cap
    vmem = pl.BlockSpec(memory_space=pltpu.VMEM)
    full = jax.ShapeDtypeStruct((cell_count, width, width), F32)
    share = (cell_count, width // images, width)
    args = list(payloads) + list(pieces) + ([] if before is None else [before])
    scratch = [
        pltpu.VMEM((cell_count, width, cap * QUAD * square), BF16),
        pltpu.VMEM((cap * QUAD * square, width), BF16),
    ]
    if last:
        out_shape = [jax.ShapeDtypeStruct(share, F32)] + [jax.ShapeDtypeStruct(share, BF16)] * (
            images - 1
        )
        scratch = [pltpu.VMEM(full.shape, F32)] + scratch
    else:
        out_shape = [full]
    return pl.pallas_call(
        functools.partial(chi_kernel, cap, pairs, cell_count, before is None, last),
        out_shape=out_shape,
        in_specs=[vmem] * len(args),
        out_specs=[vmem] * len(out_shape),
        scratch_shapes=scratch,
        compiler_params=pltpu.CompilerParams(vmem_limit_bytes=VMEM_LIMIT),
        cost_estimate=pl.CostEstimate(
            flops=2 * cap * QUAD * 3 * square * cell_count * width * width // 2,
            bytes_accessed=4 << 20,
            transcendentals=0,
        ),
        name="chi_of_payloads",
    )(*args)


def transform_kernel(cell_count, phases, own, *rest):
    *received, out, total = rest

    @pl.when(pl.program_id(0) == 0)
    def _():
        acc = own[...]
        for part in received:
            acc = acc + part[...].astype(F32)
        total[...] = acc

    points = out.shape[0]
    base = pl.program_id(0) * points
    for row in range(0, out.shape[1], 8):
        parts = [total[c, row : row + 8, :] for c in range(cell_count)]
        for i in range(points):
            acc = phases[base + i, 0] * parts[0]
            for c in range(1, cell_count):
                acc = acc + phases[base + i, c] * parts[c]
            out[i, row : row + 8, :] = acc


def transform(phases, own, received):
    cell_count, share, width = own.shape
    points = phases.shape[0]
    step = 8
    whole = pl.BlockSpec((cell_count, share, width), lambda i: (0, 0, 0))
    return pl.pallas_call(
        functools.partial(transform_kernel, cell_count),
        grid=(points // step,),
        out_shape=jax.ShapeDtypeStruct((points, share, width), F32),
        in_specs=[pl.BlockSpec(memory_space=pltpu.SMEM)] + [whole] * (1 + len(received)),
        out_specs=pl.BlockSpec((step, share, width), lambda i: (i, 0, 0)),
        scratch_shapes=[pltpu.VMEM((cell_count, share, width), F32)],
        compiler_params=pltpu.CompilerParams(vmem_limit_bytes=VMEM_LIMIT),
        cost_estimate=pl.CostEstimate(
            flops=2 * points * cell_count * share * width,
            bytes_accessed=points * share * width * 4,
            transcendentals=0,
        ),
        name="to_k_points",
    )(phases, own, *received)


def swap(array, axis, k):
    size = lax.axis_size(axis)
    return lax.ppermute(array, axis, [(i, i ^ k) for i in range(size)])


def local(blocks, block_owner, block_basis, pair_images, pair_cell, lattice, dens_occ, dens_virt):
    owners, images = lax.axis_size("ri"), lax.axis_size("image")
    pairs = pair_cell.shape[1]
    cell_count = lattice.shape[0]
    cap = max(2, (2 * blocks.shape[0] + owners - 1) // owners)

    packed = pack(owners, cap, blocks, block_owner, block_basis, pair_images, pair_cell)
    density = jnp.concatenate([dens_occ[0].T, dens_virt[0].T], axis=0)
    pieces = [density] + [swap(density, "image", k) for k in range(1, images)]
    payloads = [packed[0]] + [swap(packed[k], "ri", k) for k in range(1, owners)]

    chi = None
    for at in range(0, owners, QUAD):
        last = at + QUAD >= owners
        out = chi_part(cap, pairs, cell_count, payloads[at : at + QUAD], pieces, chi, last)
        chi = out[0]
    own, sends = out[0], out[1:]
    received = [swap(sends[k - 1], "image", k) for k in range(1, images)]

    points = jnp.arange(KGRID * KGRID, dtype=jnp.int32)
    wrapped = (
        (points // KGRID)[:, None] * lattice[None, :, 0]
        + (points % KGRID)[:, None] * lattice[None, :, 1]
    ) % KGRID
    angles = 2.0 * math.pi / KGRID * wrapped.astype(F32)
    phases = jnp.concatenate([jnp.cos(angles), jnp.sin(angles)], axis=0)
    result = transform(phases, own, received)
    return result.reshape(2, KGRID * KGRID, 1, own.shape[1], own.shape[2])


def solution(mesh):
    placed = (
        P(("image", "ri"), None, None),
        P(("image", "ri"), None),
        P(("image", "ri"), None),
        P(("image", "ri"), None, None),
        P(("image", "ri"), None),
        P(),
        P("image", None, None),
        P("image", None, None),
    )
    return jax.shard_map(
        local,
        mesh=mesh,
        in_specs=placed,
        out_specs=P(None, None, "ri", "image", None),
        check_vma=False,
    )
```

time: 252 us -> 77.9 us (0.31)
  local copies, waits for them, and re-layouts: 114 us -> 4.8 us
  matrix products: 53.7 us -> 0 us
  blocking collectives: 27.7 us -> 0 us
  Pallas kernels: 0 us -> 25 us
  between operations: 13.6 us -> 0.08 us
  starting transfers between devices: 9.56 us -> 17.5 us
    convert_element_type x4 -> x0, local copies, waits for them, and re-layouts: 66.7 us -> none  [the longest x2 66.3 us: operators(): return summed.astype(jnp.bfloat16)]
    dot_general x6 -> x0, matrix products: 53.7 us -> none  [the longest x1 33.6 us: density_terms(): jnp.einsum('sjr,sjlm,sjnq->srlqmn', select, occ_vals.reshape(row_count, p...]
    ppermute x0 -> x13, waiting for transfers between devices: none -> 29.4 us  [swap(): return lax.ppermute(array, axis, [(i, i ^ k) for i in range(size)])]
    reduce_scatter x1 -> x0, waiting for transfers between devices: 28.4 us -> none  [local(): lax.psum_scatter(chi_cells, 'image', scatter_dimension=1, tiled=True)]
    all_gather x2 -> x0, blocking collectives: 27.7 us -> none  [the longest x1 13.9 us: operators(): lax.all_gather(virt_local, 'image', axis=0, tiled=True)]
    pallas_call x0 -> x4, Pallas kernels: none -> 25 us  [the longest x1 9.82 us: transform(): pl.pallas_call(functools.partial(transform_kernel, cell_count), grid=(poi...]
    unnamed x7 -> x10, local copies, waits for them, and re-layouts: 26.2 us -> 3.92 us
    ppermute x0 -> x13, starting transfers between devices: none -> 17.5 us  [swap(): return lax.ppermute(array, axis, [(i, i ^ k) for i in range(size)])]
  transfers between devices with their start and end apart: 3 -> 13, of which waited for: 1 -> 5; matrix products, arithmetic and copies ran while one was open for 55% -> 2% of each run, Pallas kernels for 0% -> 6%
where the time goes in v1:
time: 77.9 us; the launch traced here: 77.6 us
  waiting for transfers between devices  29.4 us (38%)
  Pallas kernels  25 us (32%)
  starting transfers between devices  17.5 us (22%)
  local copies, waits for them, and re-layouts  4.8 us (6%)
  other arithmetic  0.98 us (1%)
    ppermute x13, waiting for transfers between devices, swap(): return lax.ppermute(array, axis, [(i, i ^ k) for i in range(size)])  29.4 us
    ppermute x13, starting transfers between devices, swap(): return lax.ppermute(array, axis, [(i, i ^ k) for i in range(size)])  17.5 us
    pallas_call x1, Pallas kernels, transform(): pl.pallas_call(functools.partial(transform_kernel, cell_count), grid=(poi...  9.82 us
    pallas_call x2, Pallas kernels, chi_part(): pl.pallas_call(functools.partial(chi_kernel, cap, pairs, cell_count, befo...  9.61 us
    pallas_call x1, Pallas kernels, pack(): pl.pallas_call(functools.partial(pack_kernel, n, cap, pairs), out_shape=[...  5.53 us
    unnamed x10, local copies, waits for them, and re-layouts  3.92 us
  transfers between devices with their start and end apart: 13, of which 5 were waited for; matrix products, arithmetic and copies ran while one was open for 2% of the time, Pallas kernels for 6%

profile of v1, /device:TPU:0, one launch (start us, length us, event | category | flops | bytes accessed | tf_op | source)
XLA Modules:
  0.0 77.6 jit_solution(4234465047847341545)
XLA Ops:
  0.0 0.0 copy-start
  0.0 1.2 %copy-done = bf16[32,64,256]{2,1,0:T(8,128)(2,1)S(1)} copy-done((bf16[32,64,256]{2,1,0:T(8,128)(2,1)S(1)}, bf16[32,64,256]{2,1,0:T(8,128)(2,1)}, u32[]{:S(2)}) %copy-start) | copy-done | bytes 1048600
  1.2 0.0 copy-start.1
  1.2 0.7 copy-done.1
  1.9 0.0 copy-start.2
  1.9 0.7 copy-done.2
  2.6 0.0 copy-start.3
  2.6 0.7 copy-done.3
  3.3 0.0 copy-start.4
  3.3 0.7 copy-done.4
  3.9 5.5 %pack_by_owner.1 = (bf16[528,256]{1,0:T(8,128)(2,1)S(1)}, bf16[528,256]{1,0:T(8,128)(2,1)S(1)}, bf16[528,256]{1,0:T(8,128)(2,1)S(1)}, bf16[528,256]{1,0:T(8,128)...) custom-call(s32[1,32]{1,0:T(1,128)S(1)} %bitcast.19, ...), custom_call_target="tpu_custom_call" | custom-call | bytes 6291456 | tf_op jit(solution)/shard_map/pack_by_owner/pallas_call | solution.py:101
  9.5 0.5 collective-permute-start.7
  10.0 2.6 %collective-permute-start.8 = (bf16[528,256]{1,0:T(8,128)(2,1)S(1)}, bf16[528,256]{1,0:T(8,128)(2,1)S(1)}, u32[]{:S(2)}, u32[]{:S(2)}) collective-permute-start(bf16[528,256]{1,0:T(8,128)(2,1)S(1)} %get-tuple-element.23), channel_id=1, source_target_pairs={{0,2},{1,3},{2,0},{3,1},{4,6},{5,7},{6,4},{7,5},{8,10},{9,11},{10,... | collective-permute-start | bytes 811016 | tf_op jit(solution)/shard_map/ppermute | solution.py:312
  12.6 0.8 %pad_maximum_fusion.refs_4_ = bf16[128,256]{1,0:T(8,128)(2,1)S(1)} fusion(bf16[64,256]{1,0:T(8,128)(2,1)} %bitcast.22, bf16[64,256]{1,0:T(8,128)(2,1)} %bitcast.23), kind=kLoop, calls=%fused_computation | loop fusion | flops 131072 | bytes 131072 | tf_op jit(solution)/shard_map/concatenate | solution.py:322
  13.3 3.6 %collective-permute-start.6 = (bf16[128,256]{1,0:T(8,128)(2,1)S(1)}, bf16[128,256]{1,0:T(8,128)(2,1)S(1)}, u32[]{:S(2)}, u32[]{:S(2)}) collective-permute-start(bf16[128,256]{1,0:T(8,128)(2,1)S(1)} %pad_maximum_fusion.refs_4_), channel_id=1, source_target_pairs={{0,24},{8,16},{16,8},{24,0},{1,25},{9,17},{17,9},{25,1},{2,26},{10... | collective-permute-start | bytes 196616 | tf_op jit(solution)/shard_map/ppermute | solution.py:312
  16.9 0.0 collective-permute-start.5
  16.9 0.8 %collective-permute-start.4 = (bf16[128,256]{1,0:T(8,128)(2,1)S(1)}, bf16[128,256]{1,0:T(8,128)(2,1)S(1)}, u32[]{:S(2)}, u32[]{:S(2)}) collective-permute-start(bf16[128,256]{1,0:T(8,128)(2,1)S(1)} %pad_maximum_fusion.refs_4_), channel_id=1, source_target_pairs={{0,8},{8,0},{16,24},{24,16},{1,9},{9,1},{17,25},{25,17},{2,10},{10... | collective-permute-start | bytes 196616 | tf_op jit(solution)/shard_map/ppermute | solution.py:312
  17.7 1.9 %collective-permute-done.6.refs_7_ = bf16[128,256]{1,0:T(8,128)(2,1)S(1)} collective-permute-done((bf16[128,256]{1,0:T(8,128)(2,1)S(1)}, bf16[128,256]{1,0:T(8,128)(2,1)S(1)}, u32[]{:S(2)}, u32[]{:S(2)}) %collective-permute-start.6) | collective-permute-done | bytes 65568 | tf_op jit(solution)/shard_map/ppermute | solution.py:312
  19.6 1.5 %collective-permute-start = (bf16[528,256]{1,0:T(8,128)(2,1)S(1)}, bf16[528,256]{1,0:T(8,128)(2,1)S(1)}, u32[]{:S(2)}, u32[]{:S(2)}) collective-permute-start(bf16[528,256]{1,0:T(8,128)(2,1)S(1)} %get-tuple-element.17), channel_id=1, source_target_pairs={{0,4},{1,5},{2,6},{3,7},{4,0},{5,1},{6,2},{7,3},{8,12},{9,13},{10,... | collective-permute-start | bytes 811016 | tf_op jit(solution)/shard_map/ppermute | solution.py:312
  21.1 1.7 %collective-permute-done.5.refs_6_ = bf16[128,256]{1,0:T(8,128)(2,1)S(1)} collective-permute-done((bf16[128,256]{1,0:T(8,128)(2,1)S(1)}, bf16[128,256]{1,0:T(8,128)(2,1)S(1)}, u32[]{:S(2)}, u32[]{:S(2)}) %collective-permute-start.5) | collective-permute-done | bytes 65568 | tf_op jit(solution)/shard_map/ppermute | solution.py:312
  22.8 0.8 %collective-permute-start.1 = (bf16[528,256]{1,0:T(8,128)(2,1)S(1)}, bf16[528,256]{1,0:T(8,128)(2,1)S(1)}, u32[]{:S(2)}, u32[]{:S(2)}) collective-permute-start(bf16[528,256]{1,0:T(8,128)(2,1)S(1)} %get-tuple-element.18), channel_id=1, source_target_pairs={{0,5},{1,4},{2,7},{3,6},{4,1},{5,0},{6,3},{7,2},{8,13},{9,12},{10,... | collective-permute-start | bytes 811016 | tf_op jit(solution)/shard_map/ppermute | solution.py:312
  23.7 0.0 collective-permute-done.4.refs_5_
  23.7 0.7 collective-permute-start.2
  24.3 0.0 collective-permute-done.7.refs_1_
  24.3 2.4 %collective-permute-start.3 = (bf16[528,256]{1,0:T(8,128)(2,1)S(1)}, bf16[528,256]{1,0:T(8,128)(2,1)S(1)}, u32[]{:S(2)}, u32[]{:S(2)}) collective-permute-start(bf16[528,256]{1,0:T(8,128)(2,1)S(1)} %get-tuple-element.20), channel_id=1, source_target_pairs={{0,7},{1,6},{2,5},{3,4},{4,3},{5,2},{6,1},{7,0},{8,15},{9,14},{10,... | collective-permute-start | bytes 811016 | tf_op jit(solution)/shard_map/ppermute | solution.py:312
  26.7 0.0 collective-permute-done.8.refs_2_
  26.7 0.1 collective-permute-start.9
  26.8 0.8 slice_bitcast_fusion.1
  27.6 16.6 %collective-permute-done.9.refs_3_ = bf16[528,256]{1,0:T(8,128)(2,1)S(1)} collective-permute-done((bf16[528,256]{1,0:T(8,128)(2,1)S(1)}, bf16[528,256]{1,0:T(8,128)(2,1)S(1)}, u32[]{:S(2)}, u32[]{:S(2)}) %collective-permute-start.9) | collective-permute-done | bytes 270368 | tf_op jit(solution)/shard_map/ppermute | solution.py:312
  44.2 4.7 %chi_of_payloads.2.refs_8_ = f32[4,256,256]{2,1,0:T(8,128)S(1)} custom-call(bf16[528,256]{1,0:T(8,128)(2,1)S(1)} %get-tuple-element.21.refs_0_, bf16[528,256]{1,0:T(8,128)(2,1)S(1)} %collective-permute-done.7.refs_1_, bf16[528,256]{1,0:T(8,128)(2,1)S(1)} %collective-permute-done.8.refs_2_, bf16[528,256]{1,0:T(8,128)(2,1)S(1)} %collective-permute-done.9.refs_3_, ...), custom_call_target="tpu_custom_call" | custom-call | flops 1610612736 | bytes 4194304 | tf_op jit(solution)/shard_map/chi_of_payloads/pallas_call | solution.py:251
  48.9 0.0 collective-permute-done.refs_0_
  48.9 0.0 collective-permute-done.1.refs_1_
  48.9 0.0 collective-permute-done.2.refs_2_
  48.9 0.0 collective-permute-done.3.refs_3_
  49.0 4.9 %chi_of_payloads.3 = (f32[4,64,256]{2,1,0:T(8,128)S(1)}, bf16[4,64,256]{2,1,0:T(8,128)(2,1)S(1)}, bf16[4,64,256]{2,1,0:T(8,128)(2,1)S(1)}, bf16[4,64,256]{2,1,0:T(8,128)(2,1)S(1)}) custom-call(bf16[528,256]{1,0:T(8,128)(2,1)S(1)} %collective-permute-done.refs_0_, bf16[528,256]{1,0:T(8,128)(2,1)S(1)} %collective-permute-done.1.refs_1_, ...), custom_call_target="tpu_custom_call" | custom-call | flops 1610612736 | bytes 4194304 | tf_op jit(solution)/shard_map/chi_of_payloads/pallas_call | solution.py:251
  53.8 1.1 %collective-permute-start.10 = (bf16[4,64,256]{2,1,0:T(8,128)(2,1)S(1)}, bf16[4,64,256]{2,1,0:T(8,128)(2,1)S(1)}, u32[]{:S(2)}, u32[]{:S(2)}) collective-permute-start(bf16[4,64,256]{2,1,0:T(8,128)(2,1)S(1)} %get-tuple-element.26), channel_id=1, source_target_pairs={{0,8},{8,0},{16,24},{24,16},{1,9},{9,1},{17,25},{25,17},{2,10},{10... | collective-permute-start | bytes 393224 | tf_op jit(solution)/shard_map/ppermute | solution.py:312
  54.9 2.0 %collective-permute-start.11 = (bf16[4,64,256]{2,1,0:T(8,128)(2,1)S(1)}, bf16[4,64,256]{2,1,0:T(8,128)(2,1)S(1)}, u32[]{:S(2)}, u32[]{:S(2)}) collective-permute-start(bf16[4,64,256]{2,1,0:T(8,128)(2,1)S(1)} %get-tuple-element.27), channel_id=1, source_target_pairs={{0,16},{8,24},{16,0},{24,8},{1,17},{9,25},{17,1},{25,9},{2,18},{10... | collective-permute-start | bytes 393224 | tf_op jit(solution)/shard_map/ppermute | solution.py:312
  56.9 1.3 %collective-permute-start.12 = (bf16[4,64,256]{2,1,0:T(8,128)(2,1)S(1)}, bf16[4,64,256]{2,1,0:T(8,128)(2,1)S(1)}, u32[]{:S(2)}, u32[]{:S(2)}) collective-permute-start(bf16[4,64,256]{2,1,0:T(8,128)(2,1)S(1)} %get-tuple-element.28), channel_id=1, source_target_pairs={{0,24},{8,16},{16,8},{24,0},{1,25},{9,17},{17,9},{25,1},{2,26},{10... | collective-permute-start | bytes 393224 | tf_op jit(solution)/shard_map/ppermute | solution.py:312
  58.3 0.1 fusion.4
  58.4 0.1 pad_maximum_fusion.1
  58.5 0.1 copy.10.phases
  58.6 2.6 %collective-permute-done.10.rest_0_ = bf16[4,64,256]{2,1,0:T(8,128)(2,1)S(1)} collective-permute-done((bf16[4,64,256]{2,1,0:T(8,128)(2,1)S(1)}, bf16[4,64,256]{2,1,0:T(8,128)(2,1)S(1)}, u32[]{:S(2)}, u32[]{:S(2)}) %collective-permute-start.10) | collective-permute-done | bytes 131104 | tf_op jit(solution)/shard_map/ppermute | solution.py:312
  61.2 6.6 %collective-permute-done.11.rest_1_ = bf16[4,64,256]{2,1,0:T(8,128)(2,1)S(1)} collective-permute-done((bf16[4,64,256]{2,1,0:T(8,128)(2,1)S(1)}, bf16[4,64,256]{2,1,0:T(8,128)(2,1)S(1)}, u32[]{:S(2)}, u32[]{:S(2)}) %collective-permute-start.11) | collective-permute-done | bytes 131104 | tf_op jit(solution)/shard_map/ppermute | solution.py:312
  67.8 0.0 collective-permute-done.12.rest_2_
  67.8 9.8 %to_k_points.1 = f32[128,64,256]{2,1,0:T(8,128)} custom-call(f32[128,4]{1,0:T(8,128)S(1)} %copy.10.phases, f32[4,64,256]{2,1,0:T(8,128)S(1)} %get-tuple-element.25.own, bf16[4,64,256]{2,1,0:T(8,128)(2,1)S(1)} %collective-permute-done.10.rest_0_, bf16[4,64,256]{2,1,0:T(8,128)(2,1)S(1)} %collective-permute-done.11.rest_1_, ...), custom_call_target="tpu_custom_call" | custom-call | flops 16777216 | bytes 8388608 | tf_op jit(solution)/shard_map/to_k_points/pallas_call | solution.py:293
  (1 shorter events, 0.0 us)
Async XLA Ops:
  0.0 1.2 %copy-start = (bf16[32,64,256]{2,1,0:T(8,128)(2,1)S(1)}, bf16[32,64,256]{2,1,0:T(8,128)(2,1)}, u32[]{:S(2)}) copy-start(bf16[32,64,256]{2,1,0:T(8,128)(2,1)} %blocks.1) | copy-start | bytes 3145732
  1.2 0.7 copy-start.1
  1.9 0.7 copy-start.2
  2.6 0.7 copy-start.3
  3.3 0.7 copy-start.4
  9.5 14.9 %collective-permute-start.7 = (bf16[528,256]{1,0:T(8,128)(2,1)S(1)}, bf16[528,256]{1,0:T(8,128)(2,1)S(1)}, u32[]{:S(2)}, u32[]{:S(2)}) collective-permute-start(bf16[528,256]{1,0:T(8,128)(2,1)S(1)} %get-tuple-element.22), channel_id=1, source_target_pairs={{0,1},{1,0},{2,3},{3,2},{4,5},{5,4},{6,7},{7,6},{8,9},{9,8},{10,11... | collective-permute-start | bytes 811016 | tf_op jit(solution)/shard_map/ppermute | solution.py:312
  10.0 16.7 %collective-permute-start.8 = (bf16[528,256]{1,0:T(8,128)(2,1)S(1)}, bf16[528,256]{1,0:T(8,128)(2,1)S(1)}, u32[]{:S(2)}, u32[]{:S(2)}) collective-permute-start(bf16[528,256]{1,0:T(8,128)(2,1)S(1)} %get-tuple-element.23), channel_id=1, source_target_pairs={{0,2},{1,3},{2,0},{3,1},{4,6},{5,7},{6,4},{7,5},{8,10},{9,11},{10,... | collective-permute-start | bytes 811016 | tf_op jit(solution)/shard_map/ppermute | solution.py:312
  13.3 6.3 %collective-permute-start.6 = (bf16[128,256]{1,0:T(8,128)(2,1)S(1)}, bf16[128,256]{1,0:T(8,128)(2,1)S(1)}, u32[]{:S(2)}, u32[]{:S(2)}) collective-permute-start(bf16[128,256]{1,0:T(8,128)(2,1)S(1)} %pad_maximum_fusion.refs_4_), channel_id=1, source_target_pairs={{0,24},{8,16},{16,8},{24,0},{1,25},{9,17},{17,9},{25,1},{2,26},{10... | collective-permute-start | bytes 196616 | tf_op jit(solution)/shard_map/ppermute | solution.py:312
  16.9 5.9 %collective-permute-start.5 = (bf16[128,256]{1,0:T(8,128)(2,1)S(1)}, bf16[128,256]{1,0:T(8,128)(2,1)S(1)}, u32[]{:S(2)}, u32[]{:S(2)}) collective-permute-start(bf16[128,256]{1,0:T(8,128)(2,1)S(1)} %pad_maximum_fusion.refs_4_), channel_id=1, source_target_pairs={{0,16},{8,24},{16,0},{24,8},{1,17},{9,25},{17,1},{25,9},{2,18},{10... | collective-permute-start | bytes 196616 | tf_op jit(solution)/shard_map/ppermute | solution.py:312
  16.9 6.7 %collective-permute-start.4 = (bf16[128,256]{1,0:T(8,128)(2,1)S(1)}, bf16[128,256]{1,0:T(8,128)(2,1)S(1)}, u32[]{:S(2)}, u32[]{:S(2)}) collective-permute-start(bf16[128,256]{1,0:T(8,128)(2,1)S(1)} %pad_maximum_fusion.refs_4_), channel_id=1, source_target_pairs={{0,8},{8,0},{16,24},{24,16},{1,9},{9,1},{17,25},{25,17},{2,10},{10... | collective-permute-start | bytes 196616 | tf_op jit(solution)/shard_map/ppermute | solution.py:312
  19.6 29.3 %collective-permute-start = (bf16[528,256]{1,0:T(8,128)(2,1)S(1)}, bf16[528,256]{1,0:T(8,128)(2,1)S(1)}, u32[]{:S(2)}, u32[]{:S(2)}) collective-permute-start(bf16[528,256]{1,0:T(8,128)(2,1)S(1)} %get-tuple-element.17), channel_id=1, source_target_pairs={{0,4},{1,5},{2,6},{3,7},{4,0},{5,1},{6,2},{7,3},{8,12},{9,13},{10,... | collective-permute-start | bytes 811016 | tf_op jit(solution)/shard_map/ppermute | solution.py:312
  22.8 26.1 %collective-permute-start.1 = (bf16[528,256]{1,0:T(8,128)(2,1)S(1)}, bf16[528,256]{1,0:T(8,128)(2,1)S(1)}, u32[]{:S(2)}, u32[]{:S(2)}) collective-permute-start(bf16[528,256]{1,0:T(8,128)(2,1)S(1)} %get-tuple-element.18), channel_id=1, source_target_pairs={{0,5},{1,4},{2,7},{3,6},{4,1},{5,0},{6,3},{7,2},{8,13},{9,12},{10,... | collective-permute-start | bytes 811016 | tf_op jit(solution)/shard_map/ppermute | solution.py:312
  23.7 25.3 %collective-permute-start.2 = (bf16[528,256]{1,0:T(8,128)(2,1)S(1)}, bf16[528,256]{1,0:T(8,128)(2,1)S(1)}, u32[]{:S(2)}, u32[]{:S(2)}) collective-permute-start(bf16[528,256]{1,0:T(8,128)(2,1)S(1)} %get-tuple-element.19), channel_id=1, source_target_pairs={{0,6},{1,7},{2,4},{3,5},{4,2},{5,3},{6,0},{7,1},{8,14},{9,15},{10,... | collective-permute-start | bytes 811016 | tf_op jit(solution)/shard_map/ppermute | solution.py:312
  24.3 24.6 %collective-permute-start.3 = (bf16[528,256]{1,0:T(8,128)(2,1)S(1)}, bf16[528,256]{1,0:T(8,128)(2,1)S(1)}, u32[]{:S(2)}, u32[]{:S(2)}) collective-permute-start(bf16[528,256]{1,0:T(8,128)(2,1)S(1)} %get-tuple-element.20), channel_id=1, source_target_pairs={{0,7},{1,6},{2,5},{3,4},{4,3},{5,2},{6,1},{7,0},{8,15},{9,14},{10,... | collective-permute-start | bytes 811016 | tf_op jit(solution)/shard_map/ppermute | solution.py:312
  26.7 17.4 %collective-permute-start.9 = (bf16[528,256]{1,0:T(8,128)(2,1)S(1)}, bf16[528,256]{1,0:T(8,128)(2,1)S(1)}, u32[]{:S(2)}, u32[]{:S(2)}) collective-permute-start(bf16[528,256]{1,0:T(8,128)(2,1)S(1)} %get-tuple-element.24), channel_id=1, source_target_pairs={{0,3},{1,2},{2,1},{3,0},{4,7},{5,6},{6,5},{7,4},{8,11},{9,10},{10,... | collective-permute-start | bytes 811016 | tf_op jit(solution)/shard_map/ppermute | solution.py:312
  53.8 7.4 %collective-permute-start.10 = (bf16[4,64,256]{2,1,0:T(8,128)(2,1)S(1)}, bf16[4,64,256]{2,1,0:T(8,128)(2,1)S(1)}, u32[]{:S(2)}, u32[]{:S(2)}) collective-permute-start(bf16[4,64,256]{2,1,0:T(8,128)(2,1)S(1)} %get-tuple-element.26), channel_id=1, source_target_pairs={{0,8},{8,0},{16,24},{24,16},{1,9},{9,1},{17,25},{25,17},{2,10},{10... | collective-permute-start | bytes 393224 | tf_op jit(solution)/shard_map/ppermute | solution.py:312
  54.9 12.9 %collective-permute-start.11 = (bf16[4,64,256]{2,1,0:T(8,128)(2,1)S(1)}, bf16[4,64,256]{2,1,0:T(8,128)(2,1)S(1)}, u32[]{:S(2)}, u32[]{:S(2)}) collective-permute-start(bf16[4,64,256]{2,1,0:T(8,128)(2,1)S(1)} %get-tuple-element.27), channel_id=1, source_target_pairs={{0,16},{8,24},{16,0},{24,8},{1,17},{9,25},{17,1},{25,9},{2,18},{10... | collective-permute-start | bytes 393224 | tf_op jit(solution)/shard_map/ppermute | solution.py:312
  56.9 10.9 %collective-permute-start.12 = (bf16[4,64,256]{2,1,0:T(8,128)(2,1)S(1)}, bf16[4,64,256]{2,1,0:T(8,128)(2,1)S(1)}, u32[]{:S(2)}, u32[]{:S(2)}) collective-permute-start(bf16[4,64,256]{2,1,0:T(8,128)(2,1)S(1)} %get-tuple-element.28), channel_id=1, source_target_pairs={{0,24},{8,16},{16,8},{24,0},{1,25},{9,17},{17,9},{25,1},{2,26},{10... | collective-permute-start | bytes 393224 | tf_op jit(solution)/shard_map/ppermute | solution.py:312

commit v2 on v1

v2 whole, which is shorter than its diff:
```python
import functools
import math

import jax
import jax.numpy as jnp
from jax import lax
from jax.experimental import pallas as pl
from jax.experimental.pallas import tpu as pltpu
from jax.sharding import PartitionSpec as P

KGRID = 8
PART = 5
QUAD = 4
LIST_ROWS = 16
BF16 = jnp.bfloat16
F32 = jnp.float32
VMEM_LIMIT = 48 * 1024 * 1024
CHI_FLOPS, CHI_BYTES = 1 << 20, 1 << 10
PACK_LIMIT = 48 * 1024 * 1024


def iota(shape, dim):
    return lax.broadcasted_iota(jnp.int32, shape, dim)


def dot(a, b, contract=(1, 0)):
    return lax.dot_general(
        a, b, (((contract[0],), (contract[1],)), ((), ())), preferred_element_type=F32
    )


def pack_kernel(n, cap, pairs, *refs):
    ints, from_blocks, outs, rest = refs[0], refs[1], refs[2 : 2 + n], refs[2 + n :]
    owner, blocks, table, lists, count, place, sems = rest
    rows, square, width = blocks.shape
    me = lax.axis_index("ri")
    pieces = 4
    part = rows // pieces
    started = [pltpu.make_async_copy(ints.at[pl.ds(0, 8)], owner, sems.at[pieces])]
    for i in range(pieces):
        at = pl.ds(i * part, part)
        started.append(pltpu.make_async_copy(from_blocks.at[at], blocks.at[at], sems.at[i]))
    for copy in started:
        copy.start()
    for k in range(n):
        count[k] = 0
    for k in range(n * cap):
        place[k] = 0
    table[...] = jnp.zeros_like(table)
    lists[...] = jnp.zeros_like(lists)

    distance = ints[0:1, :] ^ me
    as_column = jnp.sum(
        jnp.where(iota((rows, rows), 0) == iota((rows, rows), 1), distance, 0),
        axis=1,
        keepdims=True,
    )
    before = (as_column == distance) & (iota((rows, rows), 0) < iota((rows, rows), 1))
    rank = jnp.sum(before.astype(jnp.int32), axis=0, keepdims=True)
    chosen = iota((n * LIST_ROWS, rows), 0) == distance * LIST_ROWS + rank
    table[0 : ints.shape[0], :] = ints[...].astype(F32)
    table[ints.shape[0] - pairs : ints.shape[0], :] += 1.0
    ordered = dot(chosen.astype(BF16), table[...].astype(BF16), (1, 1))
    lists[:, 0:128] = ordered.astype(BF16)

    started[0].wait()

    @pl.loop(0, rows, unroll=4)
    def _(e):
        k = owner[0, e] ^ me
        r = count[k]
        place[k * cap + r] = e
        count[k] = r + 1

    for copy in started[1:]:
        copy.wait()
    for k in range(n):
        for r in range(cap):
            outs[k][r * square : (r + 1) * square, :] = blocks[place[k * cap + r]]
        outs[k][cap * square :, :] = lists[k * LIST_ROWS : (k + 1) * LIST_ROWS, :]


def pack(n, cap, blocks, block_owner, block_basis, pair_images, pair_cell):
    rows, square, width = blocks.shape
    pairs = pair_cell.shape[1]
    ints = jnp.concatenate(
        [
            block_owner.T,
            block_basis.T,
            jnp.transpose(pair_images, (1, 2, 0)).reshape(2 * pairs, rows),
            pair_cell.T,
        ],
        axis=0,
    )
    payload = jax.ShapeDtypeStruct((cap * square + LIST_ROWS, width), BF16)
    return pl.pallas_call(
        functools.partial(pack_kernel, n, cap, pairs),
        out_shape=[payload] * n,
        in_specs=[
            pl.BlockSpec(memory_space=pltpu.VMEM),
            pl.BlockSpec(memory_space=pltpu.HBM),
        ],
        out_specs=[pl.BlockSpec(memory_space=pltpu.VMEM)] * n,
        scratch_shapes=[
            pltpu.SMEM((8, rows), jnp.int32),
            pltpu.VMEM(blocks.shape, BF16),
            pltpu.VMEM((128, rows), F32),
            pltpu.VMEM((n * LIST_ROWS, width), BF16),
            pltpu.SMEM((n,), jnp.int32),
            pltpu.SMEM((n * cap,), jnp.int32),
            pltpu.SemaphoreType.DMA((5,)),
        ],
        compiler_params=pltpu.CompilerParams(vmem_limit_bytes=PACK_LIMIT),
        cost_estimate=pl.CostEstimate(flops=0, bytes_accessed=6 << 20, transcendentals=0),
        name="pack_by_owner",
    )(ints, blocks)


def chi_kernel(count, cap, pairs, cell_count, first, last, *refs):
    refs = list(refs)
    images = lax.axis_size("image")
    payloads = [refs.pop(0) for _ in range(count)]
    pieces = [refs.pop(0) for _ in range(images)]
    before = None if first else refs.pop(0)
    if last:
        own, *sends = [refs.pop(0) for _ in range(images)]
    total = refs.pop(0)
    mixed, stacked = refs
    z = lax.axis_index("image")
    square = (payloads[0].shape[0] - LIST_ROWS) // cap
    side = math.isqrt(square)
    quad = min(QUAD, cap)
    lanes = quad * square
    list_at = cap * square

    lane = iota((1, lanes), 1)
    listing = jnp.concatenate(
        [p[list_at : list_at + LIST_ROWS, 0:128].astype(F32)[0:8] for p in payloads], axis=0
    )
    height = 8 * count

    def columns(start):
        return jnp.concatenate(
            [listing[:, start + j : start + j + 1] for j in range(pairs)], axis=0
        ).astype(jnp.int32)

    def side_by_side(rows, at):
        out = jnp.where(lane // square == 0, rows[at : at + 1], 0.0)
        for s in range(1, quad):
            out = jnp.where(lane // square == s, rows[at + s : at + s + 1], out)
        return out

    def density_rows(basis_at, image_at, piece_at):
        block = jnp.concatenate([listing[:, basis_at : basis_at + 1]] * pairs, axis=0)
        block = block.astype(jnp.int32)
        image = columns(image_at) ^ z
        block_count = pieces[0].shape[1]
        hit = iota((height * pairs, block_count), 1) == block
        found = 0.0
        for i in range(images):
            part = pieces[i][piece_at : piece_at + square, :]
            chosen = jnp.where(hit & (image == i), 1.0, 0.0).astype(BF16)
            found = found + dot(chosen, jnp.concatenate([part] * quad, axis=0), (1, 1))
        return found

    occ = density_rows(1, 3, 0)
    virt = density_rows(2, 3 + pairs, square)
    cell = jnp.broadcast_to(columns(3 + 2 * pairs).astype(F32), (height * pairs, lanes))

    shape = (square, lanes)
    occ_mask = (iota(shape, 1) % side == iota(shape, 0) // side).astype(BF16)
    virt_mask = (iota(shape, 1) % square // side == iota(shape, 0) % side).astype(BF16)
    shape = (lanes, lanes)
    occ_spread = (iota(shape, 0) // side == iota(shape, 1) // side).astype(BF16)
    virt_spread = (
        (iota(shape, 0) // square == iota(shape, 1) // square)
        & (iota(shape, 0) % side == iota(shape, 1) % side)
    ).astype(BF16)

    groups = [(p, g) for p in range(count) for g in range(cap // quad)]
    for i, (p, g) in enumerate(groups):
        block = payloads[p][g * lanes : (g + 1) * lanes, :]
        stacked[i * lanes : (i + 1) * lanes, :] = block
        turned = block.T
        at = [j * height + 8 * p + g * quad for j in range(pairs)]
        occ_in = jnp.concatenate(
            [occ_mask * side_by_side(occ, a).astype(BF16) for a in at], axis=0
        )
        virt_in = jnp.concatenate(
            [virt_mask * side_by_side(virt, a).astype(BF16) for a in at], axis=0
        )
        terms = dot(occ_in, occ_spread) * dot(virt_in, virt_spread)
        here = [side_by_side(cell, a) for a in at]
        for c in range(cell_count):
            op = 0.0
            for j in range(pairs):
                term = terms[j * square : (j + 1) * square]
                op = op + jnp.where(here[j] == float(c + 1), term, 0.0)
            diagonal = jnp.concatenate(
                [jnp.where(lane // square == s, op, 0.0) for s in range(quad)], axis=0
            )
            mixed[c, :, i * lanes : (i + 1) * lanes] = dot(turned, diagonal.astype(BF16)).astype(
                BF16
            )
    for c in range(cell_count):
        acc = dot(mixed[c], stacked[...])
        if not first:
            acc = acc + before[c]
        total[c] = acc
    if last:
        share = own.shape[1]
        own[...] = total[:, pl.ds(pl.multiple_of(z * share, share), share), :]
        for k in range(1, images):
            at = pl.multiple_of((z ^ k) * share, share)
            sends[k - 1][...] = total[:, pl.ds(at, share), :].astype(BF16)


def chi_part(cap, pairs, cell_count, payloads, pieces, before, last):
    images, count = len(pieces), len(payloads)
    width = payloads[0].shape[1]
    square = (payloads[0].shape[0] - LIST_ROWS) // cap
    depth = count * cap * square
    vmem = pl.BlockSpec(memory_space=pltpu.VMEM)
    full = jax.ShapeDtypeStruct((cell_count, width, width), F32)
    share = (cell_count, width // images, width)
    args = list(payloads) + list(pieces) + ([] if before is None else [before])
    scratch = [pltpu.VMEM((cell_count, width, depth), BF16), pltpu.VMEM((depth, width), BF16)]
    if last:
        out_shape = [jax.ShapeDtypeStruct(share, F32)] + [jax.ShapeDtypeStruct(share, BF16)] * (
            images - 1
        )
        scratch = [pltpu.VMEM(full.shape, F32)] + scratch
    else:
        out_shape = [full]
    return pl.pallas_call(
        functools.partial(chi_kernel, count, cap, pairs, cell_count, before is None, last),
        out_shape=out_shape,
        in_specs=[vmem] * len(args),
        out_specs=[vmem] * len(out_shape),
        scratch_shapes=scratch,
        compiler_params=pltpu.CompilerParams(vmem_limit_bytes=VMEM_LIMIT),
        cost_estimate=pl.CostEstimate(
            flops=CHI_FLOPS, bytes_accessed=CHI_BYTES, transcendentals=0
        ),
        name="chi_of_payloads",
    )(*args)


def transform_kernel(cell_count, step, phases, own, *rest):
    *received, out, total, shaped, sems = rest
    acc = own[...]
    for part in received:
        acc = acc + part[...].astype(F32)
    total[...] = acc
    points, share, width = out.shape
    tile = min(share, 32)

    def copy(i):
        at = pl.ds(i * step, step)
        return pltpu.make_async_copy(shaped.at[at], out.at[at], sems.at[i])

    @pl.loop(0, points // step)
    def _(i):
        for row in range(0, share, tile):
            parts = [total[c, row : row + tile, :] for c in range(cell_count)]
            for j in range(step):
                acc = phases[0, i * step + j] * parts[0]
                for c in range(1, cell_count):
                    acc = acc + phases[c, i * step + j] * parts[c]
                shaped[i * step + j, row : row + tile, :] = acc
        copy(i).start()

    @pl.loop(0, points // step)
    def _(i):
        copy(i).wait()


def transform(phases, own, received):
    cell_count, share, width = own.shape
    points = phases.shape[1]
    step = 8
    vmem = pl.BlockSpec(memory_space=pltpu.VMEM)
    return pl.pallas_call(
        functools.partial(transform_kernel, cell_count, step),
        out_shape=jax.ShapeDtypeStruct((points, share, width), F32),
        in_specs=[pl.BlockSpec(memory_space=pltpu.SMEM)] + [vmem] * (1 + len(received)),
        out_specs=pl.BlockSpec(memory_space=pltpu.HBM),
        scratch_shapes=[
            pltpu.VMEM((cell_count, share, width), F32),
            pltpu.VMEM((points, share, width), F32),
            pltpu.SemaphoreType.DMA((points // step,)),
        ],
        compiler_params=pltpu.CompilerParams(vmem_limit_bytes=VMEM_LIMIT),
        cost_estimate=pl.CostEstimate(
            flops=2 * points * cell_count * share * width,
            bytes_accessed=points * share * width * 4,
            transcendentals=0,
        ),
        name="to_k_points",
    )(phases, own, *received)


def swap(array, axis, k):
    size = lax.axis_size(axis)
    return lax.ppermute(array, axis, [(i, i ^ k) for i in range(size)])


def local(blocks, block_owner, block_basis, pair_images, pair_cell, lattice, dens_occ, dens_virt):
    owners, images = lax.axis_size("ri"), lax.axis_size("image")
    pairs = pair_cell.shape[1]
    cell_count = lattice.shape[0]
    cap = max(2, (2 * blocks.shape[0] + owners - 1) // owners)

    packed = pack(owners, cap, blocks, block_owner, block_basis, pair_images, pair_cell)
    order = list(range(owners - 2, 1, -1)) + [owners - 1]
    if owners == 8:
        order = [6, 2, 4, 7, 3, 5]
    payload = {0: packed[0]}
    half = len(order) // 2
    payload.update({k: swap(packed[k], "ri", k) for k in order[:half]})
    for k, after in zip(order[half:], order[:half]):
        payload[after], later = lax.optimization_barrier((payload[after], packed[k]))
        payload[k] = swap(later, "ri", k)
    payload[1] = swap(packed[1], "ri", 1)
    density = jnp.concatenate([dens_occ[0].T, dens_virt[0].T], axis=0)
    pieces = density[None]
    k = 1
    while k < images:
        pieces = jnp.concatenate([pieces, swap(pieces, "image", k)], axis=0)
        k = 2 * k
    pieces = [pieces[i] for i in range(images)]

    arrival = [0, 1] + order
    early, late = arrival[: half + 2], arrival[half + 2 :]
    parts = [early[at : at + PART] for at in range(0, len(early), PART)]
    parts += [late[at : at + PART] for at in range(0, len(late), PART)]
    chi = None
    for part in parts:
        out = chi_part(
            cap, pairs, cell_count, [payload[k] for k in part], pieces, chi, part is parts[-1]
        )
        chi = out[0]
    own, sends = out[0], out[1:]
    received = [swap(sends[k - 1], "image", k) for k in range(1, images)]

    points = jnp.arange(KGRID * KGRID, dtype=jnp.int32)
    wrapped = (
        lattice[:, 0:1] * (points // KGRID)[None, :] + lattice[:, 1:2] * (points % KGRID)[None, :]
    ) % KGRID
    angles = 2.0 * math.pi / KGRID * wrapped.astype(F32)
    phases = jnp.concatenate([jnp.cos(angles), jnp.sin(angles)], axis=1)
    result = transform(phases, own, received)
    return result.reshape(2, KGRID * KGRID, 1, own.shape[1], own.shape[2])


def solution(mesh):
    placed = (
        P(("image", "ri"), None, None),
        P(("image", "ri"), None),
        P(("image", "ri"), None),
        P(("image", "ri"), None, None),
        P(("image", "ri"), None),
        P(),
        P("image", None, None),
        P("image", None, None),
    )
    return jax.shard_map(
        local,
        mesh=mesh,
        in_specs=placed,
        out_specs=P(None, None, "ri", "image", None),
        check_vma=False,
    )
```

time: 77.9 us -> 55.1 us (0.71)
  Pallas kernels: 25 us -> 14.8 us
  waiting for transfers between devices: 29.4 us -> 20.3 us
  local copies, waits for them, and re-layouts: 4.8 us -> 1.99 us
  starting transfers between devices: 17.5 us -> 15.5 us
    ppermute x13 -> x12, waiting for transfers between devices: 29.4 us -> 20.3 us  [swap(): return lax.ppermute(array, axis, [(i, i ^ k) for i in range(size)])]
    pallas_call x3, Pallas kernels: 19.4 us -> 13.8 us  [the longest x2 9.67 us: chi_part(): pl.pallas_call(functools.partial(chi_kernel, count, cap, pairs, cell_coun...]
    pallas_call x1, Pallas kernels: 5.53 us -> 0.97 us  [pack(): pl.pallas_call(functools.partial(pack_kernel, n, cap, pairs), out_shape=[...]
    unnamed x10 -> x2, local copies, waits for them, and re-layouts: 3.92 us -> 1.22 us
    ppermute x13 -> x12, starting transfers between devices: 17.5 us -> 15.5 us  [swap(): return lax.ppermute(array, axis, [(i, i ^ k) for i in range(size)])]
    broadcast_in_dim x0 -> x1, other arithmetic: none -> 0.78 us  [local(): pieces = density[None]]
  transfers between devices with their start and end apart: 13 -> 12, of which waited for: 5 -> 6; matrix products, arithmetic and copies ran while one was open for 2% -> 3% of each run, Pallas kernels for 6% -> 12%
where the time goes in v2:
time: 55.1 us; the launch traced here: 54.4 us
  waiting for transfers between devices  20.3 us (37%)
  starting transfers between devices  15.5 us (28%)
  Pallas kernels  14.8 us (27%)
  local copies, waits for them, and re-layouts  1.99 us (4%)
  other arithmetic  1.72 us (3%)
    ppermute x12, waiting for transfers between devices, swap(): return lax.ppermute(array, axis, [(i, i ^ k) for i in range(size)])  20.3 us
    ppermute x12, starting transfers between devices, swap(): return lax.ppermute(array, axis, [(i, i ^ k) for i in range(size)])  15.5 us
    pallas_call x2, Pallas kernels, chi_part(): pl.pallas_call(functools.partial(chi_kernel, count, cap, pairs, cell_coun...  9.67 us
    pallas_call x1, Pallas kernels, transform(): pl.pallas_call(functools.partial(transform_kernel, cell_count, step), out...  4.18 us
    unnamed x2, local copies, waits for them, and re-layouts  1.22 us
  transfers between devices with their start and end apart: 12, of which 6 were waited for; matrix products, arithmetic and copies ran while one was open for 3% of the time, Pallas kernels for 12%

profile of v2, /device:TPU:0, one launch (start us, length us, event | category | flops | bytes accessed | tf_op | source)
XLA Modules:
  0.0 54.4 jit_solution(2707667216055864707)
XLA Ops:
  0.0 0.8 %fusion.5 = (bf16[1,128,256]{2,1,0:T(8,128)(2,1)S(1)}, bf16[128,256]{1,0:T(8,128)(2,1)S(1)}) fusion(bf16[64,256]{1,0:T(8,128)(2,1)} %bitcast.28, bf16[64,256]{1,0:T(8,128)(2,1)} %bitcast.29), kind=kLoop, calls=%fused_computation.21 | loop fusion | flops 131072 | bytes 196608 | tf_op jit(solution)/shard_map/broadcast_in_dim | solution.py:326
  0.8 3.1 %collective-permute-start.6 = (bf16[1,128,256]{2,1,0:T(8,128)(2,1)S(1)}, bf16[1,128,256]{2,1,0:T(8,128)(2,1)S(1)}, u32[]{:S(2)}, u32[]{:S(2)}) collective-permute-start(bf16[1,128,256]{2,1,0:T(8,128)(2,1)S(1)} %get-tuple-element.43), channel_id=1, source_target_pairs={{0,8},{8,0},{16,24},{24,16},{1,9},{9,1},{17,25},{25,17},{2,10},{10... | collective-permute-start | bytes 196616 | tf_op jit(solution)/shard_map/ppermute | solution.py:305
  3.9 0.7 %pad_add_fusion.refs_0_ = s32[15,32]{1,0:T(8,128)S(1)} fusion(s32[4,32]{1,0:T(4,128)} %bitcast.31, s32[8,32]{1,0:T(8,128)} %bitcast.30, s32[2,32]{1,0:T(2,128)} %bitcast.32, s32[1,32]{1,0:T(1,128)} %bitcast.33), kind=kLoop, calls=%fused_computation.4 | loop fusion | flops 1440 | bytes 3840 | tf_op jit(solution)/shard_map/concatenate | solution.py:86
  4.6 0.0 copy-start
  4.6 1.2 %copy-done = bf16[32,64,256]{2,1,0:T(8,128)(2,1)S(1)} copy-done((bf16[32,64,256]{2,1,0:T(8,128)(2,1)S(1)}, bf16[32,64,256]{2,1,0:T(8,128)(2,1)}, u32[]{:S(2)}) %copy-start) | copy-done | bytes 1048600
  5.8 1.0 %pack_by_owner.1 = (bf16[528,256]{1,0:T(8,128)(2,1)S(1)}, bf16[528,256]{1,0:T(8,128)(2,1)S(1)}, bf16[528,256]{1,0:T(8,128)(2,1)S(1)}, bf16[528,256]{1,0:T(8,128)...) custom-call(s32[15,32]{1,0:T(8,128)S(1)} %pad_add_fusion.refs_0_, ...), custom_call_target="tpu_custom_call" | custom-call | bytes 6291456 | tf_op jit(solution)/shard_map/pack_by_owner/pallas_call | solution.py:96
  6.8 2.5 %collective-permute-start = (bf16[528,256]{1,0:T(8,128)(2,1)S(1)}, bf16[528,256]{1,0:T(8,128)(2,1)S(1)}, u32[]{:S(2)}, u32[]{:S(2)}) collective-permute-start(bf16[528,256]{1,0:T(8,128)(2,1)S(1)} %get-tuple-element.23), channel_id=1, source_target_pairs={{0,6},{1,7},{2,4},{3,5},{4,2},{5,3},{6,0},{7,1},{8,14},{9,15},{10,... | collective-permute-start | bytes 811016 | tf_op jit(solution)/shard_map/ppermute | solution.py:305
  9.3 0.5 collective-permute-start.2
  9.9 0.5 collective-permute-start.4
  10.4 0.0 collective-permute-start.8
  10.4 0.0 collective-permute-done.6
  10.4 2.7 %collective-permute-start.7 = (bf16[2,128,256]{2,1,0:T(8,128)(2,1)S(1)}, bf16[2,128,256]{2,1,0:T(8,128)(2,1)S(1)}, u32[]{:S(2)}, u32[]{:S(2)}) collective-permute-start(bf16[2,128,256]{2,1,0:T(8,128)(2,1)S(1)} %pad_maximum_fusion), channel_id=1, source_target_pairs={{0,16},{8,24},{16,0},{24,8},{1,17},{9,25},{17,1},{25,9},{2,18},{10... | collective-permute-start | bytes 393224 | tf_op jit(solution)/shard_map/ppermute | solution.py:305
  13.0 0.8 %slice_bitcast_fusion.3 = (s32[4]{0:T(128)S(1)}, s32[4]{0:T(128)S(1)}) fusion(s32[4,2]{0,1:T(2,128)} %param.13), kind=kLoop, calls=%fused_computation.20 | loop fusion | bytes 64 | tf_op jit(solution)/shard_map/mul | solution.py:348
  13.8 3.4 %collective-permute-done.refs_2_ = bf16[528,256]{1,0:T(8,128)(2,1)S(1)} collective-permute-done((bf16[528,256]{1,0:T(8,128)(2,1)S(1)}, bf16[528,256]{1,0:T(8,128)(2,1)S(1)}, u32[]{:S(2)}, u32[]{:S(2)}) %collective-permute-start) | collective-permute-done | bytes 270368 | tf_op jit(solution)/shard_map/ppermute | solution.py:305
  17.2 0.0 collective-permute-start.1
  17.2 4.8 %collective-permute-done.2.refs_3_ = bf16[528,256]{1,0:T(8,128)(2,1)S(1)} collective-permute-done((bf16[528,256]{1,0:T(8,128)(2,1)S(1)}, bf16[528,256]{1,0:T(8,128)(2,1)S(1)}, u32[]{:S(2)}, u32[]{:S(2)}) %collective-permute-start.2) | collective-permute-done | bytes 270368 | tf_op jit(solution)/shard_map/ppermute | solution.py:305
  22.0 0.0 collective-permute-start.3
  22.0 0.0 collective-permute-done.4.refs_4_
  22.0 1.7 %collective-permute-start.5 = (bf16[528,256]{1,0:T(8,128)(2,1)S(1)}, bf16[528,256]{1,0:T(8,128)(2,1)S(1)}, u32[]{:S(2)}, u32[]{:S(2)}) collective-permute-start(bf16[528,256]{1,0:T(8,128)(2,1)S(1)} %get-tuple-element.31), channel_id=1, source_target_pairs={{0,5},{1,4},{2,7},{3,6},{4,1},{5,0},{6,3},{7,2},{8,13},{9,12},{10,... | collective-permute-start | bytes 811016 | tf_op jit(solution)/shard_map/ppermute | solution.py:305
  23.7 0.0 collective-permute-done.7
  23.7 0.0 collective-permute-done.8.refs_1_
  23.7 5.8 %chi_of_payloads.2.refs_7_ = f32[4,256,256]{2,1,0:T(8,128)S(1)} custom-call(bf16[528,256]{1,0:T(8,128)(2,1)S(1)} %get-tuple-element.32.refs_0_, bf16[528,256]{1,0:T(8,128)(2,1)S(1)} %collective-permute-done.8.refs_1_, bf16[528,256]{1,0:T(8,128)(2,1)S(1)} %collective-permute-done.refs_2_, bf16[528,256]{1,0:T(8,128)(2,1)S(1)} %collective-permute-done.2.refs_3_, ...), custom_call_target="tpu_custom_call" | custom-call | flops 1048576 | bytes 1024 | tf_op jit(solution)/shard_map/chi_of_payloads/pallas_call | solution.py:235
  29.6 0.0 collective-permute-done.1.refs_0_
  29.6 3.3 %collective-permute-done.3.refs_1_ = bf16[528,256]{1,0:T(8,128)(2,1)S(1)} collective-permute-done((bf16[528,256]{1,0:T(8,128)(2,1)S(1)}, bf16[528,256]{1,0:T(8,128)(2,1)S(1)}, u32[]{:S(2)}, u32[]{:S(2)}) %collective-permute-start.3) | collective-permute-done | bytes 270368 | tf_op jit(solution)/shard_map/ppermute | solution.py:305
  32.9 0.2 collective-permute-done.5.refs_2_
  33.0 3.8 %chi_of_payloads.3 = (f32[4,64,256]{2,1,0:T(8,128)S(1)}, bf16[4,64,256]{2,1,0:T(8,128)(2,1)S(1)}, bf16[4,64,256]{2,1,0:T(8,128)(2,1)S(1)}, bf16[4,64,256]{2,1,0:T(8,128)(2,1)S(1)}) custom-call(bf16[528,256]{1,0:T(8,128)(2,1)S(1)} %collective-permute-done.1.refs_0_, bf16[528,256]{1,0:T(8,128)(2,1)S(1)} %collective-permute-done.3.refs_1_, ...), custom_call_target="tpu_custom_call" | custom-call | flops 1048576 | bytes 1024 | tf_op jit(solution)/shard_map/chi_of_payloads/pallas_call | solution.py:235
  36.9 0.3 collective-permute-start.9
  37.2 2.8 %collective-permute-start.10 = (bf16[4,64,256]{2,1,0:T(8,128)(2,1)S(1)}, bf16[4,64,256]{2,1,0:T(8,128)(2,1)S(1)}, u32[]{:S(2)}, u32[]{:S(2)}) collective-permute-start(bf16[4,64,256]{2,1,0:T(8,128)(2,1)S(1)} %get-tuple-element.39), channel_id=1, source_target_pairs={{0,16},{8,24},{16,0},{24,8},{1,17},{9,25},{17,1},{25,9},{2,18},{10... | collective-permute-start | bytes 393224 | tf_op jit(solution)/shard_map/ppermute | solution.py:305
  40.0 1.3 %collective-permute-start.11 = (bf16[4,64,256]{2,1,0:T(8,128)(2,1)S(1)}, bf16[4,64,256]{2,1,0:T(8,128)(2,1)S(1)}, u32[]{:S(2)}, u32[]{:S(2)}) collective-permute-start(bf16[4,64,256]{2,1,0:T(8,128)(2,1)S(1)} %get-tuple-element.40), channel_id=1, source_target_pairs={{0,24},{8,16},{16,8},{24,0},{1,25},{9,17},{17,9},{25,1},{2,26},{10... | collective-permute-start | bytes 393224 | tf_op jit(solution)/shard_map/ppermute | solution.py:305
  41.3 0.1 fusion.4
  41.5 0.1 pad_maximum_fusion.2.phases
  41.5 3.7 %collective-permute-done.9.rest_0_ = bf16[4,64,256]{2,1,0:T(8,128)(2,1)S(1)} collective-permute-done((bf16[4,64,256]{2,1,0:T(8,128)(2,1)S(1)}, bf16[4,64,256]{2,1,0:T(8,128)(2,1)S(1)}, u32[]{:S(2)}, u32[]{:S(2)}) %collective-permute-start.9) | collective-permute-done | bytes 131104 | tf_op jit(solution)/shard_map/ppermute | solution.py:305
  45.3 0.0 collective-permute-done.10.rest_1_
  45.3 4.9 %collective-permute-done.11.rest_2_ = bf16[4,64,256]{2,1,0:T(8,128)(2,1)S(1)} collective-permute-done((bf16[4,64,256]{2,1,0:T(8,128)(2,1)S(1)}, bf16[4,64,256]{2,1,0:T(8,128)(2,1)S(1)}, u32[]{:S(2)}, u32[]{:S(2)}) %collective-permute-start.11) | collective-permute-done | bytes 131104 | tf_op jit(solution)/shard_map/ppermute | solution.py:305
  50.2 4.2 %to_k_points.1 = f32[128,64,256]{2,1,0:T(8,128)} custom-call(f32[4,128]{1,0:T(4,128)S(1)} %pad_maximum_fusion.2.phases, f32[4,64,256]{2,1,0:T(8,128)S(1)} %get-tuple-element.37.own, bf16[4,64,256]{2,1,0:T(8,128)(2,1)S(1)} %collective-permute-done.9.rest_0_, bf16[4,64,256]{2,1,0:T(8,128)(2,1)S(1)} %collective-permute-done.10.rest_1_, ...), custom_call_target="tpu_custom_call" | custom-call | flops 16777216 | bytes 8388608 | tf_op jit(solution)/shard_map/to_k_points/pallas_call | solution.py:283
  (3 shorter events, 0.0 us)
Async XLA Ops:
  0.8 9.6 %collective-permute-start.6 = (bf16[1,128,256]{2,1,0:T(8,128)(2,1)S(1)}, bf16[1,128,256]{2,1,0:T(8,128)(2,1)S(1)}, u32[]{:S(2)}, u32[]{:S(2)}) collective-permute-start(bf16[1,128,256]{2,1,0:T(8,128)(2,1)S(1)} %get-tuple-element.43), channel_id=1, source_target_pairs={{0,8},{8,0},{16,24},{24,16},{1,9},{9,1},{17,25},{25,17},{2,10},{10... | collective-permute-start | bytes 196616 | tf_op jit(solution)/shard_map/ppermute | solution.py:305
  4.6 1.2 %copy-start = (bf16[32,64,256]{2,1,0:T(8,128)(2,1)S(1)}, bf16[32,64,256]{2,1,0:T(8,128)(2,1)}, u32[]{:S(2)}) copy-start(bf16[32,64,256]{2,1,0:T(8,128)(2,1)} %refs_1_.1) | copy-start | bytes 3145732
  6.8 10.4 %collective-permute-start = (bf16[528,256]{1,0:T(8,128)(2,1)S(1)}, bf16[528,256]{1,0:T(8,128)(2,1)S(1)}, u32[]{:S(2)}, u32[]{:S(2)}) collective-permute-start(bf16[528,256]{1,0:T(8,128)(2,1)S(1)} %get-tuple-element.23), channel_id=1, source_target_pairs={{0,6},{1,7},{2,4},{3,5},{4,2},{5,3},{6,0},{7,1},{8,14},{9,15},{10,... | collective-permute-start | bytes 811016 | tf_op jit(solution)/shard_map/ppermute | solution.py:305
  9.3 12.7 %collective-permute-start.2 = (bf16[528,256]{1,0:T(8,128)(2,1)S(1)}, bf16[528,256]{1,0:T(8,128)(2,1)S(1)}, u32[]{:S(2)}, u32[]{:S(2)}) collective-permute-start(bf16[528,256]{1,0:T(8,128)(2,1)S(1)} %get-tuple-element.26), channel_id=1, source_target_pairs={{0,2},{1,3},{2,0},{3,1},{4,6},{5,7},{6,4},{7,5},{8,10},{9,11},{10,... | collective-permute-start | bytes 811016 | tf_op jit(solution)/shard_map/ppermute | solution.py:305
  9.9 12.1 %collective-permute-start.4 = (bf16[528,256]{1,0:T(8,128)(2,1)S(1)}, bf16[528,256]{1,0:T(8,128)(2,1)S(1)}, u32[]{:S(2)}, u32[]{:S(2)}) collective-permute-start(bf16[528,256]{1,0:T(8,128)(2,1)S(1)} %get-tuple-element.29), channel_id=1, source_target_pairs={{0,4},{1,5},{2,6},{3,7},{4,0},{5,1},{6,2},{7,3},{8,12},{9,13},{10,... | collective-permute-start | bytes 811016 | tf_op jit(solution)/shard_map/ppermute | solution.py:305
  10.4 13.4 %collective-permute-start.8 = (bf16[528,256]{1,0:T(8,128)(2,1)S(1)}, bf16[528,256]{1,0:T(8,128)(2,1)S(1)}, u32[]{:S(2)}, u32[]{:S(2)}) collective-permute-start(bf16[528,256]{1,0:T(8,128)(2,1)S(1)} %get-tuple-element.33), channel_id=1, source_target_pairs={{0,1},{1,0},{2,3},{3,2},{4,5},{5,4},{6,7},{7,6},{8,9},{9,8},{10,11... | collective-permute-start | bytes 811016 | tf_op jit(solution)/shard_map/ppermute | solution.py:305
  10.4 13.3 %collective-permute-start.7 = (bf16[2,128,256]{2,1,0:T(8,128)(2,1)S(1)}, bf16[2,128,256]{2,1,0:T(8,128)(2,1)S(1)}, u32[]{:S(2)}, u32[]{:S(2)}) collective-permute-start(bf16[2,128,256]{2,1,0:T(8,128)(2,1)S(1)} %pad_maximum_fusion), channel_id=1, source_target_pairs={{0,16},{8,24},{16,0},{24,8},{1,17},{9,25},{17,1},{25,9},{2,18},{10... | collective-permute-start | bytes 393224 | tf_op jit(solution)/shard_map/ppermute | solution.py:305
  17.2 12.3 %collective-permute-start.1 = (bf16[528,256]{1,0:T(8,128)(2,1)S(1)}, bf16[528,256]{1,0:T(8,128)(2,1)S(1)}, u32[]{:S(2)}, u32[]{:S(2)}) collective-permute-start(bf16[528,256]{1,0:T(8,128)(2,1)S(1)} %get-tuple-element.25), channel_id=1, source_target_pairs={{0,7},{1,6},{2,5},{3,4},{4,3},{5,2},{6,1},{7,0},{8,15},{9,14},{10,... | collective-permute-start | bytes 811016 | tf_op jit(solution)/shard_map/ppermute | solution.py:305
  22.0 10.9 %collective-permute-start.3 = (bf16[528,256]{1,0:T(8,128)(2,1)S(1)}, bf16[528,256]{1,0:T(8,128)(2,1)S(1)}, u32[]{:S(2)}, u32[]{:S(2)}) collective-permute-start(bf16[528,256]{1,0:T(8,128)(2,1)S(1)} %get-tuple-element.28), channel_id=1, source_target_pairs={{0,3},{1,2},{2,1},{3,0},{4,7},{5,6},{6,5},{7,4},{8,11},{9,10},{10,... | collective-permute-start | bytes 811016 | tf_op jit(solution)/shard_map/ppermute | solution.py:305
  22.0 11.1 %collective-permute-start.5 = (bf16[528,256]{1,0:T(8,128)(2,1)S(1)}, bf16[528,256]{1,0:T(8,128)(2,1)S(1)}, u32[]{:S(2)}, u32[]{:S(2)}) collective-permute-start(bf16[528,256]{1,0:T(8,128)(2,1)S(1)} %get-tuple-element.31), channel_id=1, source_target_pairs={{0,5},{1,4},{2,7},{3,6},{4,1},{5,0},{6,3},{7,2},{8,13},{9,12},{10,... | collective-permute-start | bytes 811016 | tf_op jit(solution)/shard_map/ppermute | solution.py:305
  36.9 8.4 %collective-permute-start.9 = (bf16[4,64,256]{2,1,0:T(8,128)(2,1)S(1)}, bf16[4,64,256]{2,1,0:T(8,128)(2,1)S(1)}, u32[]{:S(2)}, u32[]{:S(2)}) collective-permute-start(bf16[4,64,256]{2,1,0:T(8,128)(2,1)S(1)} %get-tuple-element.38), channel_id=1, source_target_pairs={{0,8},{8,0},{16,24},{24,16},{1,9},{9,1},{17,25},{25,17},{2,10},{10... | collective-permute-start | bytes 393224 | tf_op jit(solution)/shard_map/ppermute | solution.py:305
  37.2 8.1 %collective-permute-start.10 = (bf16[4,64,256]{2,1,0:T(8,128)(2,1)S(1)}, bf16[4,64,256]{2,1,0:T(8,128)(2,1)S(1)}, u32[]{:S(2)}, u32[]{:S(2)}) collective-permute-start(bf16[4,64,256]{2,1,0:T(8,128)(2,1)S(1)} %get-tuple-element.39), channel_id=1, source_target_pairs={{0,16},{8,24},{16,0},{24,8},{1,17},{9,25},{17,1},{25,9},{2,18},{10... | collective-permute-start | bytes 393224 | tf_op jit(solution)/shard_map/ppermute | solution.py:305
  40.0 10.2 %collective-permute-start.11 = (bf16[4,64,256]{2,1,0:T(8,128)(2,1)S(1)}, bf16[4,64,256]{2,1,0:T(8,128)(2,1)S(1)}, u32[]{:S(2)}, u32[]{:S(2)}) collective-permute-start(bf16[4,64,256]{2,1,0:T(8,128)(2,1)S(1)} %get-tuple-element.40), channel_id=1, source_target_pairs={{0,24},{8,16},{16,8},{24,0},{1,25},{9,17},{17,9},{25,1},{2,26},{10... | collective-permute-start | bytes 393224 | tf_op jit(solution)/shard_map/ppermute | solution.py:305

commit v3 on v2

v3 whole, which is shorter than its diff:
```python
import functools
import math

import jax
import jax.numpy as jnp
from jax import lax
from jax.experimental import pallas as pl
from jax.experimental.pallas import tpu as pltpu
from jax.sharding import PartitionSpec as P

KGRID = 8
PART = 5
QUAD = 4
LIST_ROWS = 16
BF16 = jnp.bfloat16
F32 = jnp.float32
VMEM_LIMIT = 48 * 1024 * 1024
CHI_FLOPS, CHI_BYTES = 1 << 20, 1 << 10
PACK_LIMIT = 48 * 1024 * 1024


def iota(shape, dim):
    return lax.broadcasted_iota(jnp.int32, shape, dim)


def dot(a, b, contract=(1, 0)):
    return lax.dot_general(
        a, b, (((contract[0],), (contract[1],)), ((), ())), preferred_element_type=F32
    )


def lists_with(k):
    if k < 2:
        return [k]
    return [k, k ^ 1] if k % 2 == 0 else []


def pack_kernel(n, cap, pairs, *refs):
    ints, from_blocks, outs, rest = refs[0], refs[1], refs[2 : 2 + n], refs[2 + n :]
    owner, blocks, table, lists, count, place, sems = rest
    rows, square, width = blocks.shape
    me = lax.axis_index("ri")
    pieces = 4
    part = rows // pieces
    started = [pltpu.make_async_copy(ints.at[pl.ds(0, 8)], owner, sems.at[pieces])]
    for i in range(pieces):
        at = pl.ds(i * part, part)
        started.append(pltpu.make_async_copy(from_blocks.at[at], blocks.at[at], sems.at[i]))
    for copy in started:
        copy.start()
    for k in range(n):
        count[k] = 0
    for k in range(n * cap):
        place[k] = 0
    table[...] = jnp.zeros_like(table)
    lists[...] = jnp.zeros_like(lists)

    distance = ints[0:1, :] ^ me
    as_column = jnp.sum(
        jnp.where(iota((rows, rows), 0) == iota((rows, rows), 1), distance, 0),
        axis=1,
        keepdims=True,
    )
    before = (as_column == distance) & (iota((rows, rows), 0) < iota((rows, rows), 1))
    rank = jnp.sum(before.astype(jnp.int32), axis=0, keepdims=True)
    chosen = iota((n * LIST_ROWS, rows), 0) == distance * LIST_ROWS + rank
    table[0 : ints.shape[0], :] = ints[...].astype(F32)
    table[ints.shape[0] - pairs : ints.shape[0], :] += 1.0
    ordered = dot(chosen.astype(BF16), table[...].astype(BF16), (1, 1))
    lists[:, 0:128] = ordered.astype(BF16)

    started[0].wait()

    @pl.loop(0, rows, unroll=4)
    def _(e):
        k = owner[0, e] ^ me
        r = count[k]
        place[k * cap + r] = e
        count[k] = r + 1

    for copy in started[1:]:
        copy.wait()
    for k in range(n):
        for r in range(cap):
            outs[k][r * square : (r + 1) * square, :] = blocks[place[k * cap + r]]
        for i, of in enumerate(lists_with(k)):
            at = cap * square + i * LIST_ROWS
            outs[k][at : at + LIST_ROWS, :] = lists[of * LIST_ROWS : (of + 1) * LIST_ROWS, :]


def pack(n, cap, blocks, block_owner, block_basis, pair_images, pair_cell):
    rows, square, width = blocks.shape
    pairs = pair_cell.shape[1]
    ints = jnp.concatenate(
        [
            block_owner.T,
            block_basis.T,
            jnp.transpose(pair_images, (1, 2, 0)).reshape(2 * pairs, rows),
            pair_cell.T,
        ],
        axis=0,
    )
    heights = [cap * square + len(lists_with(k)) * LIST_ROWS for k in range(n)]
    return pl.pallas_call(
        functools.partial(pack_kernel, n, cap, pairs),
        out_shape=[jax.ShapeDtypeStruct((height, width), BF16) for height in heights],
        in_specs=[
            pl.BlockSpec(memory_space=pltpu.VMEM),
            pl.BlockSpec(memory_space=pltpu.HBM),
        ],
        out_specs=[pl.BlockSpec(memory_space=pltpu.VMEM)] * n,
        scratch_shapes=[
            pltpu.SMEM((8, rows), jnp.int32),
            pltpu.VMEM(blocks.shape, BF16),
            pltpu.VMEM((128, rows), F32),
            pltpu.VMEM((n * LIST_ROWS, width), BF16),
            pltpu.SMEM((n,), jnp.int32),
            pltpu.SMEM((n * cap,), jnp.int32),
            pltpu.SemaphoreType.DMA((5,)),
        ],
        compiler_params=pltpu.CompilerParams(vmem_limit_bytes=PACK_LIMIT),
        cost_estimate=pl.CostEstimate(flops=0, bytes_accessed=6 << 20, transcendentals=0),
        name="pack_by_owner",
    )(ints, blocks)


def by_halving(images):
    return images == 4


def shares_of(images):
    kept = [(part, [0], F32) for part in range(2)]
    if by_halving(images):
        kept += [(1, [2], F32), (1, [1, 3], BF16)]
        return kept + [(0, [k], BF16) for k in (2, 3, 1)]
    return kept + [(part, [k], BF16) for part in range(2) for k in range(1, images)]


def diagonals(cap, pairs, cell_count, side, lists, table):
    images = lax.axis_size("image")
    z = lax.axis_index("image")
    square = side * side
    quad = min(QUAD, cap)
    lanes = quad * square
    height = 8 * len(lists)
    lane = iota((1, lanes), 1)
    listing = jnp.concatenate(
        [ref[at : at + LIST_ROWS, 0:128].astype(F32)[0:8] for ref, at in lists], axis=0
    )

    def columns(start):
        return jnp.concatenate(
            [listing[:, start + j : start + j + 1] for j in range(pairs)], axis=0
        ).astype(jnp.int32)

    def side_by_side(rows, at):
        out = jnp.where(lane // square == 0, rows[at : at + 1], 0.0)
        for s in range(1, quad):
            out = jnp.where(lane // square == s, rows[at + s : at + s + 1], out)
        return out

    def density_rows(basis_at, image_at, lane_at):
        block = jnp.concatenate([listing[:, basis_at : basis_at + 1]] * pairs, axis=0)
        row = (columns(image_at) ^ z) * (table.shape[0] // images) + block.astype(jnp.int32)
        chosen = iota((height * pairs, table.shape[0]), 1) == row
        found = dot(jnp.where(chosen, 1.0, 0.0).astype(BF16), table[...])
        return jnp.concatenate([found[:, lane_at : lane_at + square]] * quad, axis=1)

    occ = density_rows(1, 3, 0)
    virt = density_rows(2, 3 + pairs, square)
    cell = jnp.broadcast_to(columns(3 + 2 * pairs).astype(F32), (height * pairs, lanes))

    shape = (square, lanes)
    occ_mask = (iota(shape, 1) % side == iota(shape, 0) // side).astype(BF16)
    virt_mask = (iota(shape, 1) % square // side == iota(shape, 0) % side).astype(BF16)
    shape = (lanes, lanes)
    occ_spread = (iota(shape, 0) // side == iota(shape, 1) // side).astype(BF16)
    virt_spread = (
        (iota(shape, 0) // square == iota(shape, 1) // square)
        & (iota(shape, 0) % side == iota(shape, 1) % side)
    ).astype(BF16)

    for p in range(len(lists)):
        for g in range(cap // quad):
            at = [j * height + 8 * p + g * quad for j in range(pairs)]
            occ_in = jnp.concatenate(
                [occ_mask * side_by_side(occ, a).astype(BF16) for a in at], axis=0
            )
            virt_in = jnp.concatenate(
                [virt_mask * side_by_side(virt, a).astype(BF16) for a in at], axis=0
            )
            terms = dot(occ_in, occ_spread) * dot(virt_in, virt_spread)
            here = [side_by_side(cell, a) for a in at]
            out = []
            for c in range(cell_count):
                op = None
                for j in range(pairs):
                    term = terms[j * square : (j + 1) * square]
                    term = jnp.where(here[j] == float(c + 1), term, 0.0)
                    op = term if op is None else op + term
                out.append(
                    jnp.concatenate(
                        [jnp.where(lane // square == s, op, 0.0) for s in range(quad)], axis=0
                    ).astype(BF16)
                )
            yield out


def early_kernel(count, cap, pairs, cell_count, square, first, *refs):
    refs = list(refs)
    images = lax.axis_size("image")
    payloads = [refs.pop(0) for _ in range(count)]
    if first:
        pieces = [refs.pop(0) for _ in range(images)]
        total, table, mixed, stacked = refs
        for i in range(images):
            block_count = pieces[i].shape[1]
            table[i * block_count : (i + 1) * block_count, :] = pieces[i][...].T
        before = None
    else:
        before, table, total, mixed, stacked = refs
    lists = [(p, cap * square) for p in payloads]
    made = diagonals(cap, pairs, cell_count, math.isqrt(square), lists, table)
    add_blocks(cap, square, payloads, made, before, total, mixed, stacked)


def add_blocks(cap, square, payloads, made, before, total, mixed, stacked):
    lanes = min(QUAD, cap) * square
    per = cap * square // lanes
    for i, operators in enumerate(made):
        p, g = divmod(i, per)
        block = payloads[p][g * lanes : (g + 1) * lanes, :]
        stacked[i * lanes : (i + 1) * lanes, :] = block
        turned = block.T
        for c, operator in enumerate(operators):
            mixed[c, :, i * lanes : (i + 1) * lanes] = dot(turned, operator).astype(BF16)
    for c in range(mixed.shape[0]):
        acc = dot(mixed[c], stacked[...])
        total[c] = acc if before is None else acc + before[c]


def operators_kernel(count, cap, pairs, cell_count, square, lists, table, out):
    places = [(lists, i * LIST_ROWS) for i in range(count)]
    made = diagonals(cap, pairs, cell_count, math.isqrt(square), places, table)
    for i, operators in enumerate(made):
        for c in range(cell_count):
            out[i * cell_count + c] = operators[c]


def late_kernel(count, cap, cell_count, square, last, *refs):
    refs = list(refs)
    images = lax.axis_size("image")
    payloads = [refs.pop(0) for _ in range(count)]
    before, operators = refs.pop(0), refs.pop(0)
    outs = [refs.pop(0) for _ in shares_of(images)] if last else []
    total, mixed, stacked = refs
    made = (
        [operators[i * cell_count + c] for c in range(cell_count)]
        for i in range(operators.shape[0] // cell_count)
    )
    add_blocks(cap, square, payloads, made, before, total, mixed, stacked)
    if last:
        z = lax.axis_index("image")
        half = outs[0].shape[1]
        for ref, (part, distances, _) in zip(outs, shares_of(images)):
            for i, k in enumerate(distances):
                at = pl.multiple_of((z ^ k) * (2 * half) + part * half, half)
                taken = total[:, pl.ds(at, half), :].astype(ref.dtype)
                if len(distances) == 1:
                    ref[...] = taken
                else:
                    ref[i * cell_count : (i + 1) * cell_count] = taken


def on_chip(kernel, name, args, out_shape, scratch=()):
    vmem = pl.BlockSpec(memory_space=pltpu.VMEM)
    return pl.pallas_call(
        kernel,
        out_shape=out_shape,
        in_specs=[vmem] * len(args),
        out_specs=[vmem] * len(out_shape),
        scratch_shapes=list(scratch),
        compiler_params=pltpu.CompilerParams(vmem_limit_bytes=VMEM_LIMIT),
        cost_estimate=pl.CostEstimate(
            flops=CHI_FLOPS, bytes_accessed=CHI_BYTES, transcendentals=0
        ),
        name=name,
    )(*args)


def chi_scratch(cell_count, width, depth):
    return [pltpu.VMEM((cell_count, width, depth), BF16), pltpu.VMEM((depth, width), BF16)]


def early_part(cap, pairs, cell_count, square, payloads, given, first):
    count, width = len(payloads), payloads[0].shape[1]
    out_shape = [jax.ShapeDtypeStruct((cell_count, width, width), F32)]
    if first:
        shape = (len(given) * given[0].shape[1], given[0].shape[0])
        out_shape.append(jax.ShapeDtypeStruct(shape, BF16))
    return on_chip(
        functools.partial(early_kernel, count, cap, pairs, cell_count, square, first),
        "chi_of_early_payloads",
        list(payloads) + list(given),
        out_shape,
        chi_scratch(cell_count, width, count * cap * square),
    )


def operators_part(cap, pairs, cell_count, square, lists, table):
    count = lists.shape[0] // LIST_ROWS
    lanes = min(QUAD, cap) * square
    groups = count * cap * square // lanes
    return on_chip(
        functools.partial(operators_kernel, count, cap, pairs, cell_count, square),
        "operators_of_late_payloads",
        [lists, table],
        [jax.ShapeDtypeStruct((groups * cell_count, lanes, lanes), BF16)],
    )[0]


def late_part(cap, cell_count, square, images, payloads, before, operators, last):
    count, width = len(payloads), payloads[0].shape[1]
    full = (cell_count, width, width)
    scratch = chi_scratch(cell_count, width, count * cap * square)
    out_shape = [jax.ShapeDtypeStruct(full, F32)]
    if last:
        half = width // images // 2
        out_shape = [
            jax.ShapeDtypeStruct((len(distances) * cell_count, half, width), dtype)
            for _, distances, dtype in shares_of(images)
        ]
        scratch = [pltpu.VMEM(full, F32)] + scratch
    return on_chip(
        functools.partial(late_kernel, count, cap, cell_count, square, last),
        "chi_of_late_payloads",
        list(payloads) + [before, operators],
        out_shape,
        scratch,
    )


def transform_kernel(cell_count, step, counts, phases, *refs):
    refs = list(refs)
    halves = [[refs.pop(0) for _ in range(n)] for n in counts]
    out, total, shaped, sems = refs
    for i, (own, *received) in enumerate(halves):
        acc = own[...]
        for part in received:
            acc = acc + part[0:cell_count].astype(F32)
        total[:, i * acc.shape[1] : (i + 1) * acc.shape[1], :] = acc
    points, share, width = out.shape
    tile = min(share, 32)

    def copy(i):
        at = pl.ds(i * step, step)
        return pltpu.make_async_copy(shaped.at[at], out.at[at], sems.at[i])

    @pl.loop(0, points // step)
    def _(i):
        for row in range(0, share, tile):
            parts = [total[c, row : row + tile, :] for c in range(cell_count)]
            for j in range(step):
                acc = phases[0, i * step + j] * parts[0]
                for c in range(1, cell_count):
                    acc = acc + phases[c, i * step + j] * parts[c]
                shaped[i * step + j, row : row + tile, :] = acc
        copy(i).start()

    @pl.loop(0, points // step)
    def _(i):
        copy(i).wait()


def transform(phases, halves):
    cell_count, rows, width = halves[0][0].shape
    share = rows * len(halves)
    points = phases.shape[1]
    step = 8
    vmem = pl.BlockSpec(memory_space=pltpu.VMEM)
    args = [x for half in halves for x in half]
    return pl.pallas_call(
        functools.partial(transform_kernel, cell_count, step, [len(half) for half in halves]),
        out_shape=jax.ShapeDtypeStruct((points, share, width), F32),
        in_specs=[pl.BlockSpec(memory_space=pltpu.SMEM)] + [vmem] * len(args),
        out_specs=pl.BlockSpec(memory_space=pltpu.HBM),
        scratch_shapes=[
            pltpu.VMEM((cell_count, share, width), F32),
            pltpu.VMEM((points, share, width), F32),
            pltpu.SemaphoreType.DMA((points // step,)),
        ],
        compiler_params=pltpu.CompilerParams(vmem_limit_bytes=VMEM_LIMIT),
        cost_estimate=pl.CostEstimate(
            flops=2 * points * cell_count * share * width,
            bytes_accessed=points * share * width * 4,
            transcendentals=0,
        ),
        name="to_k_points",
    )(phases, *args)


def swap(array, axis, k):
    size = lax.axis_size(axis)
    return lax.ppermute(array, axis, [(i, i ^ k) for i in range(size)])


def local(blocks, block_owner, block_basis, pair_images, pair_cell, lattice, dens_occ, dens_virt):
    owners, images = lax.axis_size("ri"), lax.axis_size("image")
    pairs = pair_cell.shape[1]
    cell_count = lattice.shape[0]
    cap = max(2, (2 * blocks.shape[0] + owners - 1) // owners)

    packed = pack(owners, cap, blocks, block_owner, block_basis, pair_images, pair_cell)
    square = blocks.shape[1]
    evens = [6, 2, 4] if owners == 8 else list(range(owners - 2, 1, -2))
    odds = [k ^ 1 for k in evens]
    payload = {0: packed[0]}
    payload.update({k: swap(packed[k], "ri", k) for k in evens})
    for k in odds:
        payload[k ^ 1], later = lax.optimization_barrier((payload[k ^ 1], packed[k]))
        payload[k] = swap(later, "ri", k)
    payload[evens[0]], near = lax.optimization_barrier((payload[evens[0]], packed[1]))
    payload[1] = swap(near, "ri", 1)
    lists = [payload[k][cap * square + LIST_ROWS :] for k in evens]
    lists = swap(jnp.concatenate(lists, axis=0), "ri", 1)
    density = jnp.concatenate([dens_occ[0].T, dens_virt[0].T], axis=0)
    pieces = density[None]
    k = 1
    while k < images:
        pieces = jnp.concatenate([pieces, swap(pieces, "image", k)], axis=0)
        k = 2 * k
    pieces = [pieces[i] for i in range(images)]

    given = pieces
    early = [0, 1] + evens
    for at in range(0, len(early), PART):
        chosen = [payload[k] for k in early[at : at + PART]]
        out = early_part(cap, pairs, cell_count, square, chosen, given, at == 0)
        table = out[1] if at == 0 else table
        given = [out[0], table]
    chi = out[0]
    for at in range(0, len(odds), PART):
        chosen = [payload[k] for k in odds[at : at + PART]]
        part = lists[at * LIST_ROWS : (at + len(chosen)) * LIST_ROWS]
        operators = operators_part(cap, pairs, cell_count, square, part, table)
        last = at + PART >= len(odds)
        out = late_part(cap, cell_count, square, images, chosen, chi, operators, last)
        chi = out[0]
    halves, sends = [[own] for own in out[:2]], out[2:]
    plan = shares_of(images)[2:]
    if by_halving(images):
        forward, sends, plan = sends[0], sends[1:], plan[1:]
    received = [swap(x, "image", d[0]) for x, (_, d, _) in zip(sends, plan)]
    for x, (part, _, _) in zip(received, plan):
        halves[part].append(x)
    if by_halving(images):
        forward = (forward + received[0][cell_count:].astype(F32)).astype(BF16)
        halves[1].append(swap(forward, "image", 2))

    points = jnp.arange(KGRID * KGRID, dtype=jnp.int32)
    wrapped = (
        lattice[:, 0:1] * (points // KGRID)[None, :] + lattice[:, 1:2] * (points % KGRID)[None, :]
    ) % KGRID
    angles = 2.0 * math.pi / KGRID * wrapped.astype(F32)
    phases = jnp.concatenate([jnp.cos(angles), jnp.sin(angles)], axis=1)
    result = transform(phases, halves)
    return result.reshape((2, KGRID * KGRID, 1) + result.shape[1:])


def solution(mesh):
    placed = (
        P(("image", "ri"), None, None),
        P(("image", "ri"), None),
        P(("image", "ri"), None),
        P(("image", "ri"), None, None),
        P(("image", "ri"), None),
        P(),
        P("image", None, None),
        P("image", None, None),
    )
    return jax.shard_map(
        local,
        mesh=mesh,
        in_specs=placed,
        out_specs=P(None, None, "ri", "image", None),
        check_vma=False,
    )
```

time: 55.1 us -> 53 us (0.962)
  waiting for transfers between devices: 20.3 us -> 14 us
  starting transfers between devices: 15.5 us -> 20 us
    ppermute x12 -> x15, waiting for transfers between devices: 20.3 us -> 14 us  [swap(): return lax.ppermute(array, axis, [(i, i ^ k) for i in range(size)])]
    ppermute x12 -> x15, starting transfers between devices: 15.5 us -> 20 us  [swap(): return lax.ppermute(array, axis, [(i, i ^ k) for i in range(size)])]
    pallas_call x3 -> x4, Pallas kernels: 13.8 us -> 13.8 us  [the longest x3 9.66 us: on_chip(): pl.pallas_call(kernel, out_shape=out_shape, in_specs=[vmem] * len(args),...]
  transfers between devices with their start and end apart: 12 -> 15, of which waited for: 6 -> 7; matrix products, arithmetic and copies ran while one was open for 3% -> 3% of each run, Pallas kernels for 12% -> 17%
where the time goes in v3:
time: 53 us; the launch traced here: 52.7 us
  starting transfers between devices  20 us (38%)
  Pallas kernels  14.8 us (28%)
  waiting for transfers between devices  14 us (26%)
  local copies, waits for them, and re-layouts  1.99 us (4%)
  other arithmetic  1.73 us (3%)
    ppermute x15, starting transfers between devices, swap(): return lax.ppermute(array, axis, [(i, i ^ k) for i in range(size)])  20 us
    ppermute x15, waiting for transfers between devices, swap(): return lax.ppermute(array, axis, [(i, i ^ k) for i in range(size)])  14 us
    pallas_call x3, Pallas kernels, on_chip(): pl.pallas_call(kernel, out_shape=out_shape, in_specs=[vmem] * len(args),...  9.66 us
    pallas_call x1, Pallas kernels, transform(): pl.pallas_call(functools.partial(transform_kernel, cell_count, step, [len...  4.17 us
    unnamed x2, local copies, waits for them, and re-layouts  1.22 us
  transfers between devices with their start and end apart: 15, of which 7 were waited for; matrix products, arithmetic and copies ran while one was open for 3% of the time, Pallas kernels for 17%

profile of v3, /device:TPU:0, one launch (start us, length us, event | category | flops | bytes accessed | tf_op | source)
XLA Modules:
  0.0 52.7 jit_solution(2518552340489607233)
XLA Ops:
  0.0 0.8 %fusion.5 = (bf16[1,128,256]{2,1,0:T(8,128)(2,1)S(1)}, bf16[128,256]{1,0:T(8,128)(2,1)S(1)}) fusion(bf16[64,256]{1,0:T(8,128)(2,1)} %bitcast.27, bf16[64,256]{1,0:T(8,128)(2,1)} %bitcast.28), kind=kLoop, calls=%fused_computation.23 | loop fusion | flops 131072 | bytes 196608 | tf_op jit(solution)/shard_map/broadcast_in_dim | solution.py:427
  0.8 3.1 %collective-permute-start.7 = (bf16[1,128,256]{2,1,0:T(8,128)(2,1)S(1)}, bf16[1,128,256]{2,1,0:T(8,128)(2,1)S(1)}, u32[]{:S(2)}, u32[]{:S(2)}) collective-permute-start(bf16[1,128,256]{2,1,0:T(8,128)(2,1)S(1)} %get-tuple-element.57), channel_id=1, source_target_pairs={{0,8},{8,0},{16,24},{24,16},{1,9},{9,1},{17,25},{25,17},{2,10},{10... | collective-permute-start | bytes 196616 | tf_op jit(solution)/shard_map/ppermute | solution.py:404
  3.9 0.7 %pad_add_fusion.refs_0_ = s32[15,32]{1,0:T(8,128)S(1)} fusion(s32[4,32]{1,0:T(4,128)} %bitcast.30, s32[8,32]{1,0:T(8,128)} %bitcast.29, s32[2,32]{1,0:T(2,128)} %bitcast.31, s32[1,32]{1,0:T(1,128)} %bitcast.32), kind=kLoop, calls=%fused_computation.6 | loop fusion | flops 1440 | bytes 3840 | tf_op jit(solution)/shard_map/concatenate | solution.py:94
  4.6 0.0 copy-start
  4.6 1.2 %copy-done = bf16[32,64,256]{2,1,0:T(8,128)(2,1)S(1)} copy-done((bf16[32,64,256]{2,1,0:T(8,128)(2,1)S(1)}, bf16[32,64,256]{2,1,0:T(8,128)(2,1)}, u32[]{:S(2)}) %copy-start) | copy-done | bytes 1048600
  5.8 1.0 %pack_by_owner.1 = (bf16[528,256]{1,0:T(8,128)(2,1)S(1)}, bf16[528,256]{1,0:T(8,128)(2,1)S(1)}, bf16[544,256]{1,0:T(8,128)(2,1)S(1)}, bf16[512,256]{1,0:T(8,128)...) custom-call(s32[15,32]{1,0:T(8,128)S(1)} %pad_add_fusion.refs_0_, ...), custom_call_target="tpu_custom_call" | custom-call | bytes 6291456 | tf_op jit(solution)/shard_map/pack_by_owner/pallas_call | solution.py:104
  6.8 2.5 %collective-permute-start = (bf16[544,256]{1,0:T(8,128)(2,1)S(1)}, bf16[544,256]{1,0:T(8,128)(2,1)S(1)}, u32[]{:S(2)}, u32[]{:S(2)}) collective-permute-start(bf16[544,256]{1,0:T(8,128)(2,1)S(1)} %get-tuple-element.30), channel_id=1, source_target_pairs={{0,6},{1,7},{2,4},{3,5},{4,2},{5,3},{6,0},{7,1},{8,14},{9,15},{10,... | collective-permute-start | bytes 835592 | tf_op jit(solution)/shard_map/ppermute | solution.py:404
  9.3 0.5 %collective-permute-start.2 = (bf16[544,256]{1,0:T(8,128)(2,1)S(1)}, bf16[544,256]{1,0:T(8,128)(2,1)S(1)}, u32[]{:S(2)}, u32[]{:S(2)}) collective-permute-start(bf16[544,256]{1,0:T(8,128)(2,1)S(1)} %get-tuple-element.33), channel_id=1, source_target_pairs={{0,2},{1,3},{2,0},{3,1},{4,6},{5,7},{6,4},{7,5},{8,10},{9,11},{10,... | collective-permute-start | bytes 835592 | tf_op jit(solution)/shard_map/ppermute | solution.py:404
  9.9 0.5 collective-permute-start.4
  10.4 0.8 %slice_bitcast_fusion.3 = (s32[4]{0:T(128)S(1)}, s32[4]{0:T(128)S(1)}) fusion(s32[4,2]{0,1:T(2,128)} %param.13), kind=kLoop, calls=%fused_computation.22 | loop fusion | bytes 64 | tf_op jit(solution)/shard_map/mul | solution.py:462
  11.1 0.0 collective-permute-done.7
  11.1 2.7 %collective-permute-start.8 = (bf16[2,128,256]{2,1,0:T(8,128)(2,1)S(1)}, bf16[2,128,256]{2,1,0:T(8,128)(2,1)S(1)}, u32[]{:S(2)}, u32[]{:S(2)}) collective-permute-start(bf16[2,128,256]{2,1,0:T(8,128)(2,1)S(1)} %pad_maximum_fusion), channel_id=1, source_target_pairs={{0,16},{8,24},{16,0},{24,8},{1,17},{9,25},{17,1},{25,9},{2,18},{10... | collective-permute-start | bytes 393224 | tf_op jit(solution)/shard_map/ppermute | solution.py:404
  13.8 3.6 %collective-permute-done.refs_2_ = bf16[544,256]{1,0:T(8,128)(2,1)S(1)} collective-permute-done((bf16[544,256]{1,0:T(8,128)(2,1)S(1)}, bf16[544,256]{1,0:T(8,128)(2,1)S(1)}, u32[]{:S(2)}, u32[]{:S(2)}) %collective-permute-start) | collective-permute-done | bytes 278560 | tf_op jit(solution)/shard_map/ppermute | solution.py:404
  17.4 0.0 collective-permute-start.1
  17.4 2.6 %collective-permute-start.6 = (bf16[528,256]{1,0:T(8,128)(2,1)S(1)}, bf16[528,256]{1,0:T(8,128)(2,1)S(1)}, u32[]{:S(2)}, u32[]{:S(2)}) collective-permute-start(bf16[528,256]{1,0:T(8,128)(2,1)S(1)} %get-tuple-element.42), channel_id=1, source_target_pairs={{0,1},{1,0},{2,3},{3,2},{4,5},{5,4},{6,7},{7,6},{8,9},{9,8},{10,11... | collective-permute-start | bytes 811016 | tf_op jit(solution)/shard_map/ppermute | solution.py:404
  20.0 2.5 %collective-permute-done.2.refs_3_ = bf16[544,256]{1,0:T(8,128)(2,1)S(1)} collective-permute-done((bf16[544,256]{1,0:T(8,128)(2,1)S(1)}, bf16[544,256]{1,0:T(8,128)(2,1)S(1)}, u32[]{:S(2)}, u32[]{:S(2)}) %collective-permute-start.2) | collective-permute-done | bytes 278560 | tf_op jit(solution)/shard_map/ppermute | solution.py:404
  22.5 0.0 collective-permute-start.3
  22.5 0.0 collective-permute-done.4.refs_4_
  22.5 1.7 %collective-permute-start.5 = (bf16[512,256]{1,0:T(8,128)(2,1)S(1)}, bf16[512,256]{1,0:T(8,128)(2,1)S(1)}, u32[]{:S(2)}, u32[]{:S(2)}) collective-permute-start(bf16[512,256]{1,0:T(8,128)(2,1)S(1)} %get-tuple-element.38), channel_id=1, source_target_pairs={{0,5},{1,4},{2,7},{3,6},{4,1},{5,0},{6,3},{7,2},{8,13},{9,12},{10,... | collective-permute-start | bytes 786440 | tf_op jit(solution)/shard_map/ppermute | solution.py:404
  24.2 0.0 collective-permute-done.8
  24.2 0.0 collective-permute-start.9
  24.3 0.0 collective-permute-done.6.refs_1_
  24.3 6.0 %chi_of_early_payloads.1 = (f32[4,256,256]{2,1,0:T(8,128)S(1)}, bf16[1024,128]{1,0:T(8,128)(2,1)S(1)}) custom-call(bf16[528,256]{1,0:T(8,128)(2,1)S(1)} %get-tuple-element.39.refs_0_, bf16[528,256]{1,0:T(8,128)(2,1)S(1)} %collective-permute-done.6.refs_1_, bf16[544,256]{1,0:T(8,128)(2,1)S(1)} %collective-permute-done.refs_2_, ...), custom_call_target="tpu_custom_call" | custom-call | flops 1048576 | bytes 1024 | tf_op jit(solution)/shard_map/chi_of_early_payloads/pallas_call | solution.py:277
  30.2 0.0 collective-permute-done.9.lists
  30.3 1.8 %operators_of_late_payloads.1.refs_4_ = bf16[24,256,256]{2,1,0:T(8,128)(2,1)S(1)} custom-call(bf16[48,256]{1,0:T(8,128)(2,1)S(1)} %collective-permute-done.9.lists, bf16[1024,128]{1,0:T(8,128)(2,1)S(1)} %get-tuple-element.47.table), custom_call_target="tpu_custom_call" | custom-call | flops 1048576 | bytes 1024 | tf_op jit(solution)/shard_map/operators_of_late_payloads/pallas_call | solution.py:277
  32.1 0.0 collective-permute-done.1.refs_0_
  32.1 0.6 %collective-permute-done.3.refs_1_ = bf16[512,256]{1,0:T(8,128)(2,1)S(1)} collective-permute-done((bf16[512,256]{1,0:T(8,128)(2,1)S(1)}, bf16[512,256]{1,0:T(8,128)(2,1)S(1)}, u32[]{:S(2)}, u32[]{:S(2)}) %collective-permute-start.3) | collective-permute-done | bytes 262176 | tf_op jit(solution)/shard_map/ppermute | solution.py:404
  32.6 0.3 collective-permute-done.5.refs_2_
  33.0 1.9 %chi_of_late_payloads.1 = (f32[4,32,256]{2,1,0:T(8,128)S(1)}, f32[4,32,256]{2,1,0:T(8,128)S(1)}, f32[4,32,256]{2,1,0:T(8,128)S(1)}, bf16[8,32,256]{2,1,0:T(8,128...) custom-call(bf16[512,256]{1,0:T(8,128)(2,1)S(1)} %collective-permute-d, ...), custom_call_target="tpu_custom_call" | custom-call | flops 1048576 | bytes 1024 | tf_op jit(solution)/shard_map/chi_of_late_payloads/pallas_call | solution.py:277
  34.9 0.2 collective-permute-start.13
  35.1 0.1 fusion.4
  35.2 3.0 %collective-permute-start.10 = (bf16[4,32,256]{2,1,0:T(8,128)(2,1)S(1)}, bf16[4,32,256]{2,1,0:T(8,128)(2,1)S(1)}, u32[]{:S(2)}, u32[]{:S(2)}) collective-permute-start(bf16[4,32,256]{2,1,0:T(8,128)(2,1)S(1)} %get-tuple-element.49), channel_id=1, source_target_pairs={{0,16},{8,24},{16,0},{24,8},{1,17},{9,25},{17,1},{25,9},{2,18},{10... | collective-permute-start | bytes 196616 | tf_op jit(solution)/shard_map/ppermute | solution.py:404
  38.2 1.3 %collective-permute-start.11 = (bf16[4,32,256]{2,1,0:T(8,128)(2,1)S(1)}, bf16[4,32,256]{2,1,0:T(8,128)(2,1)S(1)}, u32[]{:S(2)}, u32[]{:S(2)}) collective-permute-start(bf16[4,32,256]{2,1,0:T(8,128)(2,1)S(1)} %get-tuple-element.50), channel_id=1, source_target_pairs={{0,24},{8,16},{16,8},{24,0},{1,25},{9,17},{17,9},{25,1},{2,26},{10... | collective-permute-start | bytes 196616 | tf_op jit(solution)/shard_map/ppermute | solution.py:404
  39.5 0.2 collective-permute-start.12
  39.7 2.5 %collective-permute-done.13.refs_5_ = bf16[8,32,256]{2,1,0:T(8,128)(2,1)S(1)} collective-permute-done((bf16[8,32,256]{2,1,0:T(8,128)(2,1)S(1)}, bf16[8,32,256]{2,1,0:T(8,128)(2,1)S(1)}, u32[]{:S(2)}, u32[]{:S(2)}) %collective-permute-start.13) | collective-permute-done | bytes 131104 | tf_op jit(solution)/shard_map/ppermute | solution.py:404
  42.3 1.7 %collective-permute-start.14 = (bf16[4,32,256]{2,1,0:T(8,128)(2,1)S(1)}, bf16[4,32,256]{2,1,0:T(8,128)(2,1)S(1)}, u32[]{:S(2)}, u32[]{:S(2)}) collective-permute-start(bf16[4,32,256]{2,1,0:T(8,128)(2,1)S(1)} %add_convert_fusion), channel_id=1, source_target_pairs={{0,16},{8,24},{16,0},{24,8},{1,17},{9,25},{17,1},{25,9},{2,18},{10... | collective-permute-start | bytes 196616 | tf_op jit(solution)/shard_map/ppermute | solution.py:404
  44.0 0.1 pad_maximum_fusion.3.phases
  44.0 0.0 collective-permute-done.10.refs_1_
  44.0 2.1 %collective-permute-done.11.refs_2_ = bf16[4,32,256]{2,1,0:T(8,128)(2,1)S(1)} collective-permute-done((bf16[4,32,256]{2,1,0:T(8,128)(2,1)S(1)}, bf16[4,32,256]{2,1,0:T(8,128)(2,1)S(1)}, u32[]{:S(2)}, u32[]{:S(2)}) %collective-permute-start.11) | collective-permute-done | bytes 65568 | tf_op jit(solution)/shard_map/ppermute | solution.py:404
  46.2 0.0 collective-permute-done.12.refs_3_
  46.2 2.3 %collective-permute-done.14.refs_6_ = bf16[4,32,256]{2,1,0:T(8,128)(2,1)S(1)} collective-permute-done((bf16[4,32,256]{2,1,0:T(8,128)(2,1)S(1)}, bf16[4,32,256]{2,1,0:T(8,128)(2,1)S(1)}, u32[]{:S(2)}, u32[]{:S(2)}) %collective-permute-start.14) | collective-permute-done | bytes 65568 | tf_op jit(solution)/shard_map/ppermute | solution.py:404
  48.5 4.2 %to_k_points.1 = f32[128,64,256]{2,1,0:T(8,128)} custom-call(f32[4,128]{1,0:T(4,128)S(1)} %pad_maximum_fusion.3.phases, f32[4,32,256]{2,1,0:T(8,128)S(1)} %get-tuple-element.48.refs_0_, bf16[4,32,256]{2,1,0:T(8,128)(2,1)S(1)} %collective-permute-done.10.refs_1_, bf16[4,32,256]{2,1,0:T(8,128)(2,1)S(1)} %collective-permute-done.11.refs_2_, ...), custom_call_target="tpu_custom_call" | custom-call | flops 16777216 | bytes 8388608 | tf_op jit(solution)/shard_map/to_k_points/pallas_call | solution.py:382
  (8 shorter events, 0.1 us)
Async XLA Ops:
  0.8 10.3 %collective-permute-start.7 = (bf16[1,128,256]{2,1,0:T(8,128)(2,1)S(1)}, bf16[1,128,256]{2,1,0:T(8,128)(2,1)S(1)}, u32[]{:S(2)}, u32[]{:S(2)}) collective-permute-start(bf16[1,128,256]{2,1,0:T(8,128)(2,1)S(1)} %get-tuple-element.57), channel_id=1, source_target_pairs={{0,8},{8,0},{16,24},{24,16},{1,9},{9,1},{17,25},{25,17},{2,10},{10... | collective-permute-start | bytes 196616 | tf_op jit(solution)/shard_map/ppermute | solution.py:404
  4.6 1.2 %copy-start = (bf16[32,64,256]{2,1,0:T(8,128)(2,1)S(1)}, bf16[32,64,256]{2,1,0:T(8,128)(2,1)}, u32[]{:S(2)}) copy-start(bf16[32,64,256]{2,1,0:T(8,128)(2,1)} %refs_1_.1) | copy-start | bytes 3145732
  6.8 10.6 %collective-permute-start = (bf16[544,256]{1,0:T(8,128)(2,1)S(1)}, bf16[544,256]{1,0:T(8,128)(2,1)S(1)}, u32[]{:S(2)}, u32[]{:S(2)}) collective-permute-start(bf16[544,256]{1,0:T(8,128)(2,1)S(1)} %get-tuple-element.30), channel_id=1, source_target_pairs={{0,6},{1,7},{2,4},{3,5},{4,2},{5,3},{6,0},{7,1},{8,14},{9,15},{10,... | collective-permute-start | bytes 835592 | tf_op jit(solution)/shard_map/ppermute | solution.py:404
  9.3 13.2 %collective-permute-start.2 = (bf16[544,256]{1,0:T(8,128)(2,1)S(1)}, bf16[544,256]{1,0:T(8,128)(2,1)S(1)}, u32[]{:S(2)}, u32[]{:S(2)}) collective-permute-start(bf16[544,256]{1,0:T(8,128)(2,1)S(1)} %get-tuple-element.33), channel_id=1, source_target_pairs={{0,2},{1,3},{2,0},{3,1},{4,6},{5,7},{6,4},{7,5},{8,10},{9,11},{10,... | collective-permute-start | bytes 835592 | tf_op jit(solution)/shard_map/ppermute | solution.py:404
  9.9 12.7 %collective-permute-start.4 = (bf16[544,256]{1,0:T(8,128)(2,1)S(1)}, bf16[544,256]{1,0:T(8,128)(2,1)S(1)}, u32[]{:S(2)}, u32[]{:S(2)}) collective-permute-start(bf16[544,256]{1,0:T(8,128)(2,1)S(1)} %get-tuple-element.36), channel_id=1, source_target_pairs={{0,4},{1,5},{2,6},{3,7},{4,0},{5,1},{6,2},{7,3},{8,12},{9,13},{10,... | collective-permute-start | bytes 835592 | tf_op jit(solution)/shard_map/ppermute | solution.py:404
  11.1 13.1 %collective-permute-start.8 = (bf16[2,128,256]{2,1,0:T(8,128)(2,1)S(1)}, bf16[2,128,256]{2,1,0:T(8,128)(2,1)S(1)}, u32[]{:S(2)}, u32[]{:S(2)}) collective-permute-start(bf16[2,128,256]{2,1,0:T(8,128)(2,1)S(1)} %pad_maximum_fusion), channel_id=1, source_target_pairs={{0,16},{8,24},{16,0},{24,8},{1,17},{9,25},{17,1},{25,9},{2,18},{10... | collective-permute-start | bytes 393224 | tf_op jit(solution)/shard_map/ppermute | solution.py:404
  17.4 14.7 %collective-permute-start.1 = (bf16[512,256]{1,0:T(8,128)(2,1)S(1)}, bf16[512,256]{1,0:T(8,128)(2,1)S(1)}, u32[]{:S(2)}, u32[]{:S(2)}) collective-permute-start(bf16[512,256]{1,0:T(8,128)(2,1)S(1)} %get-tuple-element.32), channel_id=1, source_target_pairs={{0,7},{1,6},{2,5},{3,4},{4,3},{5,2},{6,1},{7,0},{8,15},{9,14},{10,... | collective-permute-start | bytes 786440 | tf_op jit(solution)/shard_map/ppermute | solution.py:404
  17.4 6.9 %collective-permute-start.6 = (bf16[528,256]{1,0:T(8,128)(2,1)S(1)}, bf16[528,256]{1,0:T(8,128)(2,1)S(1)}, u32[]{:S(2)}, u32[]{:S(2)}) collective-permute-start(bf16[528,256]{1,0:T(8,128)(2,1)S(1)} %get-tuple-element.42), channel_id=1, source_target_pairs={{0,1},{1,0},{2,3},{3,2},{4,5},{5,4},{6,7},{7,6},{8,9},{9,8},{10,11... | collective-permute-start | bytes 811016 | tf_op jit(solution)/shard_map/ppermute | solution.py:404
  22.5 10.1 %collective-permute-start.3 = (bf16[512,256]{1,0:T(8,128)(2,1)S(1)}, bf16[512,256]{1,0:T(8,128)(2,1)S(1)}, u32[]{:S(2)}, u32[]{:S(2)}) collective-permute-start(bf16[512,256]{1,0:T(8,128)(2,1)S(1)} %get-tuple-element.35), channel_id=1, source_target_pairs={{0,3},{1,2},{2,1},{3,0},{4,7},{5,6},{6,5},{7,4},{8,11},{9,10},{10,... | collective-permute-start | bytes 786440 | tf_op jit(solution)/shard_map/ppermute | solution.py:404
  22.5 10.5 %collective-permute-start.5 = (bf16[512,256]{1,0:T(8,128)(2,1)S(1)}, bf16[512,256]{1,0:T(8,128)(2,1)S(1)}, u32[]{:S(2)}, u32[]{:S(2)}) collective-permute-start(bf16[512,256]{1,0:T(8,128)(2,1)S(1)} %get-tuple-element.38), channel_id=1, source_target_pairs={{0,5},{1,4},{2,7},{3,6},{4,1},{5,0},{6,3},{7,2},{8,13},{9,12},{10,... | collective-permute-start | bytes 786440 | tf_op jit(solution)/shard_map/ppermute | solution.py:404
  24.2 6.0 %collective-permute-start.9 = (bf16[48,256]{1,0:T(8,128)(2,1)S(1)}, bf16[48,256]{1,0:T(8,128)(2,1)S(1)}, u32[]{:S(2)}, u32[]{:S(2)}) collective-permute-start(bf16[48,256]{1,0:T(8,128)(2,1)S(1)} %pad_maximum_fusion.2), channel_id=1, source_target_pairs={{0,1},{1,0},{2,3},{3,2},{4,5},{5,4},{6,7},{7,6},{8,9},{9,8},{10,11... | collective-permute-start | bytes 73736 | tf_op jit(solution)/shard_map/ppermute | solution.py:404
  34.9 7.4 %collective-permute-start.13 = (bf16[8,32,256]{2,1,0:T(8,128)(2,1)S(1)}, bf16[8,32,256]{2,1,0:T(8,128)(2,1)S(1)}, u32[]{:S(2)}, u32[]{:S(2)}) collective-permute-start(bf16[8,32,256]{2,1,0:T(8,128)(2,1)S(1)} %get-tuple-element.53), channel_id=1, source_target_pairs={{0,8},{8,0},{16,24},{24,16},{1,9},{9,1},{17,25},{25,17},{2,10},{10... | collective-permute-start | bytes 393224 | tf_op jit(solution)/shard_map/ppermute | solution.py:404
  35.2 8.8 %collective-permute-start.10 = (bf16[4,32,256]{2,1,0:T(8,128)(2,1)S(1)}, bf16[4,32,256]{2,1,0:T(8,128)(2,1)S(1)}, u32[]{:S(2)}, u32[]{:S(2)}) collective-permute-start(bf16[4,32,256]{2,1,0:T(8,128)(2,1)S(1)} %get-tuple-element.49), channel_id=1, source_target_pairs={{0,16},{8,24},{16,0},{24,8},{1,17},{9,25},{17,1},{25,9},{2,18},{10... | collective-permute-start | bytes 196616 | tf_op jit(solution)/shard_map/ppermute | solution.py:404
  38.2 8.0 %collective-permute-start.11 = (bf16[4,32,256]{2,1,0:T(8,128)(2,1)S(1)}, bf16[4,32,256]{2,1,0:T(8,128)(2,1)S(1)}, u32[]{:S(2)}, u32[]{:S(2)}) collective-permute-start(bf16[4,32,256]{2,1,0:T(8,128)(2,1)S(1)} %get-tuple-element.50), channel_id=1, source_target_pairs={{0,24},{8,16},{16,8},{24,0},{1,25},{9,17},{17,9},{25,1},{2,26},{10... | collective-permute-start | bytes 196616 | tf_op jit(solution)/shard_map/ppermute | solution.py:404
  39.5 6.7 %collective-permute-start.12 = (bf16[4,32,256]{2,1,0:T(8,128)(2,1)S(1)}, bf16[4,32,256]{2,1,0:T(8,128)(2,1)S(1)}, u32[]{:S(2)}, u32[]{:S(2)}) collective-permute-start(bf16[4,32,256]{2,1,0:T(8,128)(2,1)S(1)} %get-tuple-element.51), channel_id=1, source_target_pairs={{0,8},{8,0},{16,24},{24,16},{1,9},{9,1},{17,25},{25,17},{2,10},{10... | collective-permute-start | bytes 196616 | tf_op jit(solution)/shard_map/ppermute | solution.py:404
  42.3 6.2 %collective-permute-start.14 = (bf16[4,32,256]{2,1,0:T(8,128)(2,1)S(1)}, bf16[4,32,256]{2,1,0:T(8,128)(2,1)S(1)}, u32[]{:S(2)}, u32[]{:S(2)}) collective-permute-start(bf16[4,32,256]{2,1,0:T(8,128)(2,1)S(1)} %add_convert_fusion), channel_id=1, source_target_pairs={{0,16},{8,24},{16,0},{24,8},{1,17},{9,25},{17,1},{25,9},{2,18},{10... | collective-permute-start | bytes 196616 | tf_op jit(solution)/shard_map/ppermute | solution.py:404

commit v4 on v3

--- a/solution.py
+++ b/solution.py
@@ -36,18 +36,12 @@
 
 
 def pack_kernel(n, cap, pairs, *refs):
-    ints, from_blocks, outs, rest = refs[0], refs[1], refs[2 : 2 + n], refs[2 + n :]
-    owner, blocks, table, lists, count, place, sems = rest
+    ints, blocks, outs, rest = refs[0], refs[1], refs[2 : 2 + n], refs[2 + n :]
+    owner, table, lists, count, place, sem = rest
     rows, square, width = blocks.shape
     me = lax.axis_index("ri")
-    pieces = 4
-    part = rows // pieces
-    started = [pltpu.make_async_copy(ints.at[pl.ds(0, 8)], owner, sems.at[pieces])]
-    for i in range(pieces):
-        at = pl.ds(i * part, part)
-        started.append(pltpu.make_async_copy(from_blocks.at[at], blocks.at[at], sems.at[i]))
-    for copy in started:
-        copy.start()
+    to_scalars = pltpu.make_async_copy(ints.at[pl.ds(0, 8)], owner, sem)
+    to_scalars.start()
     for k in range(n):
         count[k] = 0
     for k in range(n * cap):
@@ -69,7 +63,7 @@
     ordered = dot(chosen.astype(BF16), table[...].astype(BF16), (1, 1))
     lists[:, 0:128] = ordered.astype(BF16)
 
-    started[0].wait()
+    to_scalars.wait()
 
     @pl.loop(0, rows, unroll=4)
     def _(e):
@@ -78,8 +72,6 @@
         place[k * cap + r] = e
         count[k] = r + 1
 
-    for copy in started[1:]:
-        copy.wait()
     for k in range(n):
         for r in range(cap):
             outs[k][r * square : (r + 1) * square, :] = blocks[place[k * cap + r]]
@@ -104,19 +96,15 @@
     return pl.pallas_call(
         functools.partial(pack_kernel, n, cap, pairs),
         out_shape=[jax.ShapeDtypeStruct((height, width), BF16) for height in heights],
-        in_specs=[
-            pl.BlockSpec(memory_space=pltpu.VMEM),
-            pl.BlockSpec(memory_space=pltpu.HBM),
-        ],
+        in_specs=[pl.BlockSpec(memory_space=pltpu.VMEM)] * 2,
         out_specs=[pl.BlockSpec(memory_space=pltpu.VMEM)] * n,
         scratch_shapes=[
             pltpu.SMEM((8, rows), jnp.int32),
-            pltpu.VMEM(blocks.shape, BF16),
             pltpu.VMEM((128, rows), F32),
             pltpu.VMEM((n * LIST_ROWS, width), BF16),
             pltpu.SMEM((n,), jnp.int32),
             pltpu.SMEM((n * cap,), jnp.int32),
-            pltpu.SemaphoreType.DMA((5,)),
+            pltpu.SemaphoreType.DMA,
         ],
         compiler_params=pltpu.CompilerParams(vmem_limit_bytes=PACK_LIMIT),
         cost_estimate=pl.CostEstimate(flops=0, bytes_accessed=6 << 20, transcendentals=0),
@@ -340,31 +328,28 @@
     )
 
 
-def transform_kernel(cell_count, step, counts, phases, *refs):
-    refs = list(refs)
-    halves = [[refs.pop(0) for _ in range(n)] for n in counts]
-    out, total, shaped, sems = refs
-    for i, (own, *received) in enumerate(halves):
-        acc = own[...]
-        for part in received:
-            acc = acc + part[0:cell_count].astype(F32)
-        total[:, i * acc.shape[1] : (i + 1) * acc.shape[1], :] = acc
-    points, share, width = out.shape
-    tile = min(share, 32)
+def transform_kernel(cell_count, step, row_at, phases, own, *rest):
+    *received, out, total, shaped, sems = rest
+    acc = own[...]
+    for part in received:
+        acc = acc + part[0:cell_count].astype(F32)
+    total[...] = acc
+    points, rows, width = shaped.shape
 
     def copy(i):
         at = pl.ds(i * step, step)
-        return pltpu.make_async_copy(shaped.at[at], out.at[at], sems.at[i])
+        return pltpu.make_async_copy(
+            shaped.at[at], out.at[at, pl.ds(row_at, rows)], sems.at[i]
+        )
 
     @pl.loop(0, points // step)
     def _(i):
-        for row in range(0, share, tile):
-            parts = [total[c, row : row + tile, :] for c in range(cell_count)]
-            for j in range(step):
-                acc = phases[0, i * step + j] * parts[0]
-                for c in range(1, cell_count):
-                    acc = acc + phases[c, i * step + j] * parts[c]
-                shaped[i * step + j, row : row + tile, :] = acc
+        parts = [total[c] for c in range(cell_count)]
+        for j in range(step):
+            acc = phases[0, i * step + j] * parts[0]
+            for c in range(1, cell_count):
+                acc = acc + phases[c, i * step + j] * parts[c]
+            shaped[i * step + j] = acc
         copy(i).start()
 
     @pl.loop(0, points // step)
@@ -372,31 +357,45 @@
         copy(i).wait()
 
 
-def transform(phases, halves):
-    cell_count, rows, width = halves[0][0].shape
-    share = rows * len(halves)
+def transform(phases, own, received, row_at, share, so_far):
+    cell_count, rows, width = own.shape
     points = phases.shape[1]
-    step = 8
+    step = 16
     vmem = pl.BlockSpec(memory_space=pltpu.VMEM)
-    args = [x for half in halves for x in half]
+    hbm = pl.BlockSpec(memory_space=pltpu.HBM)
+    args = [phases, own, *received]
+    specs = [pl.BlockSpec(memory_space=pltpu.SMEM)] + [vmem] * (1 + len(received))
+    aliases = {}
+    kernel = functools.partial(transform_kernel, cell_count, step, row_at)
+    if so_far is not None:
+        aliases = {len(args): 0}
+        inner = kernel
+        at = len(args)
+
+        def kernel(*refs):
+            inner(*refs[:at], *refs[at + 1 :])
+
+        args.append(so_far)
+        specs.append(hbm)
     return pl.pallas_call(
-        functools.partial(transform_kernel, cell_count, step, [len(half) for half in halves]),
+        kernel,
         out_shape=jax.ShapeDtypeStruct((points, share, width), F32),
-        in_specs=[pl.BlockSpec(memory_space=pltpu.SMEM)] + [vmem] * len(args),
-        out_specs=pl.BlockSpec(memory_space=pltpu.HBM),
+        in_specs=specs,
+        out_specs=hbm,
+        input_output_aliases=aliases,
         scratch_shapes=[
-            pltpu.VMEM((cell_count, share, width), F32),
-            pltpu.VMEM((points, share, width), F32),
+            pltpu.VMEM((cell_count, rows, width), F32),
+            pltpu.VMEM((points, rows, width), F32),
             pltpu.SemaphoreType.DMA((points // step,)),
         ],
         compiler_params=pltpu.CompilerParams(vmem_limit_bytes=VMEM_LIMIT),
         cost_estimate=pl.CostEstimate(
-            flops=2 * points * cell_count * share * width,
-            bytes_accessed=points * share * width * 4,
+            flops=2 * points * cell_count * rows * width,
+            bytes_accessed=points * rows * width * 4,
             transcendentals=0,
         ),
         name="to_k_points",
-    )(phases, *args)
+    )(*args)
 
 
 def swap(array, axis, k):
@@ -419,8 +418,9 @@
     for k in odds:
         payload[k ^ 1], later = lax.optimization_barrier((payload[k ^ 1], packed[k]))
         payload[k] = swap(later, "ri", k)
-    payload[evens[0]], near = lax.optimization_barrier((payload[evens[0]], packed[1]))
-    payload[1] = swap(near, "ri", 1)
+    payload[1], dens_occ, dens_virt = lax.optimization_barrier(
+        (swap(packed[1], "ri", 1), dens_occ, dens_virt)
+    )
     lists = [payload[k][cap * square + LIST_ROWS :] for k in evens]
     lists = swap(jnp.concatenate(lists, axis=0), "ri", 1)
     density = jnp.concatenate([dens_occ[0].T, dens_virt[0].T], axis=0)
@@ -463,7 +463,10 @@
     ) % KGRID
     angles = 2.0 * math.pi / KGRID * wrapped.astype(F32)
     phases = jnp.concatenate([jnp.cos(angles), jnp.sin(angles)], axis=1)
-    result = transform(phases, halves)
+    result = None
+    share = 2 * halves[0][0].shape[1]
+    for part, (own, *received) in enumerate(halves):
+        result = transform(phases, own, received, part * share // 2, share, result)
     return result.reshape((2, KGRID * KGRID, 1) + result.shape[1:])
 
 

time: 53 us -> 50.6 us (0.955)
  waiting for transfers between devices: 14 us -> 10 us
  Pallas kernels: 14.8 us -> 16.2 us
    ppermute x15, waiting for transfers between devices: 14 us -> 10 us  [swap(): return lax.ppermute(array, axis, [(i, i ^ k) for i in range(size)])]
    pallas_call x1 -> x2, Pallas kernels: 4.17 us -> 5.59 us  [transform(): pl.pallas_call(kernel, out_shape=jax.ShapeDtypeStruct((points, share, wid...]
  transfers between devices with their start and end apart: 15 -> 15, of which waited for: 7 -> 6; matrix products, arithmetic and copies ran while one was open for 3% -> 4% of each run, Pallas kernels for 17% -> 21%
where the time goes in v4:
time: 50.6 us; the launch traced here: 50.3 us
  starting transfers between devices  20.3 us (40%)
  Pallas kernels  16.2 us (32%)
  waiting for transfers between devices  10 us (20%)
  local copies, waits for them, and re-layouts  1.99 us (4%)
  other arithmetic  1.74 us (3%)
    ppermute x15, starting transfers between devices, swap(): return lax.ppermute(array, axis, [(i, i ^ k) for i in range(size)])  20.3 us
    ppermute x15, waiting for transfers between devices, swap(): return lax.ppermute(array, axis, [(i, i ^ k) for i in range(size)])  10 us
    pallas_call x3, Pallas kernels, on_chip(): pl.pallas_call(kernel, out_shape=out_shape, in_specs=[vmem] * len(args),...  9.66 us
    pallas_call x2, Pallas kernels, transform(): pl.pallas_call(kernel, out_shape=jax.ShapeDtypeStruct((points, share, wid...  5.59 us
    unnamed x2, local copies, waits for them, and re-layouts  1.22 us
  transfers between devices with their start and end apart: 15, of which 6 were waited for; matrix products, arithmetic and copies ran while one was open for 4% of the time, Pallas kernels for 21%

profile of v4, /device:TPU:0, one launch (start us, length us, event | category | flops | bytes accessed | tf_op | source)
XLA Modules:
  0.0 50.3 jit_solution(12205810937961372820)
XLA Ops:
  0.0 0.7 %pad_add_fusion.refs_0_ = s32[15,32]{1,0:T(8,128)S(1)} fusion(s32[4,32]{1,0:T(4,128)} %bitcast.30, s32[8,32]{1,0:T(8,128)} %bitcast.29, s32[2,32]{1,0:T(2,128)} %bitcast.31, s32[1,32]{1,0:T(1,128)} %bitcast.32), kind=kLoop, calls=%fused_computation.6 | loop fusion | flops 1440 | bytes 3840 | tf_op jit(solution)/shard_map/concatenate | solution.py:86
  0.7 0.0 copy-start
  0.7 1.2 %copy-done = bf16[32,64,256]{2,1,0:T(8,128)(2,1)S(1)} copy-done((bf16[32,64,256]{2,1,0:T(8,128)(2,1)S(1)}, bf16[32,64,256]{2,1,0:T(8,128)(2,1)}, u32[]{:S(2)}) %copy-start) | copy-done | bytes 1048600
  2.0 1.0 %pack_by_owner.1 = (bf16[528,256]{1,0:T(8,128)(2,1)S(1)}, bf16[528,256]{1,0:T(8,128)(2,1)S(1)}, bf16[544,256]{1,0:T(8,128)(2,1)S(1)}, bf16[512,256]{1,0:T(8,128)...) custom-call(s32[15,32]{1,0:T(8,128)S(1)} %pad_add_fusion.refs_0_, ...), custom_call_target="tpu_custom_call" | custom-call | bytes 6291456 | tf_op jit(solution)/shard_map/pack_by_owner/pallas_call | solution.py:96
  2.9 0.5 %collective-permute-start.6 = (bf16[528,256]{1,0:T(8,128)(2,1)S(1)}, bf16[528,256]{1,0:T(8,128)(2,1)S(1)}, u32[]{:S(2)}, u32[]{:S(2)}) collective-permute-start(bf16[528,256]{1,0:T(8,128)(2,1)S(1)} %get-tuple-element.41), channel_id=1, source_target_pairs={{0,1},{1,0},{2,3},{3,2},{4,5},{5,4},{6,7},{7,6},{8,9},{9,8},{10,11... | collective-permute-start | bytes 811016 | tf_op jit(solution)/shard_map/ppermute | solution.py:403
  3.5 3.5 %collective-permute-start = (bf16[544,256]{1,0:T(8,128)(2,1)S(1)}, bf16[544,256]{1,0:T(8,128)(2,1)S(1)}, u32[]{:S(2)}, u32[]{:S(2)}) collective-permute-start(bf16[544,256]{1,0:T(8,128)(2,1)S(1)} %get-tuple-element.31), channel_id=1, source_target_pairs={{0,6},{1,7},{2,4},{3,5},{4,2},{5,3},{6,0},{7,1},{8,14},{9,15},{10,... | collective-permute-start | bytes 835592 | tf_op jit(solution)/shard_map/ppermute | solution.py:403
  7.0 0.5 %collective-permute-start.2 = (bf16[544,256]{1,0:T(8,128)(2,1)S(1)}, bf16[544,256]{1,0:T(8,128)(2,1)S(1)}, u32[]{:S(2)}, u32[]{:S(2)}) collective-permute-start(bf16[544,256]{1,0:T(8,128)(2,1)S(1)} %get-tuple-element.34), channel_id=1, source_target_pairs={{0,2},{1,3},{2,0},{3,1},{4,6},{5,7},{6,4},{7,5},{8,10},{9,11},{10,... | collective-permute-start | bytes 835592 | tf_op jit(solution)/shard_map/ppermute | solution.py:403
  7.5 0.1 collective-permute-start.4
  7.6 0.0 collective-permute-done.6.refs_1_
  7.6 0.8 %fusion.5 = (bf16[1,128,256]{2,1,0:T(8,128)(2,1)S(1)}, bf16[128,256]{1,0:T(8,128)(2,1)S(1)}) fusion(bf16[64,256]{1,0:T(8,128)(2,1)} %bitcast.27, bf16[64,256]{1,0:T(8,128)(2,1)} %bitcast.28), kind=kLoop, calls=%fused_computation.23 | loop fusion | flops 131072 | bytes 196608 | tf_op jit(solution)/shard_map/broadcast_in_dim | solution.py:427
  8.4 2.0 %collective-permute-start.7 = (bf16[1,128,256]{2,1,0:T(8,128)(2,1)S(1)}, bf16[1,128,256]{2,1,0:T(8,128)(2,1)S(1)}, u32[]{:S(2)}, u32[]{:S(2)}) collective-permute-start(bf16[1,128,256]{2,1,0:T(8,128)(2,1)S(1)} %get-tuple-element.59), channel_id=1, source_target_pairs={{0,8},{8,0},{16,24},{24,16},{1,9},{9,1},{17,25},{25,17},{2,10},{10... | collective-permute-start | bytes 196616 | tf_op jit(solution)/shard_map/ppermute | solution.py:403
  10.4 0.8 %slice_bitcast_fusion.3 = (s32[4]{0:T(128)S(1)}, s32[4]{0:T(128)S(1)}) fusion(s32[4,2]{0,1:T(2,128)} %param.13), kind=kLoop, calls=%fused_computation.22 | loop fusion | bytes 64 | tf_op jit(solution)/shard_map/mul | solution.py:462
  11.2 1.5 %collective-permute-done.7 = bf16[1,128,256]{2,1,0:T(8,128)(2,1)S(1)} collective-permute-done((bf16[1,128,256]{2,1,0:T(8,128)(2,1)S(1)}, bf16[1,128,256]{2,1,0:T(8,128)(2,1)S(1)}, u32[]{:S(2)}, u32[]{:S(2)}) %collective-permute-start.7) | collective-permute-done | bytes 65568 | tf_op jit(solution)/shard_map/ppermute | solution.py:403
  12.8 3.1 %collective-permute-start.8 = (bf16[2,128,256]{2,1,0:T(8,128)(2,1)S(1)}, bf16[2,128,256]{2,1,0:T(8,128)(2,1)S(1)}, u32[]{:S(2)}, u32[]{:S(2)}) collective-permute-start(bf16[2,128,256]{2,1,0:T(8,128)(2,1)S(1)} %pad_maximum_fusion), channel_id=1, source_target_pairs={{0,16},{8,24},{16,0},{24,8},{1,17},{9,25},{17,1},{25,9},{2,18},{10... | collective-permute-start | bytes 393224 | tf_op jit(solution)/shard_map/ppermute | solution.py:403
  15.8 0.0 collective-permute-done.refs_2_
  15.8 0.6 %collective-permute-start.1 = (bf16[512,256]{1,0:T(8,128)(2,1)S(1)}, bf16[512,256]{1,0:T(8,128)(2,1)S(1)}, u32[]{:S(2)}, u32[]{:S(2)}) collective-permute-start(bf16[512,256]{1,0:T(8,128)(2,1)S(1)} %get-tuple-element.33), channel_id=1, source_target_pairs={{0,7},{1,6},{2,5},{3,4},{4,3},{5,2},{6,1},{7,0},{8,15},{9,14},{10,... | collective-permute-start | bytes 786440 | tf_op jit(solution)/shard_map/ppermute | solution.py:403
  16.4 4.6 %collective-permute-done.2.refs_3_ = bf16[544,256]{1,0:T(8,128)(2,1)S(1)} collective-permute-done((bf16[544,256]{1,0:T(8,128)(2,1)S(1)}, bf16[544,256]{1,0:T(8,128)(2,1)S(1)}, u32[]{:S(2)}, u32[]{:S(2)}) %collective-permute-start.2) | collective-permute-done | bytes 278560 | tf_op jit(solution)/shard_map/ppermute | solution.py:403
  21.0 0.3 collective-permute-start.3
  21.3 0.0 collective-permute-done.4.refs_4_
  21.3 1.4 %collective-permute-start.5 = (bf16[512,256]{1,0:T(8,128)(2,1)S(1)}, bf16[512,256]{1,0:T(8,128)(2,1)S(1)}, u32[]{:S(2)}, u32[]{:S(2)}) collective-permute-start(bf16[512,256]{1,0:T(8,128)(2,1)S(1)} %get-tuple-element.39), channel_id=1, source_target_pairs={{0,5},{1,4},{2,7},{3,6},{4,1},{5,0},{6,3},{7,2},{8,13},{9,12},{10,... | collective-permute-start | bytes 786440 | tf_op jit(solution)/shard_map/ppermute | solution.py:403
  22.7 0.0 collective-permute-start.9
  22.7 0.0 collective-permute-done.8
  22.7 6.0 %chi_of_early_payloads.1 = (f32[4,256,256]{2,1,0:T(8,128)S(1)}, bf16[1024,128]{1,0:T(8,128)(2,1)S(1)}) custom-call(bf16[528,256]{1,0:T(8,128)(2,1)S(1)} %get-tuple-element.40.refs_0_, bf16[528,256]{1,0:T(8,128)(2,1)S(1)} %collective-permute-done.6.refs_1_, bf16[544,256]{1,0:T(8,128)(2,1)S(1)} %collective-permute-done.refs_2_, ...), custom_call_target="tpu_custom_call" | custom-call | flops 1048576 | bytes 1024 | tf_op jit(solution)/shard_map/chi_of_early_payloads/pallas_call | solution.py:265
  28.7 0.0 collective-permute-done.9.lists
  28.7 1.8 %operators_of_late_payloads.1.refs_4_ = bf16[24,256,256]{2,1,0:T(8,128)(2,1)S(1)} custom-call(bf16[48,256]{1,0:T(8,128)(2,1)S(1)} %collective-permute-done.9.lists, bf16[1024,128]{1,0:T(8,128)(2,1)S(1)} %get-tuple-element.49.table), custom_call_target="tpu_custom_call" | custom-call | flops 1048576 | bytes 1024 | tf_op jit(solution)/shard_map/operators_of_late_payloads/pallas_call | solution.py:265
  30.5 0.0 collective-permute-done.1.refs_0_
  30.5 0.8 %collective-permute-done.3.refs_1_ = bf16[512,256]{1,0:T(8,128)(2,1)S(1)} collective-permute-done((bf16[512,256]{1,0:T(8,128)(2,1)S(1)}, bf16[512,256]{1,0:T(8,128)(2,1)S(1)}, u32[]{:S(2)}, u32[]{:S(2)}) %collective-permute-start.3) | collective-permute-done | bytes 262176 | tf_op jit(solution)/shard_map/ppermute | solution.py:403
  31.3 0.1 collective-permute-done.5.refs_2_
  31.4 1.9 %chi_of_late_payloads.1 = (f32[4,32,256]{2,1,0:T(8,128)S(1)}, f32[4,32,256]{2,1,0:T(8,128)S(1)}, f32[4,32,256]{2,1,0:T(8,128)S(1)}, bf16[8,32,256]{2,1,0:T(8,128...) custom-call(bf16[512,256]{1,0:T(8,128)(2,1)S(1)} %collective-permute-d, ...), custom_call_target="tpu_custom_call" | custom-call | flops 1048576 | bytes 1024 | tf_op jit(solution)/shard_map/chi_of_late_payloads/pallas_call | solution.py:265
  33.3 1.9 %collective-permute-start.10 = (bf16[8,32,256]{2,1,0:T(8,128)(2,1)S(1)}, bf16[8,32,256]{2,1,0:T(8,128)(2,1)S(1)}, u32[]{:S(2)}, u32[]{:S(2)}) collective-permute-start(bf16[8,32,256]{2,1,0:T(8,128)(2,1)S(1)} %get-tuple-element.51), channel_id=1, source_target_pairs={{0,8},{8,0},{16,24},{24,16},{1,9},{9,1},{17,25},{25,17},{2,10},{10... | collective-permute-start | bytes 393224 | tf_op jit(solution)/shard_map/ppermute | solution.py:403
  35.1 0.1 fusion.4
  35.2 2.7 %collective-permute-start.12 = (bf16[4,32,256]{2,1,0:T(8,128)(2,1)S(1)}, bf16[4,32,256]{2,1,0:T(8,128)(2,1)S(1)}, u32[]{:S(2)}, u32[]{:S(2)}) collective-permute-start(bf16[4,32,256]{2,1,0:T(8,128)(2,1)S(1)} %get-tuple-element.54), channel_id=1, source_target_pairs={{0,16},{8,24},{16,0},{24,8},{1,17},{9,25},{17,1},{25,9},{2,18},{10... | collective-permute-start | bytes 196616 | tf_op jit(solution)/shard_map/ppermute | solution.py:403
  37.9 0.0 collective-permute-start.13
  37.9 0.9 %collective-permute-start.14 = (bf16[4,32,256]{2,1,0:T(8,128)(2,1)S(1)}, bf16[4,32,256]{2,1,0:T(8,128)(2,1)S(1)}, u32[]{:S(2)}, u32[]{:S(2)}) collective-permute-start(bf16[4,32,256]{2,1,0:T(8,128)(2,1)S(1)} %get-tuple-element.56), channel_id=1, source_target_pairs={{0,8},{8,0},{16,24},{24,16},{1,9},{9,1},{17,25},{25,17},{2,10},{10... | collective-permute-start | bytes 196616 | tf_op jit(solution)/shard_map/ppermute | solution.py:403
  38.8 0.9 %collective-permute-done.10.refs_2_ = bf16[8,32,256]{2,1,0:T(8,128)(2,1)S(1)} collective-permute-done((bf16[8,32,256]{2,1,0:T(8,128)(2,1)S(1)}, bf16[8,32,256]{2,1,0:T(8,128)(2,1)S(1)}, u32[]{:S(2)}, u32[]{:S(2)}) %collective-permute-start.10) | collective-permute-done | bytes 131104 | tf_op jit(solution)/shard_map/ppermute | solution.py:403
  39.7 2.8 %collective-permute-start.11 = (bf16[4,32,256]{2,1,0:T(8,128)(2,1)S(1)}, bf16[4,32,256]{2,1,0:T(8,128)(2,1)S(1)}, u32[]{:S(2)}, u32[]{:S(2)}) collective-permute-start(bf16[4,32,256]{2,1,0:T(8,128)(2,1)S(1)} %add_convert_fusion), channel_id=1, source_target_pairs={{0,16},{8,24},{16,0},{24,8},{1,17},{9,25},{17,1},{25,9},{2,18},{10... | collective-permute-start | bytes 196616 | tf_op jit(solution)/shard_map/ppermute | solution.py:403
  42.4 0.1 pad_maximum_fusion.3.phases.refs_0_
  42.5 0.0 collective-permute-done.12.rest_0_
  42.5 2.2 %collective-permute-done.13.rest_1_ = bf16[4,32,256]{2,1,0:T(8,128)(2,1)S(1)} collective-permute-done((bf16[4,32,256]{2,1,0:T(8,128)(2,1)S(1)}, bf16[4,32,256]{2,1,0:T(8,128)(2,1)S(1)}, u32[]{:S(2)}, u32[]{:S(2)}) %collective-permute-start.13) | collective-permute-done | bytes 65568 | tf_op jit(solution)/shard_map/ppermute | solution.py:403
  44.7 0.0 collective-permute-done.14.rest_2_
  44.7 2.8 %to_k_points.2.refs_4_ = f32[128,64,256]{2,1,0:T(8,128)} custom-call(f32[4,128]{1,0:T(4,128)S(1)} %pad_maximum_fusion.3.phases.refs_0_, f32[4,32,256]{2,1,0:T(8,128)S(1)} %get-tuple-element.53.own, bf16[4,32,256]{2,1,0:T(8,128)(2,1)S(1)} %collective-permute-done.12.rest_0_, bf16[4,32,256]{2,1,0:T(8,128)(2,1)S(1)} %collective-permute-done.13.rest_1_, ...), custom_call_target="tpu_custom_call" | custom-call | flops 8388608 | bytes 4194304 | tf_op jit(solution)/shard_map/to_k_points/pallas_call | solution.py:380
  47.5 0.0 collective-permute-done.11.refs_3_
  47.5 2.8 %to_k_points.3 = f32[128,64,256]{2,1,0:T(8,128)} custom-call(f32[4,128]{1,0:T(4,128)S(1)} %pad_maximum_fusion.3.phases.refs_0_, f32[4,32,256]{2,1,0:T(8,128)S(1)} %get-tuple-element.50.refs_1_, bf16[8,32,256]{2,1,0:T(8,128)(2,1)S(1)} %collective-permute-done.10.refs_2_, ...), custom_call_target="tpu_custom_call", output_to_operand_aliasing={{}: (4, {})} | custom-call | flops 8388608 | bytes 4194304 | tf_op jit(solution)/shard_map/to_k_points/pallas_call | solution.py:380
  (8 shorter events, 0.1 us)
Async XLA Ops:
  0.7 1.2 %copy-start = (bf16[32,64,256]{2,1,0:T(8,128)(2,1)S(1)}, bf16[32,64,256]{2,1,0:T(8,128)(2,1)}, u32[]{:S(2)}) copy-start(bf16[32,64,256]{2,1,0:T(8,128)(2,1)} %refs_1_.1) | copy-start | bytes 3145732
  2.9 4.7 %collective-permute-start.6 = (bf16[528,256]{1,0:T(8,128)(2,1)S(1)}, bf16[528,256]{1,0:T(8,128)(2,1)S(1)}, u32[]{:S(2)}, u32[]{:S(2)}) collective-permute-start(bf16[528,256]{1,0:T(8,128)(2,1)S(1)} %get-tuple-element.41), channel_id=1, source_target_pairs={{0,1},{1,0},{2,3},{3,2},{4,5},{5,4},{6,7},{7,6},{8,9},{9,8},{10,11... | collective-permute-start | bytes 811016 | tf_op jit(solution)/shard_map/ppermute | solution.py:403
  3.5 12.4 %collective-permute-start = (bf16[544,256]{1,0:T(8,128)(2,1)S(1)}, bf16[544,256]{1,0:T(8,128)(2,1)S(1)}, u32[]{:S(2)}, u32[]{:S(2)}) collective-permute-start(bf16[544,256]{1,0:T(8,128)(2,1)S(1)} %get-tuple-element.31), channel_id=1, source_target_pairs={{0,6},{1,7},{2,4},{3,5},{4,2},{5,3},{6,0},{7,1},{8,14},{9,15},{10,... | collective-permute-start | bytes 835592 | tf_op jit(solution)/shard_map/ppermute | solution.py:403
  7.0 14.0 %collective-permute-start.2 = (bf16[544,256]{1,0:T(8,128)(2,1)S(1)}, bf16[544,256]{1,0:T(8,128)(2,1)S(1)}, u32[]{:S(2)}, u32[]{:S(2)}) collective-permute-start(bf16[544,256]{1,0:T(8,128)(2,1)S(1)} %get-tuple-element.34), channel_id=1, source_target_pairs={{0,2},{1,3},{2,0},{3,1},{4,6},{5,7},{6,4},{7,5},{8,10},{9,11},{10,... | collective-permute-start | bytes 835592 | tf_op jit(solution)/shard_map/ppermute | solution.py:403
  7.5 13.8 %collective-permute-start.4 = (bf16[544,256]{1,0:T(8,128)(2,1)S(1)}, bf16[544,256]{1,0:T(8,128)(2,1)S(1)}, u32[]{:S(2)}, u32[]{:S(2)}) collective-permute-start(bf16[544,256]{1,0:T(8,128)(2,1)S(1)} %get-tuple-element.37), channel_id=1, source_target_pairs={{0,4},{1,5},{2,6},{3,7},{4,0},{5,1},{6,2},{7,3},{8,12},{9,13},{10,... | collective-permute-start | bytes 835592 | tf_op jit(solution)/shard_map/ppermute | solution.py:403
  8.4 4.3 %collective-permute-start.7 = (bf16[1,128,256]{2,1,0:T(8,128)(2,1)S(1)}, bf16[1,128,256]{2,1,0:T(8,128)(2,1)S(1)}, u32[]{:S(2)}, u32[]{:S(2)}) collective-permute-start(bf16[1,128,256]{2,1,0:T(8,128)(2,1)S(1)} %get-tuple-element.59), channel_id=1, source_target_pairs={{0,8},{8,0},{16,24},{24,16},{1,9},{9,1},{17,25},{25,17},{2,10},{10... | collective-permute-start | bytes 196616 | tf_op jit(solution)/shard_map/ppermute | solution.py:403
  12.8 9.9 %collective-permute-start.8 = (bf16[2,128,256]{2,1,0:T(8,128)(2,1)S(1)}, bf16[2,128,256]{2,1,0:T(8,128)(2,1)S(1)}, u32[]{:S(2)}, u32[]{:S(2)}) collective-permute-start(bf16[2,128,256]{2,1,0:T(8,128)(2,1)S(1)} %pad_maximum_fusion), channel_id=1, source_target_pairs={{0,16},{8,24},{16,0},{24,8},{1,17},{9,25},{17,1},{25,9},{2,18},{10... | collective-permute-start | bytes 393224 | tf_op jit(solution)/shard_map/ppermute | solution.py:403
  15.8 14.7 %collective-permute-start.1 = (bf16[512,256]{1,0:T(8,128)(2,1)S(1)}, bf16[512,256]{1,0:T(8,128)(2,1)S(1)}, u32[]{:S(2)}, u32[]{:S(2)}) collective-permute-start(bf16[512,256]{1,0:T(8,128)(2,1)S(1)} %get-tuple-element.33), channel_id=1, source_target_pairs={{0,7},{1,6},{2,5},{3,4},{4,3},{5,2},{6,1},{7,0},{8,15},{9,14},{10,... | collective-permute-start | bytes 786440 | tf_op jit(solution)/shard_map/ppermute | solution.py:403
  21.0 10.3 %collective-permute-start.3 = (bf16[512,256]{1,0:T(8,128)(2,1)S(1)}, bf16[512,256]{1,0:T(8,128)(2,1)S(1)}, u32[]{:S(2)}, u32[]{:S(2)}) collective-permute-start(bf16[512,256]{1,0:T(8,128)(2,1)S(1)} %get-tuple-element.36), channel_id=1, source_target_pairs={{0,3},{1,2},{2,1},{3,0},{4,7},{5,6},{6,5},{7,4},{8,11},{9,10},{10,... | collective-permute-start | bytes 786440 | tf_op jit(solution)/shard_map/ppermute | solution.py:403
  21.3 10.1 %collective-permute-start.5 = (bf16[512,256]{1,0:T(8,128)(2,1)S(1)}, bf16[512,256]{1,0:T(8,128)(2,1)S(1)}, u32[]{:S(2)}, u32[]{:S(2)}) collective-permute-start(bf16[512,256]{1,0:T(8,128)(2,1)S(1)} %get-tuple-element.39), channel_id=1, source_target_pairs={{0,5},{1,4},{2,7},{3,6},{4,1},{5,0},{6,3},{7,2},{8,13},{9,12},{10,... | collective-permute-start | bytes 786440 | tf_op jit(solution)/shard_map/ppermute | solution.py:403
  22.7 6.0 %collective-permute-start.9 = (bf16[48,256]{1,0:T(8,128)(2,1)S(1)}, bf16[48,256]{1,0:T(8,128)(2,1)S(1)}, u32[]{:S(2)}, u32[]{:S(2)}) collective-permute-start(bf16[48,256]{1,0:T(8,128)(2,1)S(1)} %pad_maximum_fusion.2), channel_id=1, source_target_pairs={{0,1},{1,0},{2,3},{3,2},{4,5},{5,4},{6,7},{7,6},{8,9},{9,8},{10,11... | collective-permute-start | bytes 73736 | tf_op jit(solution)/shard_map/ppermute | solution.py:403
  33.3 6.4 %collective-permute-start.10 = (bf16[8,32,256]{2,1,0:T(8,128)(2,1)S(1)}, bf16[8,32,256]{2,1,0:T(8,128)(2,1)S(1)}, u32[]{:S(2)}, u32[]{:S(2)}) collective-permute-start(bf16[8,32,256]{2,1,0:T(8,128)(2,1)S(1)} %get-tuple-element.51), channel_id=1, source_target_pairs={{0,8},{8,0},{16,24},{24,16},{1,9},{9,1},{17,25},{25,17},{2,10},{10... | collective-permute-start | bytes 393224 | tf_op jit(solution)/shard_map/ppermute | solution.py:403
  35.2 7.3 %collective-permute-start.12 = (bf16[4,32,256]{2,1,0:T(8,128)(2,1)S(1)}, bf16[4,32,256]{2,1,0:T(8,128)(2,1)S(1)}, u32[]{:S(2)}, u32[]{:S(2)}) collective-permute-start(bf16[4,32,256]{2,1,0:T(8,128)(2,1)S(1)} %get-tuple-element.54), channel_id=1, source_target_pairs={{0,16},{8,24},{16,0},{24,8},{1,17},{9,25},{17,1},{25,9},{2,18},{10... | collective-permute-start | bytes 196616 | tf_op jit(solution)/shard_map/ppermute | solution.py:403
  37.9 6.8 %collective-permute-start.13 = (bf16[4,32,256]{2,1,0:T(8,128)(2,1)S(1)}, bf16[4,32,256]{2,1,0:T(8,128)(2,1)S(1)}, u32[]{:S(2)}, u32[]{:S(2)}) collective-permute-start(bf16[4,32,256]{2,1,0:T(8,128)(2,1)S(1)} %get-tuple-element.55), channel_id=1, source_target_pairs={{0,24},{8,16},{16,8},{24,0},{1,25},{9,17},{17,9},{25,1},{2,26},{10... | collective-permute-start | bytes 196616 | tf_op jit(solution)/shard_map/ppermute | solution.py:403
  37.9 6.8 %collective-permute-start.14 = (bf16[4,32,256]{2,1,0:T(8,128)(2,1)S(1)}, bf16[4,32,256]{2,1,0:T(8,128)(2,1)S(1)}, u32[]{:S(2)}, u32[]{:S(2)}) collective-permute-start(bf16[4,32,256]{2,1,0:T(8,128)(2,1)S(1)} %get-tuple-element.56), channel_id=1, source_target_pairs={{0,8},{8,0},{16,24},{24,16},{1,9},{9,1},{17,25},{25,17},{2,10},{10... | collective-permute-start | bytes 196616 | tf_op jit(solution)/shard_map/ppermute | solution.py:403
  39.7 7.9 %collective-permute-start.11 = (bf16[4,32,256]{2,1,0:T(8,128)(2,1)S(1)}, bf16[4,32,256]{2,1,0:T(8,128)(2,1)S(1)}, u32[]{:S(2)}, u32[]{:S(2)}) collective-permute-start(bf16[4,32,256]{2,1,0:T(8,128)(2,1)S(1)} %add_convert_fusion), channel_id=1, source_target_pairs={{0,16},{8,24},{16,0},{24,8},{1,17},{9,25},{17,1},{25,9},{2,18},{10... | collective-permute-start | bytes 196616 | tf_op jit(solution)/shard_map/ppermute | solution.py:403

commit v5 on v4

--- a/solution.py
+++ b/solution.py
@@ -10,6 +10,7 @@
 
 KGRID = 8
 PART = 5
+DIRECT_ROWS = 32
 QUAD = 4
 LIST_ROWS = 16
 BF16 = jnp.bfloat16
@@ -29,10 +30,8 @@
     )
 
 
-def lists_with(k):
-    if k < 2:
-        return [k]
-    return [k, k ^ 1] if k % 2 == 0 else []
+def list_height(k):
+    return LIST_ROWS if k < 2 or k % 2 == 0 else 0
 
 
 def pack_kernel(n, cap, pairs, *refs):
@@ -57,7 +56,9 @@
     )
     before = (as_column == distance) & (iota((rows, rows), 0) < iota((rows, rows), 1))
     rank = jnp.sum(before.astype(jnp.int32), axis=0, keepdims=True)
-    chosen = iota((n * LIST_ROWS, rows), 0) == distance * LIST_ROWS + rank
+    odd = jnp.where(distance < 2, 0, distance % 2)
+    place_of = (distance - odd) * LIST_ROWS + odd * 8 + rank
+    chosen = iota((n * LIST_ROWS, rows), 0) == place_of
     table[0 : ints.shape[0], :] = ints[...].astype(F32)
     table[ints.shape[0] - pairs : ints.shape[0], :] += 1.0
     ordered = dot(chosen.astype(BF16), table[...].astype(BF16), (1, 1))
@@ -75,9 +76,8 @@
     for k in range(n):
         for r in range(cap):
             outs[k][r * square : (r + 1) * square, :] = blocks[place[k * cap + r]]
-        for i, of in enumerate(lists_with(k)):
-            at = cap * square + i * LIST_ROWS
-            outs[k][at : at + LIST_ROWS, :] = lists[of * LIST_ROWS : (of + 1) * LIST_ROWS, :]
+        if list_height(k) > 0:
+            outs[k][cap * square :, :] = lists[k * LIST_ROWS : (k + 1) * LIST_ROWS, :]
 
 
 def pack(n, cap, blocks, block_owner, block_basis, pair_images, pair_cell):
@@ -92,7 +92,7 @@
         ],
         axis=0,
     )
-    heights = [cap * square + len(lists_with(k)) * LIST_ROWS for k in range(n)]
+    heights = [cap * square + list_height(k) for k in range(n)]
     return pl.pallas_call(
         functools.partial(pack_kernel, n, cap, pairs),
         out_shape=[jax.ShapeDtypeStruct((height, width), BF16) for height in heights],
@@ -116,12 +116,17 @@
     return images == 4
 
 
+def row_parts(images, share):
+    if by_halving(images):
+        return [(0, DIRECT_ROWS), (DIRECT_ROWS, share - DIRECT_ROWS)]
+    return [(0, share)]
+
+
 def shares_of(images):
-    kept = [(part, [0], F32) for part in range(2)]
-    if by_halving(images):
-        kept += [(1, [2], F32), (1, [1, 3], BF16)]
-        return kept + [(0, [k], BF16) for k in (2, 3, 1)]
-    return kept + [(part, [k], BF16) for part in range(2) for k in range(1, images)]
+    if not by_halving(images):
+        return [(0, [0], F32)] + [(0, [k], BF16) for k in range(1, images)]
+    kept = [(0, [0], F32), (1, [0], F32), (1, [2], F32), (1, [1, 3], BF16)]
+    return kept + [(0, [k], BF16) for k in (2, 3, 1)]
 
 
 def diagonals(cap, pairs, cell_count, side, lists, table):
@@ -133,7 +138,7 @@
     height = 8 * len(lists)
     lane = iota((1, lanes), 1)
     listing = jnp.concatenate(
-        [ref[at : at + LIST_ROWS, 0:128].astype(F32)[0:8] for ref, at in lists], axis=0
+        [ref[at : at + LIST_ROWS, 0:128].astype(F32)[i : i + 8] for ref, at, i in lists], axis=0
     )
 
     def columns(start):
@@ -207,7 +212,7 @@
         before = None
     else:
         before, table, total, mixed, stacked = refs
-    lists = [(p, cap * square) for p in payloads]
+    lists = [(p, cap * square, 0) for p in payloads]
     made = diagonals(cap, pairs, cell_count, math.isqrt(square), lists, table)
     add_blocks(cap, square, payloads, made, before, total, mixed, stacked)
 
@@ -228,7 +233,7 @@
 
 
 def operators_kernel(count, cap, pairs, cell_count, square, lists, table, out):
-    places = [(lists, i * LIST_ROWS) for i in range(count)]
+    places = [(lists, i * LIST_ROWS, 8) for i in range(count)]
     made = diagonals(cap, pairs, cell_count, math.isqrt(square), places, table)
     for i, operators in enumerate(made):
         for c in range(cell_count):
@@ -249,11 +254,13 @@
     add_blocks(cap, square, payloads, made, before, total, mixed, stacked)
     if last:
         z = lax.axis_index("image")
-        half = outs[0].shape[1]
+        share = total.shape[1] // images
+        parts = row_parts(images, share)
         for ref, (part, distances, _) in zip(outs, shares_of(images)):
+            start, rows = parts[part]
             for i, k in enumerate(distances):
-                at = pl.multiple_of((z ^ k) * (2 * half) + part * half, half)
-                taken = total[:, pl.ds(at, half), :].astype(ref.dtype)
+                at = pl.multiple_of((z ^ k) * share + start, 16)
+                taken = total[:, pl.ds(at, rows), :].astype(ref.dtype)
                 if len(distances) == 1:
                     ref[...] = taken
                 else:
@@ -313,10 +320,10 @@
     scratch = chi_scratch(cell_count, width, count * cap * square)
     out_shape = [jax.ShapeDtypeStruct(full, F32)]
     if last:
-        half = width // images // 2
+        parts = row_parts(images, width // images)
         out_shape = [
-            jax.ShapeDtypeStruct((len(distances) * cell_count, half, width), dtype)
-            for _, distances, dtype in shares_of(images)
+            jax.ShapeDtypeStruct((len(distances) * cell_count, parts[part][1], width), dtype)
+            for part, distances, dtype in shares_of(images)
         ]
         scratch = [pltpu.VMEM(full, F32)] + scratch
     return on_chip(
@@ -421,7 +428,7 @@
     payload[1], dens_occ, dens_virt = lax.optimization_barrier(
         (swap(packed[1], "ri", 1), dens_occ, dens_virt)
     )
-    lists = [payload[k][cap * square + LIST_ROWS :] for k in evens]
+    lists = [payload[k][cap * square :] for k in evens]
     lists = swap(jnp.concatenate(lists, axis=0), "ri", 1)
     density = jnp.concatenate([dens_occ[0].T, dens_virt[0].T], axis=0)
     pieces = density[None]
@@ -446,16 +453,16 @@
         last = at + PART >= len(odds)
         out = late_part(cap, cell_count, square, images, chosen, chi, operators, last)
         chi = out[0]
-    halves, sends = [[own] for own in out[:2]], out[2:]
-    plan = shares_of(images)[2:]
+    plan = shares_of(images)
+    parts = [[x] for x, (_, distances, _) in zip(out, plan) if distances == [0]]
+    given = dict(zip([(part, distances[0]) for part, distances, _ in plan], out))
+    for part, distances, dtype in plan:
+        if dtype == BF16:
+            k = distances[0]
+            parts[part].append(swap(given[part, k], "image", k))
     if by_halving(images):
-        forward, sends, plan = sends[0], sends[1:], plan[1:]
-    received = [swap(x, "image", d[0]) for x, (_, d, _) in zip(sends, plan)]
-    for x, (part, _, _) in zip(received, plan):
-        halves[part].append(x)
-    if by_halving(images):
-        forward = (forward + received[0][cell_count:].astype(F32)).astype(BF16)
-        halves[1].append(swap(forward, "image", 2))
+        forward = parts[1][1][cell_count:].astype(F32) + given[1, 2]
+        parts[1].append(swap(forward.astype(BF16), "image", 2))
 
     points = jnp.arange(KGRID * KGRID, dtype=jnp.int32)
     wrapped = (
@@ -464,9 +471,10 @@
     angles = 2.0 * math.pi / KGRID * wrapped.astype(F32)
     phases = jnp.concatenate([jnp.cos(angles), jnp.sin(angles)], axis=1)
     result = None
-    share = 2 * halves[0][0].shape[1]
-    for part, (own, *received) in enumerate(halves):
-        result = transform(phases, own, received, part * share // 2, share, result)
+    share = blocks.shape[2] // images
+    places = list(zip(row_parts(images, share), parts))
+    for (row_at, _), (own, *received) in places:
+        result = transform(phases, own, received, row_at, share, result)
     return result.reshape((2, KGRID * KGRID, 1) + result.shape[1:])
 
 

time: 50.6 us -> 50.3 us (level)
  transfers between devices with their start and end apart: 15 -> 15, of which waited for: 6 -> 5; matrix products, arithmetic and copies ran while one was open for 4% -> 4% of each run, Pallas kernels for 21% -> 21%
where the time goes in v5:
time: 50.3 us; the launch traced here: 50 us
  starting transfers between devices  20 us (40%)
  Pallas kernels  16.2 us (32%)
  waiting for transfers between devices  9.85 us (20%)
  local copies, waits for them, and re-layouts  1.99 us (4%)
  other arithmetic  1.74 us (3%)
    ppermute x15, starting transfers between devices, swap(): return lax.ppermute(array, axis, [(i, i ^ k) for i in range(size)])  20 us
    ppermute x15, waiting for transfers between devices, swap(): return lax.ppermute(array, axis, [(i, i ^ k) for i in range(size)])  9.85 us
    pallas_call x3, Pallas kernels, on_chip(): pl.pallas_call(kernel, out_shape=out_shape, in_specs=[vmem] * len(args),...  9.68 us
    pallas_call x2, Pallas kernels, transform(): pl.pallas_call(kernel, out_shape=jax.ShapeDtypeStruct((points, share, wid...  5.59 us
    unnamed x2, local copies, waits for them, and re-layouts  1.22 us
  transfers between devices with their start and end apart: 15, of which 5 were waited for; matrix products, arithmetic and copies ran while one was open for 4% of the time, Pallas kernels for 21%

profile of v5, /device:TPU:0, one launch (start us, length us, event | category | flops | bytes accessed | tf_op | source)
XLA Modules:
  0.0 50.0 jit_solution(3140100841752968126)
XLA Ops:
  0.0 0.7 %pad_add_fusion.refs_0_ = s32[15,32]{1,0:T(8,128)S(1)} fusion(s32[4,32]{1,0:T(4,128)} %bitcast.30, s32[8,32]{1,0:T(8,128)} %bitcast.29, s32[2,32]{1,0:T(2,128)} %bitcast.31, s32[1,32]{1,0:T(1,128)} %bitcast.32), kind=kLoop, calls=%fused_computation.6 | loop fusion | flops 1440 | bytes 3840 | tf_op jit(solution)/shard_map/concatenate | solution.py:86
  0.7 0.0 copy-start
  0.7 1.2 %copy-done = bf16[32,64,256]{2,1,0:T(8,128)(2,1)S(1)} copy-done((bf16[32,64,256]{2,1,0:T(8,128)(2,1)S(1)}, bf16[32,64,256]{2,1,0:T(8,128)(2,1)}, u32[]{:S(2)}) %copy-start) | copy-done | bytes 1048600
  2.0 1.0 %pack_by_owner.1 = (bf16[528,256]{1,0:T(8,128)(2,1)S(1)}, bf16[528,256]{1,0:T(8,128)(2,1)S(1)}, bf16[528,256]{1,0:T(8,128)(2,1)S(1)}, bf16[512,256]{1,0:T(8,128)...) custom-call(s32[15,32]{1,0:T(8,128)S(1)} %pad_add_fusion.refs_0_, ...), custom_call_target="tpu_custom_call" | custom-call | bytes 6291456 | tf_op jit(solution)/shard_map/pack_by_owner/pallas_call | solution.py:96
  2.9 0.5 %collective-permute-start.6 = (bf16[528,256]{1,0:T(8,128)(2,1)S(1)}, bf16[528,256]{1,0:T(8,128)(2,1)S(1)}, u32[]{:S(2)}, u32[]{:S(2)}) collective-permute-start(bf16[528,256]{1,0:T(8,128)(2,1)S(1)} %get-tuple-element.41), channel_id=1, source_target_pairs={{0,1},{1,0},{2,3},{3,2},{4,5},{5,4},{6,7},{7,6},{8,9},{9,8},{10,11... | collective-permute-start | bytes 811016 | tf_op jit(solution)/shard_map/ppermute | solution.py:410
  3.4 3.5 %collective-permute-start = (bf16[528,256]{1,0:T(8,128)(2,1)S(1)}, bf16[528,256]{1,0:T(8,128)(2,1)S(1)}, u32[]{:S(2)}, u32[]{:S(2)}) collective-permute-start(bf16[528,256]{1,0:T(8,128)(2,1)S(1)} %get-tuple-element.31), channel_id=1, source_target_pairs={{0,6},{1,7},{2,4},{3,5},{4,2},{5,3},{6,0},{7,1},{8,14},{9,15},{10,... | collective-permute-start | bytes 811016 | tf_op jit(solution)/shard_map/ppermute | solution.py:410
  7.0 0.5 %collective-permute-start.2 = (bf16[528,256]{1,0:T(8,128)(2,1)S(1)}, bf16[528,256]{1,0:T(8,128)(2,1)S(1)}, u32[]{:S(2)}, u32[]{:S(2)}) collective-permute-start(bf16[528,256]{1,0:T(8,128)(2,1)S(1)} %get-tuple-element.34), channel_id=1, source_target_pairs={{0,2},{1,3},{2,0},{3,1},{4,6},{5,7},{6,4},{7,5},{8,10},{9,11},{10,... | collective-permute-start | bytes 811016 | tf_op jit(solution)/shard_map/ppermute | solution.py:410
  7.5 0.1 collective-permute-start.4
  7.6 0.0 collective-permute-done.6.refs_1_
  7.6 0.8 %fusion.5 = (bf16[1,128,256]{2,1,0:T(8,128)(2,1)S(1)}, bf16[128,256]{1,0:T(8,128)(2,1)S(1)}) fusion(bf16[64,256]{1,0:T(8,128)(2,1)} %bitcast.27, bf16[64,256]{1,0:T(8,128)(2,1)} %bitcast.28), kind=kLoop, calls=%fused_computation.23 | loop fusion | flops 131072 | bytes 196608 | tf_op jit(solution)/shard_map/broadcast_in_dim | solution.py:434
  8.4 2.0 %collective-permute-start.7 = (bf16[1,128,256]{2,1,0:T(8,128)(2,1)S(1)}, bf16[1,128,256]{2,1,0:T(8,128)(2,1)S(1)}, u32[]{:S(2)}, u32[]{:S(2)}) collective-permute-start(bf16[1,128,256]{2,1,0:T(8,128)(2,1)S(1)} %get-tuple-element.59), channel_id=1, source_target_pairs={{0,8},{8,0},{16,24},{24,16},{1,9},{9,1},{17,25},{25,17},{2,10},{10... | collective-permute-start | bytes 196616 | tf_op jit(solution)/shard_map/ppermute | solution.py:410
  10.4 0.8 %slice_bitcast_fusion.3 = (s32[4]{0:T(128)S(1)}, s32[4]{0:T(128)S(1)}) fusion(s32[4,2]{0,1:T(2,128)} %param.13), kind=kLoop, calls=%fused_computation.22 | loop fusion | bytes 64 | tf_op jit(solution)/shard_map/mul | solution.py:469
  11.2 1.5 %collective-permute-done.7 = bf16[1,128,256]{2,1,0:T(8,128)(2,1)S(1)} collective-permute-done((bf16[1,128,256]{2,1,0:T(8,128)(2,1)S(1)}, bf16[1,128,256]{2,1,0:T(8,128)(2,1)S(1)}, u32[]{:S(2)}, u32[]{:S(2)}) %collective-permute-start.7) | collective-permute-done | bytes 65568 | tf_op jit(solution)/shard_map/ppermute | solution.py:410
  12.8 3.1 %collective-permute-start.8 = (bf16[2,128,256]{2,1,0:T(8,128)(2,1)S(1)}, bf16[2,128,256]{2,1,0:T(8,128)(2,1)S(1)}, u32[]{:S(2)}, u32[]{:S(2)}) collective-permute-start(bf16[2,128,256]{2,1,0:T(8,128)(2,1)S(1)} %pad_maximum_fusion), channel_id=1, source_target_pairs={{0,16},{8,24},{16,0},{24,8},{1,17},{9,25},{17,1},{25,9},{2,18},{10... | collective-permute-start | bytes 393224 | tf_op jit(solution)/shard_map/ppermute | solution.py:410
  15.8 0.0 collective-permute-done.refs_2_
  15.8 0.6 %collective-permute-start.1 = (bf16[512,256]{1,0:T(8,128)(2,1)S(1)}, bf16[512,256]{1,0:T(8,128)(2,1)S(1)}, u32[]{:S(2)}, u32[]{:S(2)}) collective-permute-start(bf16[512,256]{1,0:T(8,128)(2,1)S(1)} %get-tuple-element.33), channel_id=1, source_target_pairs={{0,7},{1,6},{2,5},{3,4},{4,3},{5,2},{6,1},{7,0},{8,15},{9,14},{10,... | collective-permute-start | bytes 786440 | tf_op jit(solution)/shard_map/ppermute | solution.py:410
  16.4 4.0 %collective-permute-done.2.refs_3_ = bf16[528,256]{1,0:T(8,128)(2,1)S(1)} collective-permute-done((bf16[528,256]{1,0:T(8,128)(2,1)S(1)}, bf16[528,256]{1,0:T(8,128)(2,1)S(1)}, u32[]{:S(2)}, u32[]{:S(2)}) %collective-permute-start.2) | collective-permute-done | bytes 270368 | tf_op jit(solution)/shard_map/ppermute | solution.py:410
  20.4 0.5 collective-permute-start.3
  20.9 0.0 collective-permute-done.4.refs_4_
  20.9 1.2 %collective-permute-start.5 = (bf16[512,256]{1,0:T(8,128)(2,1)S(1)}, bf16[512,256]{1,0:T(8,128)(2,1)S(1)}, u32[]{:S(2)}, u32[]{:S(2)}) collective-permute-start(bf16[512,256]{1,0:T(8,128)(2,1)S(1)} %get-tuple-element.39), channel_id=1, source_target_pairs={{0,5},{1,4},{2,7},{3,6},{4,1},{5,0},{6,3},{7,2},{8,13},{9,12},{10,... | collective-permute-start | bytes 786440 | tf_op jit(solution)/shard_map/ppermute | solution.py:410
  22.1 0.0 collective-permute-start.9
  22.1 0.0 collective-permute-done.8
  22.2 6.0 %chi_of_early_payloads.1 = (f32[4,256,256]{2,1,0:T(8,128)S(1)}, bf16[1024,128]{1,0:T(8,128)(2,1)S(1)}) custom-call(bf16[528,256]{1,0:T(8,128)(2,1)S(1)} %get-tuple-element.40.refs_0_, bf16[528,256]{1,0:T(8,128)(2,1)S(1)} %collective-permute-done.6.refs_1_, bf16[528,256]{1,0:T(8,128)(2,1)S(1)} %collective-permute-done.refs_2_, ...), custom_call_target="tpu_custom_call" | custom-call | flops 1048576 | bytes 1024 | tf_op jit(solution)/shard_map/chi_of_early_payloads/pallas_call | solution.py:272
  28.2 0.0 collective-permute-done.9.lists
  28.2 1.8 %operators_of_late_payloads.1.refs_4_ = bf16[24,256,256]{2,1,0:T(8,128)(2,1)S(1)} custom-call(bf16[48,256]{1,0:T(8,128)(2,1)S(1)} %collective-permute-done.9.lists, bf16[1024,128]{1,0:T(8,128)(2,1)S(1)} %get-tuple-element.49.table), custom_call_target="tpu_custom_call" | custom-call | flops 1048576 | bytes 1024 | tf_op jit(solution)/shard_map/operators_of_late_payloads/pallas_call | solution.py:272
  30.0 0.0 collective-permute-done.1.refs_0_
  30.0 1.2 %collective-permute-done.3.refs_1_ = bf16[512,256]{1,0:T(8,128)(2,1)S(1)} collective-permute-done((bf16[512,256]{1,0:T(8,128)(2,1)S(1)}, bf16[512,256]{1,0:T(8,128)(2,1)S(1)}, u32[]{:S(2)}, u32[]{:S(2)}) %collective-permute-start.3) | collective-permute-done | bytes 262176 | tf_op jit(solution)/shard_map/ppermute | solution.py:410
  31.2 0.0 collective-permute-done.5.refs_2_
  31.2 1.9 %chi_of_late_payloads.1 = (f32[4,32,256]{2,1,0:T(8,128)S(1)}, f32[4,32,256]{2,1,0:T(8,128)S(1)}, f32[4,32,256]{2,1,0:T(8,128)S(1)}, bf16[8,32,256]{2,1,0:T(8,128...) custom-call(bf16[512,256]{1,0:T(8,128)(2,1)S(1)} %collective-permute-d, ...), custom_call_target="tpu_custom_call" | custom-call | flops 1048576 | bytes 1024 | tf_op jit(solution)/shard_map/chi_of_late_payloads/pallas_call | solution.py:272
  33.1 1.7 %collective-permute-start.10 = (bf16[8,32,256]{2,1,0:T(8,128)(2,1)S(1)}, bf16[8,32,256]{2,1,0:T(8,128)(2,1)S(1)}, u32[]{:S(2)}, u32[]{:S(2)}) collective-permute-start(bf16[8,32,256]{2,1,0:T(8,128)(2,1)S(1)} %get-tuple-element.51), channel_id=1, source_target_pairs={{0,8},{8,0},{16,24},{24,16},{1,9},{9,1},{17,25},{25,17},{2,10},{10... | collective-permute-start | bytes 393224 | tf_op jit(solution)/shard_map/ppermute | solution.py:410
  34.8 0.1 fusion.4
  34.9 2.7 %collective-permute-start.12 = (bf16[4,32,256]{2,1,0:T(8,128)(2,1)S(1)}, bf16[4,32,256]{2,1,0:T(8,128)(2,1)S(1)}, u32[]{:S(2)}, u32[]{:S(2)}) collective-permute-start(bf16[4,32,256]{2,1,0:T(8,128)(2,1)S(1)} %get-tuple-element.54), channel_id=1, source_target_pairs={{0,16},{8,24},{16,0},{24,8},{1,17},{9,25},{17,1},{25,9},{2,18},{10... | collective-permute-start | bytes 196616 | tf_op jit(solution)/shard_map/ppermute | solution.py:410
  37.6 0.2 collective-permute-start.13
  37.7 0.7 %collective-permute-start.14 = (bf16[4,32,256]{2,1,0:T(8,128)(2,1)S(1)}, bf16[4,32,256]{2,1,0:T(8,128)(2,1)S(1)}, u32[]{:S(2)}, u32[]{:S(2)}) collective-permute-start(bf16[4,32,256]{2,1,0:T(8,128)(2,1)S(1)} %get-tuple-element.56), channel_id=1, source_target_pairs={{0,8},{8,0},{16,24},{24,16},{1,9},{9,1},{17,25},{25,17},{2,10},{10... | collective-permute-start | bytes 196616 | tf_op jit(solution)/shard_map/ppermute | solution.py:410
  38.4 0.9 %collective-permute-done.10.refs_2_ = bf16[8,32,256]{2,1,0:T(8,128)(2,1)S(1)} collective-permute-done((bf16[8,32,256]{2,1,0:T(8,128)(2,1)S(1)}, bf16[8,32,256]{2,1,0:T(8,128)(2,1)S(1)}, u32[]{:S(2)}, u32[]{:S(2)}) %collective-permute-start.10) | collective-permute-done | bytes 131104 | tf_op jit(solution)/shard_map/ppermute | solution.py:410
  39.4 2.7 %collective-permute-start.11 = (bf16[4,32,256]{2,1,0:T(8,128)(2,1)S(1)}, bf16[4,32,256]{2,1,0:T(8,128)(2,1)S(1)}, u32[]{:S(2)}, u32[]{:S(2)}) collective-permute-start(bf16[4,32,256]{2,1,0:T(8,128)(2,1)S(1)} %add_convert_fusion), channel_id=1, source_target_pairs={{0,16},{8,24},{16,0},{24,8},{1,17},{9,25},{17,1},{25,9},{2,18},{10... | collective-permute-start | bytes 196616 | tf_op jit(solution)/shard_map/ppermute | solution.py:410
  42.1 0.1 pad_maximum_fusion.3.phases.refs_0_
  42.2 0.0 collective-permute-done.12.rest_0_
  42.2 2.2 %collective-permute-done.13.rest_1_ = bf16[4,32,256]{2,1,0:T(8,128)(2,1)S(1)} collective-permute-done((bf16[4,32,256]{2,1,0:T(8,128)(2,1)S(1)}, bf16[4,32,256]{2,1,0:T(8,128)(2,1)S(1)}, u32[]{:S(2)}, u32[]{:S(2)}) %collective-permute-start.13) | collective-permute-done | bytes 65568 | tf_op jit(solution)/shard_map/ppermute | solution.py:410
  44.4 0.0 collective-permute-done.14.rest_2_
  44.4 2.8 %to_k_points.2.refs_4_ = f32[128,64,256]{2,1,0:T(8,128)} custom-call(f32[4,128]{1,0:T(4,128)S(1)} %pad_maximum_fusion.3.phases.refs_0_, f32[4,32,256]{2,1,0:T(8,128)S(1)} %get-tuple-element.53.own, bf16[4,32,256]{2,1,0:T(8,128)(2,1)S(1)} %collective-permute-done.12.rest_0_, bf16[4,32,256]{2,1,0:T(8,128)(2,1)S(1)} %collective-permute-done.13.rest_1_, ...), custom_call_target="tpu_custom_call" | custom-call | flops 8388608 | bytes 4194304 | tf_op jit(solution)/shard_map/to_k_points/pallas_call | solution.py:387
  47.2 0.0 collective-permute-done.11.refs_3_
  47.2 2.8 %to_k_points.3 = f32[128,64,256]{2,1,0:T(8,128)} custom-call(f32[4,128]{1,0:T(4,128)S(1)} %pad_maximum_fusion.3.phases.refs_0_, f32[4,32,256]{2,1,0:T(8,128)S(1)} %get-tuple-element.50.refs_1_, bf16[8,32,256]{2,1,0:T(8,128)(2,1)S(1)} %collective-permute-done.10.refs_2_, ...), custom_call_target="tpu_custom_call", output_to_operand_aliasing={{}: (4, {})} | custom-call | flops 8388608 | bytes 4194304 | tf_op jit(solution)/shard_map/to_k_points/pallas_call | solution.py:387
  (8 shorter events, 0.1 us)
Async XLA Ops:
  0.7 1.2 %copy-start = (bf16[32,64,256]{2,1,0:T(8,128)(2,1)S(1)}, bf16[32,64,256]{2,1,0:T(8,128)(2,1)}, u32[]{:S(2)}) copy-start(bf16[32,64,256]{2,1,0:T(8,128)(2,1)} %refs_1_.1) | copy-start | bytes 3145732
  2.9 4.7 %collective-permute-start.6 = (bf16[528,256]{1,0:T(8,128)(2,1)S(1)}, bf16[528,256]{1,0:T(8,128)(2,1)S(1)}, u32[]{:S(2)}, u32[]{:S(2)}) collective-permute-start(bf16[528,256]{1,0:T(8,128)(2,1)S(1)} %get-tuple-element.41), channel_id=1, source_target_pairs={{0,1},{1,0},{2,3},{3,2},{4,5},{5,4},{6,7},{7,6},{8,9},{9,8},{10,11... | collective-permute-start | bytes 811016 | tf_op jit(solution)/shard_map/ppermute | solution.py:410
  3.4 12.4 %collective-permute-start = (bf16[528,256]{1,0:T(8,128)(2,1)S(1)}, bf16[528,256]{1,0:T(8,128)(2,1)S(1)}, u32[]{:S(2)}, u32[]{:S(2)}) collective-permute-start(bf16[528,256]{1,0:T(8,128)(2,1)S(1)} %get-tuple-element.31), channel_id=1, source_target_pairs={{0,6},{1,7},{2,4},{3,5},{4,2},{5,3},{6,0},{7,1},{8,14},{9,15},{10,... | collective-permute-start | bytes 811016 | tf_op jit(solution)/shard_map/ppermute | solution.py:410
  7.0 13.4 %collective-permute-start.2 = (bf16[528,256]{1,0:T(8,128)(2,1)S(1)}, bf16[528,256]{1,0:T(8,128)(2,1)S(1)}, u32[]{:S(2)}, u32[]{:S(2)}) collective-permute-start(bf16[528,256]{1,0:T(8,128)(2,1)S(1)} %get-tuple-element.34), channel_id=1, source_target_pairs={{0,2},{1,3},{2,0},{3,1},{4,6},{5,7},{6,4},{7,5},{8,10},{9,11},{10,... | collective-permute-start | bytes 811016 | tf_op jit(solution)/shard_map/ppermute | solution.py:410
  7.5 13.4 %collective-permute-start.4 = (bf16[528,256]{1,0:T(8,128)(2,1)S(1)}, bf16[528,256]{1,0:T(8,128)(2,1)S(1)}, u32[]{:S(2)}, u32[]{:S(2)}) collective-permute-start(bf16[528,256]{1,0:T(8,128)(2,1)S(1)} %get-tuple-element.37), channel_id=1, source_target_pairs={{0,4},{1,5},{2,6},{3,7},{4,0},{5,1},{6,2},{7,3},{8,12},{9,13},{10,... | collective-permute-start | bytes 811016 | tf_op jit(solution)/shard_map/ppermute | solution.py:410
  8.4 4.3 %collective-permute-start.7 = (bf16[1,128,256]{2,1,0:T(8,128)(2,1)S(1)}, bf16[1,128,256]{2,1,0:T(8,128)(2,1)S(1)}, u32[]{:S(2)}, u32[]{:S(2)}) collective-permute-start(bf16[1,128,256]{2,1,0:T(8,128)(2,1)S(1)} %get-tuple-element.59), channel_id=1, source_target_pairs={{0,8},{8,0},{16,24},{24,16},{1,9},{9,1},{17,25},{25,17},{2,10},{10... | collective-permute-start | bytes 196616 | tf_op jit(solution)/shard_map/ppermute | solution.py:410
  12.8 9.4 %collective-permute-start.8 = (bf16[2,128,256]{2,1,0:T(8,128)(2,1)S(1)}, bf16[2,128,256]{2,1,0:T(8,128)(2,1)S(1)}, u32[]{:S(2)}, u32[]{:S(2)}) collective-permute-start(bf16[2,128,256]{2,1,0:T(8,128)(2,1)S(1)} %pad_maximum_fusion), channel_id=1, source_target_pairs={{0,16},{8,24},{16,0},{24,8},{1,17},{9,25},{17,1},{25,9},{2,18},{10... | collective-permute-start | bytes 393224 | tf_op jit(solution)/shard_map/ppermute | solution.py:410
  15.8 14.2 %collective-permute-start.1 = (bf16[512,256]{1,0:T(8,128)(2,1)S(1)}, bf16[512,256]{1,0:T(8,128)(2,1)S(1)}, u32[]{:S(2)}, u32[]{:S(2)}) collective-permute-start(bf16[512,256]{1,0:T(8,128)(2,1)S(1)} %get-tuple-element.33), channel_id=1, source_target_pairs={{0,7},{1,6},{2,5},{3,4},{4,3},{5,2},{6,1},{7,0},{8,15},{9,14},{10,... | collective-permute-start | bytes 786440 | tf_op jit(solution)/shard_map/ppermute | solution.py:410
  20.4 10.8 %collective-permute-start.3 = (bf16[512,256]{1,0:T(8,128)(2,1)S(1)}, bf16[512,256]{1,0:T(8,128)(2,1)S(1)}, u32[]{:S(2)}, u32[]{:S(2)}) collective-permute-start(bf16[512,256]{1,0:T(8,128)(2,1)S(1)} %get-tuple-element.36), channel_id=1, source_target_pairs={{0,3},{1,2},{2,1},{3,0},{4,7},{5,6},{6,5},{7,4},{8,11},{9,10},{10,... | collective-permute-start | bytes 786440 | tf_op jit(solution)/shard_map/ppermute | solution.py:410
  20.9 10.3 %collective-permute-start.5 = (bf16[512,256]{1,0:T(8,128)(2,1)S(1)}, bf16[512,256]{1,0:T(8,128)(2,1)S(1)}, u32[]{:S(2)}, u32[]{:S(2)}) collective-permute-start(bf16[512,256]{1,0:T(8,128)(2,1)S(1)} %get-tuple-element.39), channel_id=1, source_target_pairs={{0,5},{1,4},{2,7},{3,6},{4,1},{5,0},{6,3},{7,2},{8,13},{9,12},{10,... | collective-permute-start | bytes 786440 | tf_op jit(solution)/shard_map/ppermute | solution.py:410
  22.1 6.0 %collective-permute-start.9 = (bf16[48,256]{1,0:T(8,128)(2,1)S(1)}, bf16[48,256]{1,0:T(8,128)(2,1)S(1)}, u32[]{:S(2)}, u32[]{:S(2)}) collective-permute-start(bf16[48,256]{1,0:T(8,128)(2,1)S(1)} %pad_maximum_fusion.2), channel_id=1, source_target_pairs={{0,1},{1,0},{2,3},{3,2},{4,5},{5,4},{6,7},{7,6},{8,9},{9,8},{10,11... | collective-permute-start | bytes 73736 | tf_op jit(solution)/shard_map/ppermute | solution.py:410
  33.1 6.3 %collective-permute-start.10 = (bf16[8,32,256]{2,1,0:T(8,128)(2,1)S(1)}, bf16[8,32,256]{2,1,0:T(8,128)(2,1)S(1)}, u32[]{:S(2)}, u32[]{:S(2)}) collective-permute-start(bf16[8,32,256]{2,1,0:T(8,128)(2,1)S(1)} %get-tuple-element.51), channel_id=1, source_target_pairs={{0,8},{8,0},{16,24},{24,16},{1,9},{9,1},{17,25},{25,17},{2,10},{10... | collective-permute-start | bytes 393224 | tf_op jit(solution)/shard_map/ppermute | solution.py:410
  34.9 7.3 %collective-permute-start.12 = (bf16[4,32,256]{2,1,0:T(8,128)(2,1)S(1)}, bf16[4,32,256]{2,1,0:T(8,128)(2,1)S(1)}, u32[]{:S(2)}, u32[]{:S(2)}) collective-permute-start(bf16[4,32,256]{2,1,0:T(8,128)(2,1)S(1)} %get-tuple-element.54), channel_id=1, source_target_pairs={{0,16},{8,24},{16,0},{24,8},{1,17},{9,25},{17,1},{25,9},{2,18},{10... | collective-permute-start | bytes 196616 | tf_op jit(solution)/shard_map/ppermute | solution.py:410
  37.6 6.8 %collective-permute-start.13 = (bf16[4,32,256]{2,1,0:T(8,128)(2,1)S(1)}, bf16[4,32,256]{2,1,0:T(8,128)(2,1)S(1)}, u32[]{:S(2)}, u32[]{:S(2)}) collective-permute-start(bf16[4,32,256]{2,1,0:T(8,128)(2,1)S(1)} %get-tuple-element.55), channel_id=1, source_target_pairs={{0,24},{8,16},{16,8},{24,0},{1,25},{9,17},{17,9},{25,1},{2,26},{10... | collective-permute-start | bytes 196616 | tf_op jit(solution)/shard_map/ppermute | solution.py:410
  37.7 6.7 %collective-permute-start.14 = (bf16[4,32,256]{2,1,0:T(8,128)(2,1)S(1)}, bf16[4,32,256]{2,1,0:T(8,128)(2,1)S(1)}, u32[]{:S(2)}, u32[]{:S(2)}) collective-permute-start(bf16[4,32,256]{2,1,0:T(8,128)(2,1)S(1)} %get-tuple-element.56), channel_id=1, source_target_pairs={{0,8},{8,0},{16,24},{24,16},{1,9},{9,1},{17,25},{25,17},{2,10},{10... | collective-permute-start | bytes 196616 | tf_op jit(solution)/shard_map/ppermute | solution.py:410
  39.4 7.8 %collective-permute-start.11 = (bf16[4,32,256]{2,1,0:T(8,128)(2,1)S(1)}, bf16[4,32,256]{2,1,0:T(8,128)(2,1)S(1)}, u32[]{:S(2)}, u32[]{:S(2)}) collective-permute-start(bf16[4,32,256]{2,1,0:T(8,128)(2,1)S(1)} %add_convert_fusion), channel_id=1, source_target_pairs={{0,16},{8,24},{16,0},{24,8},{1,17},{9,25},{17,1},{25,9},{2,18},{10... | collective-permute-start | bytes 196616 | tf_op jit(solution)/shard_map/ppermute | solution.py:410

commit v6 on v5

--- a/solution.py
+++ b/solution.py
@@ -217,7 +217,7 @@
     add_blocks(cap, square, payloads, made, before, total, mixed, stacked)
 
 
-def add_blocks(cap, square, payloads, made, before, total, mixed, stacked):
+def add_blocks(cap, square, payloads, made, before, total, mixed, stacked, kept=None):
     lanes = min(QUAD, cap) * square
     per = cap * square // lanes
     for i, operators in enumerate(made):
@@ -225,11 +225,17 @@
         block = payloads[p][g * lanes : (g + 1) * lanes, :]
         stacked[i * lanes : (i + 1) * lanes, :] = block
         turned = block.T
+        if kept is not None:
+            turned = jnp.concatenate([turned[rows] for rows in kept], axis=0)
         for c, operator in enumerate(operators):
             mixed[c, :, i * lanes : (i + 1) * lanes] = dot(turned, operator).astype(BF16)
     for c in range(mixed.shape[0]):
         acc = dot(mixed[c], stacked[...])
-        total[c] = acc if before is None else acc + before[c]
+        if kept is not None:
+            acc = acc + jnp.concatenate([before[c, rows, :] for rows in kept], axis=0)
+        elif before is not None:
+            acc = acc + before[c]
+        total[c] = acc
 
 
 def operators_kernel(count, cap, pairs, cell_count, square, lists, table, out):
@@ -240,31 +246,32 @@
             out[i * cell_count + c] = operators[c]
 
 
-def late_kernel(count, cap, cell_count, square, last, *refs):
+def late_kernel(count, cap, cell_count, square, part, *refs):
     refs = list(refs)
     images = lax.axis_size("image")
     payloads = [refs.pop(0) for _ in range(count)]
     before, operators = refs.pop(0), refs.pop(0)
-    outs = [refs.pop(0) for _ in shares_of(images)] if last else []
-    total, mixed, stacked = refs
     made = (
         [operators[i * cell_count + c] for c in range(cell_count)]
         for i in range(operators.shape[0] // cell_count)
     )
-    add_blocks(cap, square, payloads, made, before, total, mixed, stacked)
-    if last:
-        z = lax.axis_index("image")
-        share = total.shape[1] // images
-        parts = row_parts(images, share)
-        for ref, (part, distances, _) in zip(outs, shares_of(images)):
-            start, rows = parts[part]
-            for i, k in enumerate(distances):
-                at = pl.multiple_of((z ^ k) * share + start, 16)
-                taken = total[:, pl.ds(at, rows), :].astype(ref.dtype)
-                if len(distances) == 1:
-                    ref[...] = taken
-                else:
-                    ref[i * cell_count : (i + 1) * cell_count] = taken
+    if part is None:
+        total, mixed, stacked = refs
+        add_blocks(cap, square, payloads, made, before, total, mixed, stacked)
+        return
+    share = before.shape[1] // images
+    start, rows = row_parts(images, share)[part]
+    held = [entry for entry in shares_of(images) if entry[0] == part]
+    outs = [refs.pop(0) for _ in held]
+    total, mixed, stacked = refs
+    kept = [slice(i * share + start, i * share + start + rows) for i in range(images)]
+    add_blocks(cap, square, payloads, made, before, total, mixed, stacked, kept)
+    z = lax.axis_index("image")
+    for ref, (_, distances, _) in zip(outs, held):
+        for i, k in enumerate(distances):
+            at = pl.multiple_of((z ^ k) * rows, 16)
+            taken = total[:, pl.ds(at, rows), :].astype(ref.dtype)
+            ref[i * cell_count : (i + 1) * cell_count] = taken
 
 
 def on_chip(kernel, name, args, out_shape, scratch=()):
@@ -314,20 +321,24 @@
     )[0]
 
 
-def late_part(cap, cell_count, square, images, payloads, before, operators, last):
+def late_part(cap, cell_count, square, images, payloads, before, operators, part):
     count, width = len(payloads), payloads[0].shape[1]
-    full = (cell_count, width, width)
-    scratch = chi_scratch(cell_count, width, count * cap * square)
-    out_shape = [jax.ShapeDtypeStruct(full, F32)]
-    if last:
-        parts = row_parts(images, width // images)
+    depth = count * cap * square
+    scratch = chi_scratch(cell_count, width, depth)
+    out_shape = [jax.ShapeDtypeStruct((cell_count, width, width), F32)]
+    if part is not None:
+        rows = row_parts(images, width // images)[part][1]
         out_shape = [
-            jax.ShapeDtypeStruct((len(distances) * cell_count, parts[part][1], width), dtype)
-            for part, distances, dtype in shares_of(images)
+            jax.ShapeDtypeStruct((len(distances) * cell_count, rows, width), dtype)
+            for of, distances, dtype in shares_of(images)
+            if of == part
         ]
-        scratch = [pltpu.VMEM(full, F32)] + scratch
+        scratch = [pltpu.VMEM((cell_count, images * rows, width), F32)] + chi_scratch(
+            cell_count, images * rows, depth
+        )
+        scratch[2] = pltpu.VMEM((depth, width), BF16)
     return on_chip(
-        functools.partial(late_kernel, count, cap, cell_count, square, last),
+        functools.partial(late_kernel, count, cap, cell_count, square, part),
         "chi_of_late_payloads",
         list(payloads) + [before, operators],
         out_shape,
@@ -450,9 +461,13 @@
         chosen = [payload[k] for k in odds[at : at + PART]]
         part = lists[at * LIST_ROWS : (at + len(chosen)) * LIST_ROWS]
         operators = operators_part(cap, pairs, cell_count, square, part, table)
-        last = at + PART >= len(odds)
-        out = late_part(cap, cell_count, square, images, chosen, chi, operators, last)
-        chi = out[0]
+        args = (cap, cell_count, square, images, chosen, chi, operators)
+        if at + PART < len(odds):
+            chi = late_part(*args, None)[0]
+            continue
+        count = len(row_parts(images, blocks.shape[2] // images))
+        by_part = {part: iter(late_part(*args, part)) for part in reversed(range(count))}
+        out = [next(by_part[part]) for part, _, _ in shares_of(images)]
     plan = shares_of(images)
     parts = [[x] for x, (_, distances, _) in zip(out, plan) if distances == [0]]
     given = dict(zip([(part, distances[0]) for part, distances, _ in plan], out))

time: 50.3 us -> 50.7 us (level)
  starting transfers between devices: 20 us -> 20.9 us
  waiting for transfers between devices: 9.85 us -> 9.06 us
    ppermute x15, starting transfers between devices: 20 us -> 20.9 us  [swap(): return lax.ppermute(array, axis, [(i, i ^ k) for i in range(size)])]
    ppermute x15, waiting for transfers between devices: 9.85 us -> 9.06 us  [swap(): return lax.ppermute(array, axis, [(i, i ^ k) for i in range(size)])]
    pallas_call x3 -> x4, Pallas kernels: 9.68 us -> 10.1 us  [on_chip(): pl.pallas_call(kernel, out_shape=out_shape, in_specs=[vmem] * len(args),...]
  transfers between devices with their start and end apart: 15 -> 15, of which waited for: 5 -> 5; matrix products, arithmetic and copies ran while one was open for 4% -> 4% of each run, Pallas kernels for 21% -> 23%
where the time goes in v6:
time: 50.7 us; the launch traced here: 50.4 us
  starting transfers between devices  20.9 us (41%)
  Pallas kernels  16.6 us (33%)
  waiting for transfers between devices  9.06 us (18%)
  local copies, waits for them, and re-layouts  1.99 us (4%)
  other arithmetic  1.73 us (3%)
    ppermute x15, starting transfers between devices, swap(): return lax.ppermute(array, axis, [(i, i ^ k) for i in range(size)])  20.9 us
    pallas_call x4, Pallas kernels, on_chip(): pl.pallas_call(kernel, out_shape=out_shape, in_specs=[vmem] * len(args),...  10.1 us
    ppermute x15, waiting for transfers between devices, swap(): return lax.ppermute(array, axis, [(i, i ^ k) for i in range(size)])  9.06 us
    pallas_call x2, Pallas kernels, transform(): pl.pallas_call(kernel, out_shape=jax.ShapeDtypeStruct((points, share, wid...  5.6 us
    unnamed x2, local copies, waits for them, and re-layouts  1.22 us
  transfers between devices with their start and end apart: 15, of which 5 were waited for; matrix products, arithmetic and copies ran while one was open for 4% of the time, Pallas kernels for 23%

profile of v6, /device:TPU:0, one launch (start us, length us, event | category | flops | bytes accessed | tf_op | source)
XLA Modules:
  0.0 50.4 jit_solution(4182591395016981991)
XLA Ops:
  0.0 0.7 %pad_add_fusion.refs_0_ = s32[15,32]{1,0:T(8,128)S(1)} fusion(s32[4,32]{1,0:T(4,128)} %bitcast.30, s32[8,32]{1,0:T(8,128)} %bitcast.29, s32[2,32]{1,0:T(2,128)} %bitcast.31, s32[1,32]{1,0:T(1,128)} %bitcast.32), kind=kLoop, calls=%fused_computation.6 | loop fusion | flops 1440 | bytes 3840 | tf_op jit(solution)/shard_map/concatenate | solution.py:86
  0.7 0.0 copy-start
  0.7 1.2 %copy-done = bf16[32,64,256]{2,1,0:T(8,128)(2,1)S(1)} copy-done((bf16[32,64,256]{2,1,0:T(8,128)(2,1)S(1)}, bf16[32,64,256]{2,1,0:T(8,128)(2,1)}, u32[]{:S(2)}) %copy-start) | copy-done | bytes 1048600
  2.0 1.0 %pack_by_owner.1 = (bf16[528,256]{1,0:T(8,128)(2,1)S(1)}, bf16[528,256]{1,0:T(8,128)(2,1)S(1)}, bf16[528,256]{1,0:T(8,128)(2,1)S(1)}, bf16[512,256]{1,0:T(8,128)...) custom-call(s32[15,32]{1,0:T(8,128)S(1)} %pad_add_fusion.refs_0_, ...), custom_call_target="tpu_custom_call" | custom-call | bytes 6291456 | tf_op jit(solution)/shard_map/pack_by_owner/pallas_call | solution.py:96
  2.9 0.5 %collective-permute-start.6 = (bf16[528,256]{1,0:T(8,128)(2,1)S(1)}, bf16[528,256]{1,0:T(8,128)(2,1)S(1)}, u32[]{:S(2)}, u32[]{:S(2)}) collective-permute-start(bf16[528,256]{1,0:T(8,128)(2,1)S(1)} %get-tuple-element.41), channel_id=1, source_target_pairs={{0,1},{1,0},{2,3},{3,2},{4,5},{5,4},{6,7},{7,6},{8,9},{9,8},{10,11... | collective-permute-start | bytes 811016 | tf_op jit(solution)/shard_map/ppermute | solution.py:421
  3.4 3.5 %collective-permute-start = (bf16[528,256]{1,0:T(8,128)(2,1)S(1)}, bf16[528,256]{1,0:T(8,128)(2,1)S(1)}, u32[]{:S(2)}, u32[]{:S(2)}) collective-permute-start(bf16[528,256]{1,0:T(8,128)(2,1)S(1)} %get-tuple-element.31), channel_id=1, source_target_pairs={{0,6},{1,7},{2,4},{3,5},{4,2},{5,3},{6,0},{7,1},{8,14},{9,15},{10,... | collective-permute-start | bytes 811016 | tf_op jit(solution)/shard_map/ppermute | solution.py:421
  7.0 0.5 %collective-permute-start.2 = (bf16[528,256]{1,0:T(8,128)(2,1)S(1)}, bf16[528,256]{1,0:T(8,128)(2,1)S(1)}, u32[]{:S(2)}, u32[]{:S(2)}) collective-permute-start(bf16[528,256]{1,0:T(8,128)(2,1)S(1)} %get-tuple-element.34), channel_id=1, source_target_pairs={{0,2},{1,3},{2,0},{3,1},{4,6},{5,7},{6,4},{7,5},{8,10},{9,11},{10,... | collective-permute-start | bytes 811016 | tf_op jit(solution)/shard_map/ppermute | solution.py:421
  7.5 0.1 collective-permute-start.4
  7.6 0.0 collective-permute-done.6.refs_1_
  7.6 0.8 %fusion.5 = (bf16[1,128,256]{2,1,0:T(8,128)(2,1)S(1)}, bf16[128,256]{1,0:T(8,128)(2,1)S(1)}) fusion(bf16[64,256]{1,0:T(8,128)(2,1)} %bitcast.27, bf16[64,256]{1,0:T(8,128)(2,1)} %bitcast.28), kind=kLoop, calls=%fused_computation.23 | loop fusion | flops 131072 | bytes 196608 | tf_op jit(solution)/shard_map/broadcast_in_dim | solution.py:445
  8.4 2.0 %collective-permute-start.7 = (bf16[1,128,256]{2,1,0:T(8,128)(2,1)S(1)}, bf16[1,128,256]{2,1,0:T(8,128)(2,1)S(1)}, u32[]{:S(2)}, u32[]{:S(2)}) collective-permute-start(bf16[1,128,256]{2,1,0:T(8,128)(2,1)S(1)} %get-tuple-element.59), channel_id=1, source_target_pairs={{0,8},{8,0},{16,24},{24,16},{1,9},{9,1},{17,25},{25,17},{2,10},{10... | collective-permute-start | bytes 196616 | tf_op jit(solution)/shard_map/ppermute | solution.py:421
  10.4 0.8 %slice_bitcast_fusion.3 = (s32[4]{0:T(128)S(1)}, s32[4]{0:T(128)S(1)}) fusion(s32[4,2]{0,1:T(2,128)} %param.13), kind=kLoop, calls=%fused_computation.22 | loop fusion | bytes 64 | tf_op jit(solution)/shard_map/mul | solution.py:484
  11.2 1.5 %collective-permute-done.7 = bf16[1,128,256]{2,1,0:T(8,128)(2,1)S(1)} collective-permute-done((bf16[1,128,256]{2,1,0:T(8,128)(2,1)S(1)}, bf16[1,128,256]{2,1,0:T(8,128)(2,1)S(1)}, u32[]{:S(2)}, u32[]{:S(2)}) %collective-permute-start.7) | collective-permute-done | bytes 65568 | tf_op jit(solution)/shard_map/ppermute | solution.py:421
  12.8 3.1 %collective-permute-start.8 = (bf16[2,128,256]{2,1,0:T(8,128)(2,1)S(1)}, bf16[2,128,256]{2,1,0:T(8,128)(2,1)S(1)}, u32[]{:S(2)}, u32[]{:S(2)}) collective-permute-start(bf16[2,128,256]{2,1,0:T(8,128)(2,1)S(1)} %pad_maximum_fusion), channel_id=1, source_target_pairs={{0,16},{8,24},{16,0},{24,8},{1,17},{9,25},{17,1},{25,9},{2,18},{10... | collective-permute-start | bytes 393224 | tf_op jit(solution)/shard_map/ppermute | solution.py:421
  15.8 0.0 collective-permute-done.refs_2_
  15.8 0.6 %collective-permute-start.1 = (bf16[512,256]{1,0:T(8,128)(2,1)S(1)}, bf16[512,256]{1,0:T(8,128)(2,1)S(1)}, u32[]{:S(2)}, u32[]{:S(2)}) collective-permute-start(bf16[512,256]{1,0:T(8,128)(2,1)S(1)} %get-tuple-element.33), channel_id=1, source_target_pairs={{0,7},{1,6},{2,5},{3,4},{4,3},{5,2},{6,1},{7,0},{8,15},{9,14},{10,... | collective-permute-start | bytes 786440 | tf_op jit(solution)/shard_map/ppermute | solution.py:421
  16.4 4.0 %collective-permute-done.2.refs_3_ = bf16[528,256]{1,0:T(8,128)(2,1)S(1)} collective-permute-done((bf16[528,256]{1,0:T(8,128)(2,1)S(1)}, bf16[528,256]{1,0:T(8,128)(2,1)S(1)}, u32[]{:S(2)}, u32[]{:S(2)}) %collective-permute-start.2) | collective-permute-done | bytes 270368 | tf_op jit(solution)/shard_map/ppermute | solution.py:421
  20.4 0.5 collective-permute-start.3
  20.9 0.0 collective-permute-done.4.refs_4_
  20.9 1.2 %collective-permute-start.5 = (bf16[512,256]{1,0:T(8,128)(2,1)S(1)}, bf16[512,256]{1,0:T(8,128)(2,1)S(1)}, u32[]{:S(2)}, u32[]{:S(2)}) collective-permute-start(bf16[512,256]{1,0:T(8,128)(2,1)S(1)} %get-tuple-element.39), channel_id=1, source_target_pairs={{0,5},{1,4},{2,7},{3,6},{4,1},{5,0},{6,3},{7,2},{8,13},{9,12},{10,... | collective-permute-start | bytes 786440 | tf_op jit(solution)/shard_map/ppermute | solution.py:421
  22.1 0.0 collective-permute-start.9
  22.1 0.0 collective-permute-done.8
  22.2 6.0 %chi_of_early_payloads.1 = (f32[4,256,256]{2,1,0:T(8,128)S(1)}, bf16[1024,128]{1,0:T(8,128)(2,1)S(1)}) custom-call(bf16[528,256]{1,0:T(8,128)(2,1)S(1)} %get-tuple-element.40.refs_0_, bf16[528,256]{1,0:T(8,128)(2,1)S(1)} %collective-permute-done.6.refs_1_, bf16[528,256]{1,0:T(8,128)(2,1)S(1)} %collective-permute-done.refs_2_, ...), custom_call_target="tpu_custom_call" | custom-call | flops 1048576 | bytes 1024 | tf_op jit(solution)/shard_map/chi_of_early_payloads/pallas_call | solution.py:279
  28.2 0.0 collective-permute-done.9.lists
  28.2 1.8 %operators_of_late_payloads.1.refs_4_ = bf16[24,256,256]{2,1,0:T(8,128)(2,1)S(1)} custom-call(bf16[48,256]{1,0:T(8,128)(2,1)S(1)} %collective-permute-done.9.lists, bf16[1024,128]{1,0:T(8,128)(2,1)S(1)} %get-tuple-element.49.table), custom_call_target="tpu_custom_call" | custom-call | flops 1048576 | bytes 1024 | tf_op jit(solution)/shard_map/operators_of_late_payloads/pallas_call | solution.py:279
  30.0 0.0 collective-permute-done.1.refs_0_
  30.0 1.2 %collective-permute-done.3.refs_1_ = bf16[512,256]{1,0:T(8,128)(2,1)S(1)} collective-permute-done((bf16[512,256]{1,0:T(8,128)(2,1)S(1)}, bf16[512,256]{1,0:T(8,128)(2,1)S(1)}, u32[]{:S(2)}, u32[]{:S(2)}) %collective-permute-start.3) | collective-permute-done | bytes 262176 | tf_op jit(solution)/shard_map/ppermute | solution.py:421
  31.2 0.0 collective-permute-done.5.refs_2_
  31.2 1.1 %chi_of_late_payloads.2 = (f32[4,32,256]{2,1,0:T(8,128)S(1)}, f32[4,32,256]{2,1,0:T(8,128)S(1)}, bf16[8,32,256]{2,1,0:T(8,128)(2,1)S(1)}) custom-call(bf16[512,256]{1,0:T(8,128)(2,1)S(1)} %collective-permute-done.1.refs_0_, bf16[512,256]{1,0:T(8,128)(2,1)S(1)} %collective-permute-done.3.refs_1_, bf16[512,256]{1,0:T(8,128)(2,1)S(1)} %collective-permute-done.5.refs_2_, ...), custom_call_target="tpu_custom_call" | custom-call | flops 1048576 | bytes 1024 | tf_op jit(solution)/shard_map/chi_of_late_payloads/pallas_call | solution.py:279
  32.3 1.7 %collective-permute-start.10 = (bf16[8,32,256]{2,1,0:T(8,128)(2,1)S(1)}, bf16[8,32,256]{2,1,0:T(8,128)(2,1)S(1)}, u32[]{:S(2)}, u32[]{:S(2)}) collective-permute-start(bf16[8,32,256]{2,1,0:T(8,128)(2,1)S(1)} %get-tuple-element.51), channel_id=1, source_target_pairs={{0,8},{8,0},{16,24},{24,16},{1,9},{9,1},{17,25},{25,17},{2,10},{10... | collective-permute-start | bytes 393224 | tf_op jit(solution)/shard_map/ppermute | solution.py:421
  34.0 0.1 fusion.4
  34.1 1.1 %chi_of_late_payloads.3 = (f32[4,32,256]{2,1,0:T(8,128)S(1)}, bf16[4,32,256]{2,1,0:T(8,128)(2,1)S(1)}, bf16[4,32,256]{2,1,0:T(8,128)(2,1)S(1)}, bf16[4,32,256]{2,1,0:T(8,128)(2,1)S(1)}) custom-call(bf16[512,256]{1,0:T(8,128)(2,1)S(1)} %collective-permute-done.1.refs_0_, bf16[512,256]{1,0:T(8,128)(2,1)S(1)} %collective-permute-done.3.refs_1_, ...), custom_call_target="tpu_custom_call" | custom-call | flops 1048576 | bytes 1024 | tf_op jit(solution)/shard_map/chi_of_late_payloads/pallas_call | solution.py:279
  35.3 2.7 %collective-permute-start.12 = (bf16[4,32,256]{2,1,0:T(8,128)(2,1)S(1)}, bf16[4,32,256]{2,1,0:T(8,128)(2,1)S(1)}, u32[]{:S(2)}, u32[]{:S(2)}) collective-permute-start(bf16[4,32,256]{2,1,0:T(8,128)(2,1)S(1)} %get-tuple-element.54), channel_id=1, source_target_pairs={{0,16},{8,24},{16,0},{24,8},{1,17},{9,25},{17,1},{25,9},{2,18},{10... | collective-permute-start | bytes 196616 | tf_op jit(solution)/shard_map/ppermute | solution.py:421
  37.9 0.2 collective-permute-start.13
  38.1 0.7 %collective-permute-start.14 = (bf16[4,32,256]{2,1,0:T(8,128)(2,1)S(1)}, bf16[4,32,256]{2,1,0:T(8,128)(2,1)S(1)}, u32[]{:S(2)}, u32[]{:S(2)}) collective-permute-start(bf16[4,32,256]{2,1,0:T(8,128)(2,1)S(1)} %get-tuple-element.56), channel_id=1, source_target_pairs={{0,8},{8,0},{16,24},{24,16},{1,9},{9,1},{17,25},{25,17},{2,10},{10... | collective-permute-start | bytes 196616 | tf_op jit(solution)/shard_map/ppermute | solution.py:421
  38.8 0.0 collective-permute-done.10.refs_2_
  38.8 3.6 %collective-permute-start.11 = (bf16[4,32,256]{2,1,0:T(8,128)(2,1)S(1)}, bf16[4,32,256]{2,1,0:T(8,128)(2,1)S(1)}, u32[]{:S(2)}, u32[]{:S(2)}) collective-permute-start(bf16[4,32,256]{2,1,0:T(8,128)(2,1)S(1)} %add_convert_fusion), channel_id=1, source_target_pairs={{0,16},{8,24},{16,0},{24,8},{1,17},{9,25},{17,1},{25,9},{2,18},{10... | collective-permute-start | bytes 196616 | tf_op jit(solution)/shard_map/ppermute | solution.py:421
  42.4 0.1 pad_maximum_fusion.3.phases.refs_0_
  42.5 0.4 collective-permute-done.12.rest_0_
  42.9 1.9 %collective-permute-done.13.rest_1_ = bf16[4,32,256]{2,1,0:T(8,128)(2,1)S(1)} collective-permute-done((bf16[4,32,256]{2,1,0:T(8,128)(2,1)S(1)}, bf16[4,32,256]{2,1,0:T(8,128)(2,1)S(1)}, u32[]{:S(2)}, u32[]{:S(2)}) %collective-permute-start.13) | collective-permute-done | bytes 65568 | tf_op jit(solution)/shard_map/ppermute | solution.py:421
  44.8 0.0 collective-permute-done.14.rest_2_
  44.8 2.8 %to_k_points.2.refs_4_ = f32[128,64,256]{2,1,0:T(8,128)} custom-call(f32[4,128]{1,0:T(4,128)S(1)} %pad_maximum_fusion.3.phases.refs_0_, f32[4,32,256]{2,1,0:T(8,128)S(1)} %get-tuple-element.53.own, bf16[4,32,256]{2,1,0:T(8,128)(2,1)S(1)} %collective-permute-done.12.rest_0_, bf16[4,32,256]{2,1,0:T(8,128)(2,1)S(1)} %collective-permute-done.13.rest_1_, ...), custom_call_target="tpu_custom_call" | custom-call | flops 8388608 | bytes 4194304 | tf_op jit(solution)/shard_map/to_k_points/pallas_call | solution.py:398
  47.6 0.0 collective-permute-done.11.refs_3_
  47.6 2.8 %to_k_points.3 = f32[128,64,256]{2,1,0:T(8,128)} custom-call(f32[4,128]{1,0:T(4,128)S(1)} %pad_maximum_fusion.3.phases.refs_0_, f32[4,32,256]{2,1,0:T(8,128)S(1)} %get-tuple-element.50.refs_1_, bf16[8,32,256]{2,1,0:T(8,128)(2,1)S(1)} %collective-permute-done.10.refs_2_, ...), custom_call_target="tpu_custom_call", output_to_operand_aliasing={{}: (4, {})} | custom-call | flops 8388608 | bytes 4194304 | tf_op jit(solution)/shard_map/to_k_points/pallas_call | solution.py:398
  (8 shorter events, 0.1 us)
Async XLA Ops:
  0.7 1.2 %copy-start = (bf16[32,64,256]{2,1,0:T(8,128)(2,1)S(1)}, bf16[32,64,256]{2,1,0:T(8,128)(2,1)}, u32[]{:S(2)}) copy-start(bf16[32,64,256]{2,1,0:T(8,128)(2,1)} %refs_1_.1) | copy-start | bytes 3145732
  2.9 4.7 %collective-permute-start.6 = (bf16[528,256]{1,0:T(8,128)(2,1)S(1)}, bf16[528,256]{1,0:T(8,128)(2,1)S(1)}, u32[]{:S(2)}, u32[]{:S(2)}) collective-permute-start(bf16[528,256]{1,0:T(8,128)(2,1)S(1)} %get-tuple-element.41), channel_id=1, source_target_pairs={{0,1},{1,0},{2,3},{3,2},{4,5},{5,4},{6,7},{7,6},{8,9},{9,8},{10,11... | collective-permute-start | bytes 811016 | tf_op jit(solution)/shard_map/ppermute | solution.py:421
  3.4 12.4 %collective-permute-start = (bf16[528,256]{1,0:T(8,128)(2,1)S(1)}, bf16[528,256]{1,0:T(8,128)(2,1)S(1)}, u32[]{:S(2)}, u32[]{:S(2)}) collective-permute-start(bf16[528,256]{1,0:T(8,128)(2,1)S(1)} %get-tuple-element.31), channel_id=1, source_target_pairs={{0,6},{1,7},{2,4},{3,5},{4,2},{5,3},{6,0},{7,1},{8,14},{9,15},{10,... | collective-permute-start | bytes 811016 | tf_op jit(solution)/shard_map/ppermute | solution.py:421
  7.0 13.4 %collective-permute-start.2 = (bf16[528,256]{1,0:T(8,128)(2,1)S(1)}, bf16[528,256]{1,0:T(8,128)(2,1)S(1)}, u32[]{:S(2)}, u32[]{:S(2)}) collective-permute-start(bf16[528,256]{1,0:T(8,128)(2,1)S(1)} %get-tuple-element.34), channel_id=1, source_target_pairs={{0,2},{1,3},{2,0},{3,1},{4,6},{5,7},{6,4},{7,5},{8,10},{9,11},{10,... | collective-permute-start | bytes 811016 | tf_op jit(solution)/shard_map/ppermute | solution.py:421
  7.5 13.4 %collective-permute-start.4 = (bf16[528,256]{1,0:T(8,128)(2,1)S(1)}, bf16[528,256]{1,0:T(8,128)(2,1)S(1)}, u32[]{:S(2)}, u32[]{:S(2)}) collective-permute-start(bf16[528,256]{1,0:T(8,128)(2,1)S(1)} %get-tuple-element.37), channel_id=1, source_target_pairs={{0,4},{1,5},{2,6},{3,7},{4,0},{5,1},{6,2},{7,3},{8,12},{9,13},{10,... | collective-permute-start | bytes 811016 | tf_op jit(solution)/shard_map/ppermute | solution.py:421
  8.4 4.3 %collective-permute-start.7 = (bf16[1,128,256]{2,1,0:T(8,128)(2,1)S(1)}, bf16[1,128,256]{2,1,0:T(8,128)(2,1)S(1)}, u32[]{:S(2)}, u32[]{:S(2)}) collective-permute-start(bf16[1,128,256]{2,1,0:T(8,128)(2,1)S(1)} %get-tuple-element.59), channel_id=1, source_target_pairs={{0,8},{8,0},{16,24},{24,16},{1,9},{9,1},{17,25},{25,17},{2,10},{10... | collective-permute-start | bytes 196616 | tf_op jit(solution)/shard_map/ppermute | solution.py:421
  12.8 9.4 %collective-permute-start.8 = (bf16[2,128,256]{2,1,0:T(8,128)(2,1)S(1)}, bf16[2,128,256]{2,1,0:T(8,128)(2,1)S(1)}, u32[]{:S(2)}, u32[]{:S(2)}) collective-permute-start(bf16[2,128,256]{2,1,0:T(8,128)(2,1)S(1)} %pad_maximum_fusion), channel_id=1, source_target_pairs={{0,16},{8,24},{16,0},{24,8},{1,17},{9,25},{17,1},{25,9},{2,18},{10... | collective-permute-start | bytes 393224 | tf_op jit(solution)/shard_map/ppermute | solution.py:421
  15.8 14.2 %collective-permute-start.1 = (bf16[512,256]{1,0:T(8,128)(2,1)S(1)}, bf16[512,256]{1,0:T(8,128)(2,1)S(1)}, u32[]{:S(2)}, u32[]{:S(2)}) collective-permute-start(bf16[512,256]{1,0:T(8,128)(2,1)S(1)} %get-tuple-element.33), channel_id=1, source_target_pairs={{0,7},{1,6},{2,5},{3,4},{4,3},{5,2},{6,1},{7,0},{8,15},{9,14},{10,... | collective-permute-start | bytes 786440 | tf_op jit(solution)/shard_map/ppermute | solution.py:421
  20.4 10.8 %collective-permute-start.3 = (bf16[512,256]{1,0:T(8,128)(2,1)S(1)}, bf16[512,256]{1,0:T(8,128)(2,1)S(1)}, u32[]{:S(2)}, u32[]{:S(2)}) collective-permute-start(bf16[512,256]{1,0:T(8,128)(2,1)S(1)} %get-tuple-element.36), channel_id=1, source_target_pairs={{0,3},{1,2},{2,1},{3,0},{4,7},{5,6},{6,5},{7,4},{8,11},{9,10},{10,... | collective-permute-start | bytes 786440 | tf_op jit(solution)/shard_map/ppermute | solution.py:421
  20.9 10.3 %collective-permute-start.5 = (bf16[512,256]{1,0:T(8,128)(2,1)S(1)}, bf16[512,256]{1,0:T(8,128)(2,1)S(1)}, u32[]{:S(2)}, u32[]{:S(2)}) collective-permute-start(bf16[512,256]{1,0:T(8,128)(2,1)S(1)} %get-tuple-element.39), channel_id=1, source_target_pairs={{0,5},{1,4},{2,7},{3,6},{4,1},{5,0},{6,3},{7,2},{8,13},{9,12},{10,... | collective-permute-start | bytes 786440 | tf_op jit(solution)/shard_map/ppermute | solution.py:421
  22.1 6.0 %collective-permute-start.9 = (bf16[48,256]{1,0:T(8,128)(2,1)S(1)}, bf16[48,256]{1,0:T(8,128)(2,1)S(1)}, u32[]{:S(2)}, u32[]{:S(2)}) collective-permute-start(bf16[48,256]{1,0:T(8,128)(2,1)S(1)} %pad_maximum_fusion.2), channel_id=1, source_target_pairs={{0,1},{1,0},{2,3},{3,2},{4,5},{5,4},{6,7},{7,6},{8,9},{9,8},{10,11... | collective-permute-start | bytes 73736 | tf_op jit(solution)/shard_map/ppermute | solution.py:421
  32.3 6.5 %collective-permute-start.10 = (bf16[8,32,256]{2,1,0:T(8,128)(2,1)S(1)}, bf16[8,32,256]{2,1,0:T(8,128)(2,1)S(1)}, u32[]{:S(2)}, u32[]{:S(2)}) collective-permute-start(bf16[8,32,256]{2,1,0:T(8,128)(2,1)S(1)} %get-tuple-element.51), channel_id=1, source_target_pairs={{0,8},{8,0},{16,24},{24,16},{1,9},{9,1},{17,25},{25,17},{2,10},{10... | collective-permute-start | bytes 393224 | tf_op jit(solution)/shard_map/ppermute | solution.py:421
  35.3 7.6 %collective-permute-start.12 = (bf16[4,32,256]{2,1,0:T(8,128)(2,1)S(1)}, bf16[4,32,256]{2,1,0:T(8,128)(2,1)S(1)}, u32[]{:S(2)}, u32[]{:S(2)}) collective-permute-start(bf16[4,32,256]{2,1,0:T(8,128)(2,1)S(1)} %get-tuple-element.54), channel_id=1, source_target_pairs={{0,16},{8,24},{16,0},{24,8},{1,17},{9,25},{17,1},{25,9},{2,18},{10... | collective-permute-start | bytes 196616 | tf_op jit(solution)/shard_map/ppermute | solution.py:421
  37.9 6.9 %collective-permute-start.13 = (bf16[4,32,256]{2,1,0:T(8,128)(2,1)S(1)}, bf16[4,32,256]{2,1,0:T(8,128)(2,1)S(1)}, u32[]{:S(2)}, u32[]{:S(2)}) collective-permute-start(bf16[4,32,256]{2,1,0:T(8,128)(2,1)S(1)} %get-tuple-element.55), channel_id=1, source_target_pairs={{0,24},{8,16},{16,8},{24,0},{1,25},{9,17},{17,9},{25,1},{2,26},{10... | collective-permute-start | bytes 196616 | tf_op jit(solution)/shard_map/ppermute | solution.py:421
  38.1 6.7 %collective-permute-start.14 = (bf16[4,32,256]{2,1,0:T(8,128)(2,1)S(1)}, bf16[4,32,256]{2,1,0:T(8,128)(2,1)S(1)}, u32[]{:S(2)}, u32[]{:S(2)}) collective-permute-start(bf16[4,32,256]{2,1,0:T(8,128)(2,1)S(1)} %get-tuple-element.56), channel_id=1, source_target_pairs={{0,8},{8,0},{16,24},{24,16},{1,9},{9,1},{17,25},{25,17},{2,10},{10... | collective-permute-start | bytes 196616 | tf_op jit(solution)/shard_map/ppermute | solution.py:421
  38.8 8.8 %collective-permute-start.11 = (bf16[4,32,256]{2,1,0:T(8,128)(2,1)S(1)}, bf16[4,32,256]{2,1,0:T(8,128)(2,1)S(1)}, u32[]{:S(2)}, u32[]{:S(2)}) collective-permute-start(bf16[4,32,256]{2,1,0:T(8,128)(2,1)S(1)} %add_convert_fusion), channel_id=1, source_target_pairs={{0,16},{8,24},{16,0},{24,8},{1,17},{9,25},{17,1},{25,9},{2,18},{10... | collective-permute-start | bytes 196616 | tf_op jit(solution)/shard_map/ppermute | solution.py:421
